TPU v7x, 128 devices: a whole 4x4x4 slice. The times are simulated.
128 devices in a mesh: gauss: 64 (over z, x, y), view: 2 (over core).
Axes of the slice: x: 4, y: 4, z: 4, core: 2. Of those that a mesh axis runs over, the one named last changes fastest.
Arguments:
- gauss_rows: float32 [64, 2097152], P(None, 'gauss')
- vis_shard: int32 [4096, 512, 1], P(('gauss', 'view')), may hold values from 0 to 63; in each aligned block of 16384 rows (0 to 16383, 16384 to 32767, ..., all dimensions but the last counted through in order) at most 512 rows name the same one
- vis_row: int32 [4096, 512], P(('gauss', 'view')), may hold values from 0 to 32767
- tile_index: int32 [4096], P(('gauss', 'view')), may hold values from 0 to 65279
- cotangent: float32 [4096, 29, 256], P(('gauss', 'view')), may hold values from -120 to 120
Outputs:
- images: float32 [4096, 29, 256], P(('gauss', 'view'))
- gradient: float32 [64, 2097152], P(None, ('gauss', 'view'))
Inputs may be any that keep to these rules, and one draw needn't show every extreme that they name: `vis_shard`: within the lists of one device (aligned blocks of 16384 entries, tiles in order) no shard is named more than 512 times, a bound that some block reaches.
All inputs are finite; a program needn't handle non-finite values.
Results may differ from a plain program's by a relative error of at most 0.0003.
Values sent between devices are 32-bit elements; how exact they have to be, the bound alone decides.
A program may use at most 128 MiB of HBM per device.

v0:
```python
import jax
import jax.numpy as jnp
from jax import lax
from jax.sharding import PartitionSpec as P

CHANNELS = 29
TILE_SIDE = 16
PIXELS = 256
VIEWS = 8
SCREEN_TILES = 8160


TWO_PI = 6.283185307179586


def composite(entry_params, view_cos, cotangent):
    pixel = jnp.arange(PIXELS)
    across = (pixel % TILE_SIDE).astype(jnp.float32) + 0.5
    down = (pixel // TILE_SIDE).astype(jnp.float32) + 0.5

    def render(params):
        off_x = across[None, :] - params[:, 0][:, None]
        off_y = down[None, :] - params[:, 1][:, None]
        conic_a = jnp.exp(params[:, 2])
        conic_c = jnp.exp(params[:, 4])
        conic_b = 0.9 * jnp.tanh(params[:, 3]) * jnp.sqrt(conic_a * conic_c)
        power = -0.5 * (
            conic_a[:, None] * off_x * off_x
            + 2.0 * conic_b[:, None] * off_x * off_y
            + conic_c[:, None] * off_y * off_y
        )
        alpha = 0.99 * jax.nn.sigmoid(params[:, 5])[:, None] * jnp.exp(power)
        logs = jnp.log(1.0 - alpha)
        before = jnp.cumsum(logs, axis=0) - logs
        weight = jnp.exp(before) * alpha
        colour = params[:, 6 : 6 + CHANNELS] + view_cos * params[:, 6 + CHANNELS : 6 + 2 * CHANNELS]
        return lax.dot_general(
            colour, weight, (((0,), (0,)), ((), ())), precision=lax.Precision.HIGHEST
        )

    image, pull = jax.vjp(render, entry_params)
    grads = pull(cotangent)
    return (image, grads[0])


def per_device(gauss_rows, vis_shard, vis_row, tile_index, cotangent):
    shards = lax.axis_size("gauss")
    tiles, length = vis_row.shape
    entries = tiles * length
    capacity = 2 * entries // shards
    width = gauss_rows.shape[0]
    own_cols = gauss_rows.shape[1]
    shard_of = vis_shard.reshape(entries)
    row_of = vis_row.reshape(entries)
    hits = (shard_of[:, None] == jnp.arange(shards, dtype=jnp.int32)[None, :]).astype(jnp.int32)
    place = jnp.sum((jnp.cumsum(hits, axis=0) - 1) * hits, axis=1)
    slot_of = shard_of * capacity + place
    requests = (
        jnp.zeros((shards * capacity,), jnp.int32).at[slot_of].set(row_of).reshape(shards, capacity)
    )
    row_major = jnp.transpose(gauss_rows)
    asked = lax.all_to_all(requests, "gauss", split_axis=0, concat_axis=0, tiled=True)
    fetched = jnp.take(row_major, asked.reshape(-1), axis=0).reshape(
        asked.shape[0], asked.shape[1], width
    )
    sent = lax.all_to_all(fetched, "gauss", split_axis=0, concat_axis=0, tiled=True)
    entry_rows = jnp.take(sent.reshape(shards * capacity, width), slot_of, axis=0)
    tile_rows = entry_rows.reshape(tiles, length, width)
    view_cos = jnp.cos(TWO_PI * (tile_index // SCREEN_TILES).astype(jnp.float32) / VIEWS)

    def one_tile(packed):
        return composite(packed[0], packed[1], packed[2])

    images, grads = lax.map(one_tile, (tile_rows, view_cos, cotangent), batch_size=4)
    entry_grads = grads.reshape(entries, width)
    outgoing = (
        jnp.zeros((shards * capacity, width), jnp.float32)
        .at[slot_of]
        .set(entry_grads)
        .reshape(shards, capacity, width)
    )
    returned = lax.all_to_all(outgoing, "gauss", split_axis=0, concat_axis=0, tiled=True)
    row_totals = (
        jnp.zeros((own_cols, width), jnp.float32)
        .at[asked.reshape(-1)]
        .add(returned.reshape(shards * capacity, width))
    )
    totals = jnp.transpose(row_totals)
    half = own_cols // 2
    summed = lax.psum(totals, "view")
    gradient = lax.dynamic_slice_in_dim(summed, lax.axis_index("view") * half, half, 1)
    return (images, gradient)


def solution(mesh):
    placed = (
        P(None, "gauss"),
        P(("gauss", "view"), None, None),
        P(("gauss", "view"), None),
        P(("gauss", "view")),
        P(("gauss", "view"), None, None),
    )
    return jax.shard_map(
        per_device,
        mesh=mesh,
        in_specs=placed,
        out_specs=(P(("gauss", "view"), None, None), P(None, ("gauss", "view"))),
        check_vma=False,
    )
```

profile of v0, /device:TPU:1, one launch (start us, length us, event | category | flops | bytes accessed | tf_op | source)
XLA Modules:
  0.0 1285.5 jit_solution(6050833279133911840)
XLA Ops:
  12.1 5.1 add_add_fusion
  17.2 5.4 copy.87
  22.7 5.0 fusion.78
  27.7 60.9 %scatter_custom_fusion = s32[32768]{0:T(1024)} fusion(s32[16384]{0:T(1024)S(1)} %bitcast.185, s32[16384]{0:T(1024)S(1)} %bitcast.189, s32[]{:T(128)} %constant.161.clone.1), kind=kCustom, calls=%fused_computation.159 | custom fusion | bytes 131076 | tf_op jit(solution)/shard_map/scatter | solution.py:59
  88.7 12.0 all-to-all-start
  100.6 12.2 copy.88
  113.1 114.0 %gather_fusion = f32[32768,64]{1,0:T(8,128)} fusion(f32[32768,64]{1,0:T(8,128)} %bitcast.160, s32[32768]{0:T(1024)S(1)} %broadcast_clamp_fusion), kind=kCustom, calls=%fused_computation | custom fusion | bytes 16908288 | tf_op jit(solution)/shard_map/jit(_take)/gather | solution.py:63
  227.0 12.7 copy.89
  239.8 8.6 broadcast_select_fusion
  248.3 10.2 all-to-all-start.1
  260.5 115.3 %all-to-all-done.1 = f32[64,512,64]{1,2,0:T(8,128)} async-done(((f32[64,512,64]{1,2,0:T(8,128)}), f32[64,512,64]{1,2,0:T(8,128)}, u32[]{:S(2)}, u32[]{:S(2)}) %all-to-all-start.1) | async-done | bytes 8388640 | tf_op jit(solution)/shard_map/all_to_all | solution.py:66
  375.8 12.2 copy.90
  388.0 60.2 %gather_fusion.1 = f32[16384,64]{1,0:T(8,128)} fusion(f32[32768,64]{1,0:T(8,128)} %bitcast.161, s32[16384]{0:T(1024)S(1)} %broadcast_clamp_fusion.1), kind=kCustom, calls=%fused_computation.1 | custom fusion | bytes 8454144 | tf_op jit(solution)/shard_map/jit(_take)/gather | solution.py:67
  448.2 6.8 copy.91
  455.0 5.0 broadcast_select_fusion.1
  460.0 336.8 %while.14 = (s32[]{:T(128)}, f32[8,4,29,256]{3,2,1,0:T(8,128)}, f32[8,4,512,64]{2,3,1,0:T(8,128)}, f32[8,4,512,64]{2,3,1,0:T(8,128)}, f32[8,4]{1,0:T(8,128)S(1)}...) while((s32[]{:T(128)}, f32[8,4,29,256]{3,2,1,0:T(8,128)}, f32[8,4,512,64]{2,3,1,0:T(8,128)}, ...), condition=%wide.region_15.16_spmd, body=%wide.region_4.15_spmd.sunk | while | flops 729014272 | bytes 76312840 | solution.py:74
  464.6 4.6 fusion.108
  470.0 6.3 fusion.110
  476.3 9.6 fusion.111
  491.4 4.8 fusion.114
  496.5 2.9 broadcast_multiply_fusion.12
  506.6 4.6 fusion.108
  512.1 6.3 fusion.110
  518.4 9.6 fusion.111
  533.5 4.8 fusion.114
  538.5 2.9 broadcast_multiply_fusion.12
  548.6 4.6 fusion.108
  554.1 6.3 fusion.110
  560.4 9.6 fusion.111
  575.5 4.8 fusion.114
  580.6 2.9 broadcast_multiply_fusion.12
  590.7 4.6 fusion.108
  596.1 6.3 fusion.110
  602.4 9.6 fusion.111
  617.6 4.8 fusion.114
  622.6 2.9 broadcast_multiply_fusion.12
  632.7 4.6 fusion.108
  638.2 6.3 fusion.110
  644.5 9.6 fusion.111
  659.6 4.8 fusion.114
  664.6 2.9 broadcast_multiply_fusion.12
  674.7 4.6 fusion.108
  680.2 6.3 fusion.110
  686.5 9.6 fusion.111
  701.6 4.8 fusion.114
  716.8 4.6 fusion.108
  722.3 6.3 fusion.110
  728.5 9.6 fusion.111
  743.7 4.8 fusion.114
  748.7 2.9 broadcast_multiply_fusion.12
  758.8 4.6 fusion.108
  764.3 6.3 fusion.110
  770.6 9.6 fusion.111
  785.7 4.8 fusion.114
  790.8 2.9 broadcast_multiply_fusion.12
  796.8 6.9 copy.101
  803.7 47.4 %scatter_custom_fusion.1 = f32[32768,64]{1,0:T(8,128)} fusion(s32[16384]{0:T(1024)S(1)} %bitcast.187, f32[16384,64]{1,0:T(8,128)} %bitcast.169, f32[]{:T(128)} %constant.162.clone.1), kind=kCustom, calls=%fused_computation.140 | custom fusion | bytes 8389120 | tf_op jit(solution)/shard_map/scatter | solution.py:79
  851.1 12.7 copy.96
  863.8 103.4 %all_to_all.19 = f32[64,512,64]{1,2,0:T(8,128)} all-to-all(f32[64,512,64]{1,2,0:T(8,128)} %copy.96), channel_id=1, replica_groups=mesh['gauss'=64,'view'=2] {'gauss'}, dimensions={0} | all-to-all | bytes 16777216 | tf_op jit(solution)/shard_map/all_to_all | solution.py:82
  967.1 12.2 copy.102
  979.3 215.3 %scatter_custom_fusion.2 = f32[32768,64]{1,0:T(8,128)} fusion(s32[32768]{0:T(1024)} %bitcast.183, f32[32768,64]{1,0:T(8,128)} %bitcast.167, f32[]{:T(128)} %constant.162.clone.1), kind=kCustom, calls=%fused_computation.138 | custom fusion | flops 2097152 | bytes 8389120 | tf_op jit(solution)/shard_map/scatter-add | solution.py:86
  1197.3 68.7 %all-reduce.10.cloned.1.call-done = f32[64,32768]{0,1:T(8,128)} async-done(((f32[64,32768]{0,1:T(8,128)}), f32[64,32768]{0,1:T(8,128)}) %all-reduce.10.cloned.1.call-update) | async-done | bytes 8388624 | tf_op jit(solution)/shard_map/psum | solution.py:90
  1266.0 5.7 constant_dynamic-slice_fusion.1
  1271.7 6.8 copy.99
  (359 shorter events, 121.1 us)
Async XLA Ops:
  9.7 2.0 copy-start.3
  17.2 5.5 copy-start.8
  17.2 5.5 copy-start.6
  88.7 24.2 %all-to-all-start = ((s32[64,1,512]{2,1,0:T(1,128)}), s32[64,1,512]{2,1,0:T(1,128)S(1)}, u32[]{:S(2)}, u32[]{:S(2)}) async-start(s32[64,1,512]{2,1,0:T(1,128)} %bitcast.26), calls=%async_computation | async-start | bytes 262144 | tf_op jit(solution)/shard_map/all_to_all | solution.py:62
  113.0 114.0 %copy-start.7 = (s32[32768,1]{0,1:T(1,128)}, s32[32768,1]{0,1:T(1,128)S(1)}, u32[]{:S(2)}) copy-start(s32[32768,1]{0,1:T(1,128)S(1)} %compare_select_fusion) | copy-start | bytes 393220
  248.3 10.3 copy-start.5
  248.3 127.5 %all-to-all-start.1 = ((f32[64,512,64]{1,2,0:T(8,128)}), f32[64,512,64]{1,2,0:T(8,128)}, u32[]{:S(2)}, u32[]{:S(2)}) async-start(f32[64,512,64]{1,2,0:T(8,128)} %broadcast_select_fusion), calls=%async_computation.1 | async-start | bytes 16777216 | tf_op jit(solution)/shard_map/all_to_all | solution.py:66
  258.5 1.8 copy-start.9
  258.5 1007.5 %all-reduce.10.cloned.1.call-start = ((), (), s32[]{:S(2)}) async-start(), calls=%async_computation.3 | async-start | bytes 33554432 | tf_op jit(solution)/shard_map/psum | solution.py:90
  470.0 6.3 copy-start
  486.4 1.6 copy-start.1
  486.4 2.2 copy-start.2
  512.0 6.4 copy-start
  528.4 1.6 copy-start.1
  528.4 2.2 copy-start.2
  554.0 6.4 copy-start
  570.5 1.6 copy-start.1
  570.5 2.2 copy-start.2
  596.1 6.4 copy-start
  612.5 1.6 copy-start.1
  612.5 2.2 copy-start.2
  638.1 6.4 copy-start
  654.5 1.6 copy-start.1
  654.6 2.2 copy-start.2
  680.1 6.4 copy-start
  696.6 1.6 copy-start.1
  696.6 2.2 copy-start.2
  722.2 6.4 copy-start
  738.6 1.6 copy-start.1
  738.6 2.2 copy-start.2
  764.2 6.4 copy-start
  780.7 1.6 copy-start.1
  780.7 2.2 copy-start.2
  1194.6 1.2 copy-start.4
Sparse Core Ops, SparseCore 0:
  1194.8 71.1 all-reduce.9
where the time goes:
time: 1300 us; the launch traced here: 1290 us
  local copies, waits for them, and re-layouts  438 us (34%)
  other arithmetic  432 us (33%)
  waiting for transfers between devices  184 us (14%)
  blocking collectives  103 us (8%)
  matrix products  89.5 us (7%)
  starting transfers between devices  22.2 us (2%)
  between operations  14.4 us (1%)
    scatter-add x1, other arithmetic, per_device(): row_totals = jnp.zeros((own_cols, width), jnp.float32).at[asked.reshape(-...  215 us
    gather x2, local copies, waits for them, and re-layouts, per_device(): jnp.take(row_major, asked.reshape(-1), axis=0)  127 us
    another operation x50, other arithmetic  121 us
    all_to_all x1, waiting for transfers between devices, per_device(): lax.all_to_all(fetched, 'gauss', split_axis=0, concat_axis=0, tiled=True)  115 us
    all_to_all x1, blocking collectives, per_device(): lax.all_to_all(outgoing, 'gauss', split_axis=0, concat_axis=0, tiled=True)  103 us
    dot_general x24, matrix products, render(): lax.dot_general(colour, weight, (((0,), (0,)), ((), ())), precision=lax.P...  89.5 us
    psum x1, waiting for transfers between devices, per_device(): summed = lax.psum(totals, 'view')  68.7 us
    gather x2, local copies, waits for them, and re-layouts, per_device(): jnp.take(sent.reshape(shards * capacity, width), slot_of, axis=0)  67 us
  transfers between devices with their start and end apart: 3, of which 2 were waited for; matrix products, arithmetic and copies ran while one was open for 1% of the time, Pallas kernels for 0%

commit v1 on v0

v1 whole, which is shorter than its diff:
```python
import functools

import jax
import jax.numpy as jnp
from jax import lax
from jax.experimental import pallas as pl
from jax.experimental.pallas import tpu as pltpu
from jax.sharding import PartitionSpec as P

CHANNELS = 29
TILE_SIDE = 16
PIXELS = 256
VIEWS = 8
SCREEN_TILES = 8160
GEOM = 6
WIRE = 40
TWO_PI = 6.283185307179586
LOG2E = 1.4426950408889634
VMEM = pltpu.VMEM
SMEM = pltpu.SMEM
F32 = jnp.float32
BF16 = jnp.bfloat16
I32 = jnp.int32
ROWS = 32
GROUP = 16


def params():
    return pltpu.CompilerParams(vmem_limit_bytes=60 * 2**20)


def whole(space):
    return pl.BlockSpec(memory_space=space)


def iota(shape, dim):
    return lax.broadcasted_iota(I32, shape, dim)


def dot(a, b, contract=((1,), (0,))):
    return lax.dot_general(a, b, (contract, ((), ())), preferred_element_type=F32)


def split(x):
    high = x.astype(BF16).astype(F32)
    return high, x - high


def route_kernel(shard_ref, row_ref, view_ref, ask_row_ref, ask_view_ref, valid_ref, slot_ref):
    shards, capacity = ask_row_ref.shape
    chunks, width = shard_ref.shape
    before = (iota((width, width), 0) < iota((width, width), 1)).astype(F32).astype(BF16)
    spare = iota((shards, capacity), 1)

    def step(i, state):
        carry, total = state
        shard = shard_ref[pl.ds(i, 1), :]
        row = row_ref[pl.ds(i, 1), :]
        view = view_ref[pl.ds(i, 1), :]
        named = iota((shards, width), 0) == shard
        hot = named.astype(F32)
        seen = dot(hot.astype(BF16), before) + carry
        place = jnp.sum(hot * seen, axis=0, keepdims=True).astype(I32)
        slot_ref[pl.ds(i, 1), :] = shard * capacity + place
        at = (iota((capacity, width), 0) == place).astype(F32).astype(BF16)
        low = (row & 255).astype(F32)
        high = (row >> 8).astype(F32)
        values = jnp.concatenate([hot * low, hot * high, hot * view.astype(F32), hot], axis=0)
        total = total + dot(values.astype(BF16), at, ((1,), (1,)))
        return carry + jnp.sum(hot, axis=1, keepdims=True), total

    def pair(i, state):
        for u in range(4):
            state = step(4 * i + u, state)
        return state

    start = (jnp.zeros((shards, 1), F32), jnp.zeros((4 * shards, capacity), F32))
    _, total = lax.fori_loop(0, chunks // 4, pair, start)
    low, high, view, valid = (total[shards * k : shards * (k + 1)].astype(I32) for k in range(4))
    ask_row_ref[...] = jnp.where(valid > 0, low + 256 * high, spare)
    ask_view_ref[...] = view
    valid_ref[...] = valid


def route(shard, row, view, shards, capacity):
    grid = jax.ShapeDtypeStruct((shards, capacity), I32)
    return pl.pallas_call(
        route_kernel,
        out_shape=(grid, grid, grid, jax.ShapeDtypeStruct(shard.shape, I32)),
        in_specs=[whole(VMEM)] * 3,
        out_specs=(whole(VMEM),) * 4,
        compiler_params=params(),
        name="route",
    )(shard, row, view)


def fetch_kernel(ask_ref, ask_vec_ref, cos_ref, rows_ref, out_ref, clash_ref, table, got):
    source = pl.program_id(0)
    width, columns = rows_ref.shape
    capacity = got.shape[0]

    @pl.when(source == 0)
    def _():
        def turn(i, _):
            at = pl.multiple_of(i * capacity, capacity)
            table[pl.ds(at, capacity), 0:width] = rows_ref[:, pl.ds(at, capacity)].T
            return 0

        lax.fori_loop(0, columns // capacity, turn, 0)
        asked = ask_vec_ref[...]
        lane = iota(asked.shape, 1) % GROUP
        same = jnp.zeros(asked.shape, F32)
        for d in range(1, GROUP):
            same = jnp.where((pltpu.roll(asked, d, 1) == asked) & (lane >= d), 1.0, same)
        pool = (iota((capacity, 128), 0) // GROUP == iota((capacity, 128), 1)).astype(F32)
        clash_ref[...] = dot(same.astype(BF16), pool.astype(BF16)).astype(I32)

    def pick(i, _):
        at = pl.multiple_of(i * ROWS, ROWS)
        for u in range(ROWS):
            got[pl.ds(at + u, 1), :] = table[pl.ds(ask_ref[source, at + u], 1), :]
        return 0

    lax.fori_loop(0, capacity // ROWS, pick, 0)
    turned = got[...].T
    second = jnp.concatenate(
        [
            jnp.zeros((GEOM, capacity), F32),
            turned[GEOM + CHANNELS : GEOM + 2 * CHANNELS],
            jnp.zeros((WIRE - GEOM - CHANNELS, capacity), F32),
        ],
        axis=0,
    )
    out_ref[0] = turned[0:WIRE] + cos_ref[0] * second


def fetch(asked, cos, gauss_rows):
    shards, capacity = asked.shape
    width, columns = gauss_rows.shape
    return pl.pallas_call(
        fetch_kernel,
        grid=(shards,),
        out_shape=(
            jax.ShapeDtypeStruct((shards, WIRE, capacity), F32),
            jax.ShapeDtypeStruct((shards, 128), I32),
        ),
        in_specs=[
            whole(SMEM),
            pl.BlockSpec((shards, capacity), lambda i: (0, 0)),
            pl.BlockSpec((1, 1, capacity), lambda i: (i, 0, 0)),
            pl.BlockSpec((width, columns), lambda i: (0, 0), pipeline_mode=pl.Buffered(1)),
        ],
        out_specs=(
            pl.BlockSpec((1, WIRE, capacity), lambda i: (i, 0, 0)),
            pl.BlockSpec((shards, 128), lambda i: (0, 0)),
        ),
        scratch_shapes=[VMEM((columns, 128), F32), VMEM((capacity, 128), F32)],
        compiler_params=params(),
        name="fetch",
    )(asked, asked, cos, gauss_rows)


def composite_kernel(
    slot_ref, wire_ref, valid_ref, cot_ref, images_ref, out_ref,
    table, rows, alpha, ratio, logs, before, weight, weight_hi, weight_lo, pull, parts, after, earlier, later,
):
    shards, _, capacity = wire_ref.shape
    tiles, length = slot_ref.shape
    half = length // 2
    side = TILE_SIDE

    def unpack(s, _):
        at = pl.multiple_of(s * capacity, capacity)
        table[pl.ds(at, capacity), 0:WIRE] = wire_ref[s].T
        return 0

    lax.fori_loop(0, shards, unpack, 0)
    above = iota((2 * half, half), 0) % half
    beside = iota((2 * half, half), 1)
    earlier[...] = (above < beside).astype(F32).astype(BF16)
    later[...] = (above > beside).astype(F32).astype(BF16)

    def put(ref, at, x):
        high, low = split(x)
        high, low = high.astype(BF16), low.astype(BF16)
        ref[pl.ds(at, side), 0:half] = high[:, 0:half]
        ref[pl.ds(at, side), half : 2 * half] = low[:, 0:half]
        ref[pl.ds(at, side), 2 * half : 3 * half] = high[:, half:]
        ref[pl.ds(at, side), 3 * half : 4 * half] = low[:, half:]

    def tile(t, _):
        def pick(i, _):
            at = pl.multiple_of(i * ROWS, ROWS)
            for u in range(ROWS):
                rows[pl.ds(at + u, 1), :] = table[pl.ds(slot_ref[t, at + u], 1), :]
            return 0

        lax.fori_loop(0, length // ROWS, pick, 0)
        turned = rows[...].T
        x0, y0, r2, r3, r4, r5 = (turned[k : k + 1] for k in range(GEOM))
        conic_a = jnp.exp(r2)
        conic_c = jnp.exp(r4)
        skew = jnp.tanh(r3)
        middle = jnp.sqrt(conic_a * conic_c)
        conic_b = 0.9 * skew * middle
        opaque = 1.0 / (1.0 + jnp.exp(-r5))
        spot = iota((side, length), 0).astype(F32) + 0.5
        dx = spot - x0
        dy = spot - y0
        scale = -0.5 * LOG2E
        part_x = (scale * conic_a) * dx * dx
        cross = (2.0 * scale * conic_b) * dx
        part_y = (scale * conic_c) * dy * dy + jnp.log2(0.99 * opaque)

        for py in range(side):
            at = py * side
            a = jnp.exp2(part_x + (cross * dy[py : py + 1] + part_y[py : py + 1]))
            log = jnp.log2(1.0 - a)
            alpha[pl.ds(at, side), :] = a
            ratio[pl.ds(at, side), :] = a * jnp.exp2(-log)
            put(logs, at, log)

        before[:, 0:half] = dot(logs[:, 0 : 2 * half], earlier[...])
        before[:, half:] = dot(logs[:, 2 * half :], earlier[...])

        for py in range(side):
            at = py * side
            b = before[pl.ds(at, side), :]
            last = (
                b[:, half - 1 : half]
                + logs[pl.ds(at, side), half - 1 : half].astype(F32)
                + logs[pl.ds(at, side), 2 * half - 1 : 2 * half].astype(F32)
            )
            b = jnp.concatenate([b[:, 0:half], b[:, half:] + last], axis=1)
            w = jnp.exp2(b) * alpha[pl.ds(at, side), :]
            high, low = split(w)
            weight[pl.ds(at, side), :] = w
            weight_hi[pl.ds(at, side), :] = high.astype(BF16)
            weight_lo[pl.ds(at, side), :] = low.astype(BF16)

        channel = iota((WIRE, length), 0)
        colour = jnp.where((channel >= GEOM) & (channel < GEOM + CHANNELS), turned[0:WIRE], 0.0)
        colour_hi, colour_lo = split(colour)
        cot = cot_ref[t]
        cot_hi, cot_lo = split(cot)
        fill = jnp.zeros((128 - 3 * WIRE, length), F32)
        fill_cot = jnp.zeros((128 - 3 * WIRE, PIXELS), F32)
        both = jnp.concatenate([colour_hi, colour_lo], axis=0).astype(BF16)
        image = dot(both, weight_hi[...], ((1,), (1,)))
        image_lo = dot(both, weight_lo[...], ((1,), (1,)))
        image = image[0:WIRE] + image[WIRE:] + image_lo[0:WIRE]
        images_ref[t] = image[GEOM : GEOM + CHANNELS]
        both = jnp.concatenate([cot_hi, cot_lo], axis=0).astype(BF16)
        grad = dot(both, weight_hi[...])
        grad_lo = dot(both, weight_lo[...])
        grad = grad[0:WIRE] + grad[WIRE:] + grad_lo[0:WIRE]
        three = jnp.concatenate([cot_hi, cot_lo, cot_hi, fill_cot], axis=0).T.astype(BF16)
        other = jnp.concatenate([colour_hi, colour_hi, colour_lo, fill], axis=0).astype(BF16)
        pull[...] = dot(three, other)

        for py in range(side):
            at = py * side
            q = pull[pl.ds(at, side), :] * weight[pl.ds(at, side), :]
            pull[pl.ds(at, side), :] = q
            put(parts, at, q)

        after[:, 0:half] = dot(parts[:, 0 : 2 * half], later[...])
        after[:, half:] = dot(parts[:, 2 * half :], later[...])

        m0 = jnp.zeros((side, length), F32)
        m1 = jnp.zeros((side, length), F32)
        m2 = jnp.zeros((side, length), F32)
        for py in range(side):
            at = py * side
            s = after[pl.ds(at, side), :]
            q = pull[pl.ds(at, side), :]
            first = s[:, half : half + 1] + q[:, half : half + 1]
            s = jnp.concatenate([s[:, 0:half] + first, s[:, half:]], axis=1)
            h = q - s * ratio[pl.ds(at, side), :]
            hy = h * dy[py : py + 1]
            m0 = m0 + h
            m1 = m1 + hy
            m2 = m2 + hy * dy[py : py + 1]

        def total(x):
            return jnp.sum(x, axis=0, keepdims=True)

        m0x = m0 * dx
        s0, sx, sy, sxx, sxy, syy = total(m0), total(m0x), total(m1), total(m0x * dx), total(m1 * dx), total(m2)
        shared = -0.5 * conic_b * sxy
        geometry = (
            conic_a * sx + conic_b * sy,
            conic_b * sx + conic_c * sy,
            shared - 0.5 * conic_a * sxx,
            -0.9 * (1.0 - skew * skew) * middle * sxy,
            shared - 0.5 * conic_c * syy,
            (1.0 - opaque) * s0,
        )
        for k, value in enumerate(geometry):
            grad = jnp.where(channel == k, value, grad)
        rows[:, 0:WIRE] = grad.T

        def give(i, _):
            at = pl.multiple_of(i * ROWS, ROWS)
            for u in range(ROWS):
                table[pl.ds(slot_ref[t, at + u], 1), :] = rows[pl.ds(at + u, 1), :]
            return 0

        lax.fori_loop(0, length // ROWS, give, 0)
        return 0

    lax.fori_loop(0, tiles, tile, 0)

    def pack(s, _):
        at = pl.multiple_of(s * capacity, capacity)
        turned = table[pl.ds(at, capacity), :].T
        out_ref[s] = jnp.where(valid_ref[s] > 0, turned[0:WIRE], 0.0)
        return 0

    lax.fori_loop(0, shards, pack, 0)


def composite(slot, wire, valid, cot):
    shards, _, capacity = wire.shape
    tiles, length = slot.shape
    full = (PIXELS, length)
    return pl.pallas_call(
        composite_kernel,
        out_shape=(
            jax.ShapeDtypeStruct((tiles, CHANNELS, PIXELS), F32),
            jax.ShapeDtypeStruct(wire.shape, F32),
        ),
        in_specs=[whole(SMEM), whole(VMEM), whole(VMEM), whole(VMEM)],
        out_specs=(whole(VMEM), whole(VMEM)),
        scratch_shapes=[
            VMEM((shards * capacity, 128), F32),
            VMEM((length, 128), F32),
            VMEM(full, F32),
            VMEM(full, F32),
            VMEM((PIXELS, 2 * length), BF16),
            VMEM(full, F32),
            VMEM(full, F32),
            VMEM(full, BF16),
            VMEM(full, BF16),
            VMEM(full, F32),
            VMEM((PIXELS, 2 * length), BF16),
            VMEM(full, F32),
            VMEM((length, length // 2), BF16),
            VMEM((length, length // 2), BF16),
        ],
        compiler_params=params(),
        name="composite",
    )(slot, wire, valid, cot)


def collect_kernel(half_ref, ask_ref, clash_ref, cos_ref, wire_ref, keep_ref, send_ref, table, rows):
    source = pl.program_id(0)
    width, half = keep_ref.shape
    capacity = rows.shape[0]

    @pl.when(source == 0)
    def _():
        table[...] = jnp.zeros_like(table)
        rows[...] = jnp.zeros_like(rows)

    back = wire_ref[0]
    scaled = cos_ref[0] * back
    turned = jnp.concatenate([back[0 : GEOM + CHANNELS], scaled[GEOM : GEOM + CHANNELS]], axis=0)
    rows[:, 0:width] = turned.T

    def add(i, _):
        at = pl.multiple_of(i * GROUP, GROUP)

        @pl.when(clash_ref[source, i] == 0)
        def _():
            places = [ask_ref[source, at + u] for u in range(GROUP)]
            sums = [table[pl.ds(r, 1), :] + rows[pl.ds(at + u, 1), :] for u, r in enumerate(places)]
            for r, value in zip(places, sums):
                table[pl.ds(r, 1), :] = value

        @pl.when(clash_ref[source, i] != 0)
        def _():
            for u in range(GROUP):
                table[pl.ds(ask_ref[source, at + u], 1), :] += rows[pl.ds(at + u, 1), :]

        return 0

    lax.fori_loop(0, capacity // GROUP, add, 0)

    @pl.when(source == pl.num_programs(0) - 1)
    def _():
        for ref, base in ((keep_ref, half_ref[0]), (send_ref, half - half_ref[0])):
            def turn(i, _):
                at = pl.multiple_of(i * capacity, capacity)
                there = pl.multiple_of(base + at, capacity)
                ref[:, pl.ds(at, capacity)] = table[pl.ds(there, capacity), :].T[0:width]
                return 0

            lax.fori_loop(0, half // capacity, turn, 0)


def collect(half, asked, clash, cos, wire, width, columns):
    shards, _, capacity = wire.shape
    part = jax.ShapeDtypeStruct((width, columns // 2), F32)
    part_spec = pl.BlockSpec((width, columns // 2), lambda i: (0, 0), pipeline_mode=pl.Buffered(1))
    return pl.pallas_call(
        collect_kernel,
        grid=(shards,),
        out_shape=(part, part),
        in_specs=[
            whole(SMEM),
            whole(SMEM),
            whole(SMEM),
            pl.BlockSpec((1, 1, capacity), lambda i: (i, 0, 0)),
            pl.BlockSpec((1, WIRE, capacity), lambda i: (i, 0, 0)),
        ],
        out_specs=(part_spec, part_spec),
        scratch_shapes=[VMEM((columns, 128), F32), VMEM((capacity, 128), F32)],
        compiler_params=params(),
        name="collect",
    )(half, asked, clash, cos, wire)


def per_device(gauss_rows, vis_shard, vis_row, tile_index, cotangent):
    shards = lax.axis_size("gauss")
    tiles, length = vis_row.shape
    entries = tiles * length
    capacity = 2 * entries // shards
    width, columns = gauss_rows.shape
    view = jnp.broadcast_to((tile_index // SCREEN_TILES)[:, None], (tiles, length))
    chunk = (entries // 256, 256)
    ask_row, ask_view, valid, slot = route(
        vis_shard.reshape(chunk), vis_row.reshape(chunk), view.reshape(chunk), shards, capacity
    )
    requests = jnp.stack([ask_row, ask_view], axis=1)
    asked = lax.all_to_all(requests, "gauss", split_axis=0, concat_axis=0, tiled=True)
    asked_row = asked[:, 0]
    cos = jnp.cos(TWO_PI * asked[:, 1:2].astype(F32) / VIEWS)
    fetched, clash = fetch(asked_row, cos, gauss_rows)
    sent = lax.all_to_all(fetched, "gauss", split_axis=0, concat_axis=0, tiled=True)
    cot = jnp.pad(cotangent, ((0, 0), (GEOM, WIRE - GEOM - CHANNELS), (0, 0)))
    images, outgoing = composite(
        slot.reshape(tiles, length), sent, valid.reshape(shards, 1, capacity), cot
    )
    returned = lax.all_to_all(outgoing, "gauss", split_axis=0, concat_axis=0, tiled=True)
    half = (lax.axis_index("view") * (columns // 2)).astype(I32).reshape(1)
    keep, send = collect(half, asked_row, clash, cos, returned, width, columns)
    other = lax.ppermute(send, "view", [(0, 1), (1, 0)])
    return (images, keep + other)


def solution(mesh):
    placed = (
        P(None, "gauss"),
        P(("gauss", "view"), None, None),
        P(("gauss", "view"), None),
        P(("gauss", "view")),
        P(("gauss", "view"), None, None),
    )
    return jax.shard_map(
        per_device,
        mesh=mesh,
        in_specs=placed,
        out_specs=(P(("gauss", "view"), None, None), P(None, ("gauss", "view"))),
        check_vma=False,
    )
```

time: 1300 us -> 670 us (0.52)
  Pallas kernels: 0 us -> 477 us
  local copies, waits for them, and re-layouts: 438 us -> 10.4 us
  other arithmetic: 432 us -> 10.7 us
  matrix products: 89.5 us -> 0 us
  blocking collectives: 103 us -> 21.2 us
  waiting for transfers between devices: 184 us -> 130 us
  between operations: 14.4 us -> 0.71 us
    pallas_call x0 -> x4, Pallas kernels: none -> 477 us  [the longest x1 199 us: collect(): pl.pallas_call(collect_kernel, grid=(shards,), out_shape=(part, part), in...]
    scatter-add x1 -> x0, other arithmetic: 215 us -> none  [per_device(): row_totals = jnp.zeros((own_cols, width), jnp.float32).at[asked.reshape(-...]
    gather x4 -> x0, local copies, waits for them, and re-layouts: 194 us -> none  [the longest x2 127 us: per_device(): jnp.take(row_major, asked.reshape(-1), axis=0)]
    another operation x50 -> x1, other arithmetic: 121 us -> 0.21 us  [per_device(): requests = jnp.stack([ask_row, ask_view], axis=1)]
    scatter x2 -> x0, local copies, waits for them, and re-layouts: 108 us -> none  [the longest x1 60.9 us: per_device(): jnp.zeros((shards * capacity,), jnp.int32).at[slot_of].set(row_of)]
    dot_general x24 -> x0, matrix products: 89.5 us -> none  [render(): lax.dot_general(colour, weight, (((0,), (0,)), ((), ())), precision=lax.P...]
    all_to_all x1, blocking collectives: 103 us -> 21.2 us  [per_device(): lax.all_to_all(requests, 'gauss', split_axis=0, concat_axis=0, tiled=True)]
    psum x1 -> x0, waiting for transfers between devices: 68.7 us -> none  [per_device(): summed = lax.psum(totals, 'view')]
  transfers between devices with their start and end apart: 3 -> 3, of which waited for: 2 -> 3; matrix products, arithmetic and copies ran while one was open for 1% -> 1% of each run, Pallas kernels for 0% -> 0%
where the time goes in v1:
time: 670 us; the launch traced here: 668 us
  Pallas kernels  477 us (71%)
  waiting for transfers between devices  130 us (19%)
  blocking collectives  21.2 us (3%)
  starting transfers between devices  18.3 us (3%)
  other arithmetic  10.7 us (2%)
  local copies, waits for them, and re-layouts  10.4 us (2%)
    pallas_call x1, Pallas kernels, collect(): pl.pallas_call(collect_kernel, grid=(shards,), out_shape=(part, part), in...  199 us
    pallas_call x1, Pallas kernels, composite(): pl.pallas_call(composite_kernel, out_shape=(jax.ShapeDtypeStruct((tiles,...  146 us
    pallas_call x1, Pallas kernels, fetch(): pl.pallas_call(fetch_kernel, grid=(shards,), out_shape=(jax.ShapeDtypeStr...  108 us
    all_to_all x1, waiting for transfers between devices, per_device(): lax.all_to_all(outgoing, 'gauss', split_axis=0, concat_axis=0, tiled=True)  63.2 us
    all_to_all x1, waiting for transfers between devices, per_device(): lax.all_to_all(fetched, 'gauss', split_axis=0, concat_axis=0, tiled=True)  61.1 us
    pallas_call x1, Pallas kernels, route(): pl.pallas_call(route_kernel, out_shape=(grid, grid, grid, jax.ShapeDtypeS...  23.9 us
    all_to_all x1, blocking collectives, per_device(): lax.all_to_all(requests, 'gauss', split_axis=0, concat_axis=0, tiled=True)  21.2 us
  transfers between devices with their start and end apart: 3, of which 3 were waited for; matrix products, arithmetic and copies ran while one was open for 1% of the time, Pallas kernels for 0%

profile of v1, /device:TPU:1, one launch (start us, length us, event | category | flops | bytes accessed | tf_op | source)
XLA Modules:
  0.0 668.2 jit_solution(11393513090820612525)
XLA Ops:
  0.6 0.7 and_select_fusion
  1.3 0.1 broadcast_in_dim.10
  1.4 0.1 broadcast_in_dim.11
  1.5 1.0 reduce
  2.5 0.6 reshape.22.shard_ref
  3.1 1.5 reshape.23.row_ref
  4.6 0.7 broadcast_in_dim.12.view_ref
  5.3 23.9 %route.1 = (s32[64,512]{1,0:T(8,128)}, s32[64,512]{1,0:T(8,128)}, s32[64,512]{1,0:T(8,128)}, s32[64,256]{1,0:T(8,128)}) custom-call(s32[64,256]{1,0:T(8,128)} %reshape.22.shard_ref, s32[64,256]{1,0:T(8,128)} %reshape.23.row_ref, s32[64,256]{1,0:T(8,128)} %broadcast_in_dim.12.view_ref), custom_call_target="tpu_custom_call" | custom-call | tf_op jit(solution)/shard_map/route/pallas_call | solution.py:87
  29.2 1.0 stack.9
  30.2 1.0 stack.10
  31.2 0.2 pad_add_fusion
  31.4 21.2 %all_to_all.15 = s32[64,2,512]{2,1,0:T(2,128)S(1)} all-to-all(s32[64,2,512]{2,1,0:T(2,128)S(1)} %pad_add_fusion), channel_id=1, replica_groups=mesh['gauss'=64,'view'=2] {'gauss'}, dimensions={0} | all-to-all | bytes 524288 | tf_op jit(solution)/shard_map/all_to_all | solution.py:436
  52.6 0.1 slice.8
  52.7 0.7 copy.13
  53.3 4.1 fusion.1.cos_ref
  57.4 108.0 %fetch.1 = (f32[64,40,512]{2,1,0:T(8,128)}, s32[64,128]{1,0:T(8,128)}) custom-call(s32[64,512]{1,0:T(8,128)} %bitcast.4, s32[64,512]{1,0:T(8,128)} %bitcast.5, f32[64,1,512]{2,1,0:T(1,128)} %fusion.1.cos_ref, f32[64,32768]{1,0:T(8,128)} %rows_ref.1), custom_call_target="tpu_custom_call" | custom-call | tf_op jit(solution)/shard_map/fetch/pallas_call | solution.py:140
  165.4 0.0 copy-start.3
  165.4 0.0 copy-start.2
  165.4 0.0 copy-start.1
  165.5 5.8 all-to-all-start.1
  171.3 0.0 copy-done.3
  171.3 0.6 reshape.24.slot_ref
  171.9 0.0 copy-done.2
  171.9 0.7 reshape.25.valid_ref
  172.7 0.0 copy-done.1
  172.7 0.6 copy.9
  173.3 1.2 pad.4.cot_ref
  174.5 61.1 %all-to-all-done.1.wire_ref = f32[64,40,512]{2,1,0:T(8,128)} async-done(((f32[64,40,512]{2,1,0:T(8,128)}), f32[64,40,512]{2,1,0:T(8,128)}, u32[]{:S(2)}, u32[]{:S(2)}) %all-to-all-start.1) | async-done | bytes 5242912 | tf_op jit(solution)/shard_map/all_to_all | solution.py:440
  235.5 146.2 %composite.1 = (f32[32,29,256]{2,1,0:T(8,128)}, f32[64,40,512]{2,1,0:T(8,128)}) custom-call(s32[32,512]{1,0:T(8,128)} %reshape.24.slot_ref, f32[64,40,512]{2,1,0:T(8,128)} %all-to-all-done.1.wire_ref, s32[64,1,512]{2,1,0:T(1,128)} %reshape.25.valid_ref, f32[32,40,256]{2,1,0:T(8,128)} %pad.4.cot_ref), custom_call_target="tpu_custom_call" | custom-call | tf_op jit(solution)/shard_map/composite/pallas_call | solution.py:327
  381.8 8.6 %all-to-all-start.2 = ((f32[64,40,512]{2,1,0:T(8,128)}), f32[64,40,512]{2,1,0:T(8,128)}, u32[]{:S(2)}, u32[]{:S(2)}) async-start(f32[64,40,512]{2,1,0:T(8,128)} %get-tuple-element.19), calls=%async_computation.2 | async-start | bytes 10485760 | tf_op jit(solution)/shard_map/all_to_all | solution.py:445
  390.4 0.0 copy-start
  390.5 63.2 %all-to-all-done.2.wire_ref = f32[64,40,512]{2,1,0:T(8,128)} async-done(((f32[64,40,512]{2,1,0:T(8,128)}), f32[64,40,512]{2,1,0:T(8,128)}, u32[]{:S(2)}, u32[]{:S(2)}) %all-to-all-start.2) | async-done | bytes 5242912 | tf_op jit(solution)/shard_map/all_to_all | solution.py:445
  453.7 199.0 %collect.1 = (f32[64,16384]{1,0:T(8,128)}, f32[64,16384]{1,0:T(8,128)}) custom-call(s32[1]{0:T(128)} %bitcast.half_ref, s32[64,512]{1,0:T(8,128)} %bitcast.6, s32[64,128]{1,0:T(8,128)} %get-tuple-element.18.clash_ref, f32[64,1,512]{2,1,0:T(1,128)} %fusion.1.cos_ref, f32[64,40,512]{2,1,0:T(8,128)} %all-to-all-done.2.wire_ref), custom_call_target="tpu_custom_call" | custom-call | tf_op jit(solution)/shard_map/collect/pallas_call | solution.py:406
  652.7 3.8 collective-permute-start
  656.5 0.0 copy-done
  656.5 1.5 copy.10
  658.0 5.5 collective-permute-done
  663.5 4.7 add.6
Async XLA Ops:
  165.4 5.9 copy-start.3
  165.4 6.5 copy-start.2
  165.4 7.3 %copy-start.1 = (f32[32,29,256]{2,0,1:T(8,128)S(1)}, f32[32,29,256]{2,0,1:T(8,128)}, u32[]{:S(2)}) copy-start(f32[32,29,256]{2,0,1:T(8,128)} %param.9) | copy-start | bytes 2850820
  165.5 70.1 %all-to-all-start.1 = ((f32[64,40,512]{2,1,0:T(8,128)}), f32[64,40,512]{2,1,0:T(8,128)}, u32[]{:S(2)}, u32[]{:S(2)}) async-start(f32[64,40,512]{2,1,0:T(8,128)} %get-tuple-element.15), calls=%async_computation.1 | async-start | bytes 10485760 | tf_op jit(solution)/shard_map/all_to_all | solution.py:440
  381.8 71.9 %all-to-all-start.2 = ((f32[64,40,512]{2,1,0:T(8,128)}), f32[64,40,512]{2,1,0:T(8,128)}, u32[]{:S(2)}, u32[]{:S(2)}) async-start(f32[64,40,512]{2,1,0:T(8,128)} %get-tuple-element.19), calls=%async_computation.2 | async-start | bytes 10485760 | tf_op jit(solution)/shard_map/all_to_all | solution.py:445
  390.4 266.1 %copy-start = (f32[32,29,256]{2,1,0:T(8,128)S(1)}, f32[32,29,256]{2,1,0:T(8,128)}, u32[]{:S(2)}) copy-start(f32[32,29,256]{2,1,0:T(8,128)} %get-tuple-element.24) | copy-start | bytes 2850820
  652.7 10.8 %collective-permute-start = (f32[64,16384]{1,0:T(8,128)}, f32[64,16384]{1,0:T(8,128)S(1)}, u32[]{:S(2)}, u32[]{:S(2)}) collective-permute-start(f32[64,16384]{1,0:T(8,128)} %get-tuple-element.21), channel_id=1, source_target_pairs={{0,1},{1,0},{2,3},{3,2},{4,5},{5,4},{6,7},{7,6},{8,9},{9,8},{10,11... | collective-permute-start | bytes 12582920 | tf_op jit(solution)/shard_map/ppermute | solution.py:448

commit v2 on v0

v2 whole, which is shorter than its diff:
```python
import functools

import jax
import jax.numpy as jnp
from jax import lax
from jax.experimental import pallas as pl
from jax.experimental.pallas import tpu as pltpu
from jax.sharding import PartitionSpec as P

CHANNELS = 29
TILE_SIDE = 16
PIXELS = 256
VIEWS = 8
SCREEN_TILES = 8160
GEOM = 6
WIRE = 40
TWO_PI = 6.283185307179586
LOG2E = 1.4426950408889634
VMEM = pltpu.VMEM
SMEM = pltpu.SMEM
F32 = jnp.float32
BF16 = jnp.bfloat16
I32 = jnp.int32
ROWS = 32
GROUP = 16
BLOCK = 128


def params(**more):
    return pltpu.CompilerParams(vmem_limit_bytes=60 * 2**20, **more)


def whole(space):
    return pl.BlockSpec(memory_space=space)


def iota(shape, dim):
    return lax.broadcasted_iota(I32, shape, dim)


def dot(a, b, contract=((1,), (0,))):
    return lax.dot_general(a, b, (contract, ((), ())), preferred_element_type=F32)


def split(x):
    high = x.astype(BF16).astype(F32)
    return high, x - high


def route_kernel(shard_ref, row_ref, view_ref, ask_ref, valid_ref, entry_ref, slot_ref):
    shards, _, capacity = ask_ref.shape
    chunks, width = shard_ref.shape
    step = 4
    before = (iota((width, width), 0) < iota((width, width), 1)).astype(F32).astype(BF16)
    spare = iota((shards, capacity), 1)
    lane = iota((1, width), 1).astype(F32)

    def some(i, state):
        carry, total = state
        shard = [shard_ref[pl.ds(step * i + u, 1), :] for u in range(step)]
        hot = [(iota((shards, width), 0) == shard[u]).astype(F32) for u in range(step)]
        seen = dot(jnp.concatenate(hot, axis=0).astype(BF16), before)
        at, values = [], []
        for u in range(step):
            here = step * i + u
            place = jnp.sum(hot[u] * (seen[shards * u : shards * (u + 1)] + carry), axis=0, keepdims=True)
            carry = carry + jnp.sum(hot[u], axis=1, keepdims=True)
            place = place.astype(I32)
            slot_ref[pl.ds(here, 1), :] = shard[u] * capacity + place
            at.append((iota((capacity, width), 0) == place).astype(F32).astype(BF16))
            row = row_ref[pl.ds(here, 1), :]
            parts = (
                (row & 255).astype(F32),
                (row >> 8).astype(F32),
                (view_ref[pl.ds(here, 1), :] + 1).astype(F32),
                lane,
                jnp.full((1, width), here, I32).astype(F32),
            )
            values.append(jnp.concatenate([hot[u] * part for part in parts], axis=0).astype(BF16))
        at = jnp.concatenate(at, axis=1)
        values = jnp.concatenate(values, axis=1)
        return carry, total + dot(values, at, ((1,), (1,)))

    start = (jnp.zeros((shards, 1), F32), jnp.zeros((5 * shards, capacity), F32))
    _, total = lax.fori_loop(0, chunks // step, some, start)
    low, high, view, lane, chunk = (total[shards * k : shards * (k + 1)].astype(I32) for k in range(5))
    valid = view > 0
    ask_ref[:, 0, :] = jnp.where(valid, low + 256 * high, spare)
    ask_ref[:, 1, :] = jnp.where(valid, view - 1, 0)
    valid_ref[...] = valid.astype(I32)
    entry_ref[...] = lane + width * chunk


def route(shard, row, view, shards, capacity):
    grid = jax.ShapeDtypeStruct((shards, capacity), I32)
    return pl.pallas_call(
        route_kernel,
        out_shape=(
            jax.ShapeDtypeStruct((shards, 2, capacity), I32),
            grid,
            grid,
            jax.ShapeDtypeStruct(shard.shape, I32),
        ),
        in_specs=[whole(VMEM)] * 3,
        out_specs=(whole(VMEM),) * 4,
        compiler_params=params(),
        name="route",
    )(shard, row, view)


def exchange(pick, finish, table, even, odd, send, out_ref, send_sem, recv_sem, own_sem, ready):
    shards, _, capacity = send.shape
    blocks = capacity // BLOCK
    me = lax.axis_index("gauss")

    def other(k):
        return lax.rem(me + k + shards, shards)

    def copy(to, by):
        return pltpu.make_async_remote_copy(
            src_ref=send.at[to],
            dst_ref=out_ref.at[by],
            send_sem=send_sem.at[to],
            recv_sem=recv_sem.at[by],
            device_id={"gauss": to},
            device_id_type=pl.DeviceIdType.MESH,
        )

    own = pltpu.make_async_copy(send.at[me], out_ref.at[me], own_sem)
    ready()

    def one(k, _):
        to, last = other(k), other(k - 1)
        for c in range(blocks):
            now, past = (even, odd) if c % 2 == 0 else (odd, even)
            where, part = (to, c - 1) if c else (last, blocks - 1)
            finish(past, where, part)
            for u in range(BLOCK):
                now[u : u + 1, :] = table[pl.ds(pick(to, c * BLOCK + u), 1), :]
            if c == 0:

                @pl.when(k == 1)
                def _():
                    own.start()

                @pl.when(k > 1)
                def _():
                    copy(last, me).start()

        return 0

    lax.fori_loop(0, shards, one, 0)
    last = other(-1)
    finish(odd, last, blocks - 1)
    copy(last, me).start()
    own.wait()

    def end(k, _):
        copy(other(k), me).wait_send()
        copy(me, other(-k)).wait_recv()
        return 0

    lax.fori_loop(1, shards, end, 0)


def greet():
    shards = lax.axis_size("gauss")
    me = lax.axis_index("gauss")
    barrier = pltpu.get_barrier_semaphore()

    def hail(k, _):
        pl.semaphore_signal(
            barrier, inc=1, device_id={"gauss": lax.rem(me + k, shards)}, device_id_type=pl.DeviceIdType.MESH
        )
        return 0

    lax.fori_loop(1, shards, hail, 0)

    def wait():
        pl.semaphore_wait(barrier, shards - 1)

    return wait


def exchange_scratch(shards, capacity):
    return [
        VMEM((BLOCK, 128), F32),
        VMEM((BLOCK, 128), F32),
        VMEM((shards, WIRE, capacity), F32),
        pltpu.SemaphoreType.DMA((shards,)),
        pltpu.SemaphoreType.DMA((shards,)),
        pltpu.SemaphoreType.DMA,
    ]


def fetch_kernel(
    ask_ref, ask_vec_ref, cos_ref, rows_ref, out_ref, clash_ref, table, even, odd, send, send_sem, recv_sem, own_sem
):
    width, columns = rows_ref.shape
    shards, _, capacity = send.shape
    wait = greet()

    def turn(i, _):
        at = pl.multiple_of(i * 512, 512)
        table[pl.ds(at, 512), 0:width] = rows_ref[:, pl.ds(at, 512)].T
        return 0

    lax.fori_loop(0, columns // 512, turn, 0)
    asked = ask_vec_ref[...]
    lane = iota(asked.shape, 1) % GROUP
    same = jnp.zeros(asked.shape, F32)
    for d in range(1, GROUP):
        same = jnp.where((pltpu.roll(asked, d, 1) == asked) & (lane >= d), 1.0, same)
    pool = (iota((capacity, 128), 0) // BLOCK == iota((capacity, 128), 1)).astype(F32)
    clash_ref[...] = dot(same.astype(BF16), pool.astype(BF16)).astype(I32)

    def pick(to, slot):
        return ask_ref[to * capacity + slot]

    def finish(rows, to, part):
        turned = rows[...].T
        second = jnp.concatenate(
            [
                jnp.zeros((GEOM, BLOCK), F32),
                turned[GEOM + CHANNELS : GEOM + 2 * CHANNELS],
                jnp.zeros((WIRE - GEOM - CHANNELS, BLOCK), F32),
            ],
            axis=0,
        )
        lanes = slice(part * BLOCK, (part + 1) * BLOCK)
        send[to, :, lanes] = turned[0:WIRE] + cos_ref[to, :, lanes] * second

    exchange(pick, finish, table, even, odd, send, out_ref, send_sem, recv_sem, own_sem, wait)


def fetch(asked, cos, gauss_rows):
    shards, capacity = asked.shape
    width, columns = gauss_rows.shape
    return pl.pallas_call(
        fetch_kernel,
        out_shape=(
            jax.ShapeDtypeStruct((shards, WIRE, capacity), F32),
            jax.ShapeDtypeStruct((shards, 128), I32),
        ),
        in_specs=[whole(SMEM), whole(VMEM), whole(VMEM), whole(VMEM)],
        out_specs=(whole(pl.ANY), whole(VMEM)),
        scratch_shapes=[VMEM((columns, 128), F32)] + exchange_scratch(shards, capacity),
        compiler_params=params(collective_id=0, has_side_effects=True),
        name="fetch",
    )(asked.reshape(-1), asked, cos, gauss_rows)


def send_back_kernel(
    entry_ref, valid_ref, grads_ref, out_ref, even, odd, send, send_sem, recv_sem, own_sem
):
    capacity = send.shape[2]
    wait = greet()

    def pick(to, slot):
        return entry_ref[to * capacity + slot]

    def finish(rows, to, part):
        lanes = slice(part * BLOCK, (part + 1) * BLOCK)
        send[to, :, lanes] = jnp.where(valid_ref[to, :, lanes] > 0, rows[...].T[0:WIRE], 0.0)

    exchange(pick, finish, grads_ref, even, odd, send, out_ref, send_sem, recv_sem, own_sem, wait)


def send_back(entry, valid, grads):
    shards, _, capacity = valid.shape
    return pl.pallas_call(
        send_back_kernel,
        out_shape=jax.ShapeDtypeStruct((shards, WIRE, capacity), F32),
        in_specs=[whole(SMEM), whole(VMEM), whole(VMEM)],
        out_specs=whole(pl.ANY),
        scratch_shapes=exchange_scratch(shards, capacity),
        compiler_params=params(collective_id=1, has_side_effects=True),
        name="send_back",
    )(entry, valid, grads)


def composite_kernel(
    slot_ref, wire_ref, cot_ref, images_ref, out_ref,
    table, rows, alpha, ratio, logs, before, weight, weight_hi, weight_lo, pull, parts, after, earlier, later,
):
    t = pl.program_id(0)
    shards, _, capacity = wire_ref.shape
    length = rows.shape[0]
    half = length // 2
    side = TILE_SIDE

    @pl.when(t == 0)
    def _():
        def unpack(s, _):
            at = pl.multiple_of(s * capacity, capacity)
            table[pl.ds(at, capacity), 0:WIRE] = wire_ref[s].T
            return 0

        lax.fori_loop(0, shards, unpack, 0)
        above = iota((2 * half, half), 0) % half
        beside = iota((2 * half, half), 1)
        earlier[...] = (above < beside).astype(F32).astype(BF16)
        later[...] = (above > beside).astype(F32).astype(BF16)

    def put(ref, at, x):
        high, low = split(x)
        high, low = high.astype(BF16), low.astype(BF16)
        ref[pl.ds(at, side), 0:half] = high[:, 0:half]
        ref[pl.ds(at, side), half : 2 * half] = low[:, 0:half]
        ref[pl.ds(at, side), 2 * half : 3 * half] = high[:, half:]
        ref[pl.ds(at, side), 3 * half : 4 * half] = low[:, half:]

    def pick(i, _):
        at = pl.multiple_of(i * ROWS, ROWS)
        for u in range(ROWS):
            rows[pl.ds(at + u, 1), :] = table[pl.ds(slot_ref[t * length + at + u], 1), :]
        return 0

    lax.fori_loop(0, length // ROWS, pick, 0)
    turned = rows[...].T
    x0, y0, r2, r3, r4, r5 = (turned[k : k + 1] for k in range(GEOM))
    conic_a = jnp.exp(r2)
    conic_c = jnp.exp(r4)
    skew = jnp.tanh(r3)
    middle = jnp.sqrt(conic_a * conic_c)
    conic_b = 0.9 * skew * middle
    opaque = 1.0 / (1.0 + jnp.exp(-r5))
    spot = iota((side, length), 0).astype(F32) + 0.5
    dx = spot - x0
    dy = spot - y0
    scale = -0.5 * LOG2E
    part_x = (scale * conic_a) * dx * dx
    cross = (2.0 * scale * conic_b) * dx
    part_y = (scale * conic_c) * dy * dy + jnp.log2(0.99 * opaque)

    for py in range(side):
        at = py * side
        a = jnp.exp2(part_x + (cross * dy[py : py + 1] + part_y[py : py + 1]))
        log = jnp.log2(1.0 - a)
        alpha[pl.ds(at, side), :] = a
        ratio[pl.ds(at, side), :] = a * jnp.exp2(-log)
        put(logs, at, log)

    before[:, 0:half] = dot(logs[:, 0 : 2 * half], earlier[...])
    before[:, half:] = dot(logs[:, 2 * half :], earlier[...])

    for py in range(side):
        at = py * side
        b = before[pl.ds(at, side), :]
        last = (
            b[:, half - 1 : half]
            + logs[pl.ds(at, side), half - 1 : half].astype(F32)
            + logs[pl.ds(at, side), 2 * half - 1 : 2 * half].astype(F32)
        )
        b = jnp.concatenate([b[:, 0:half], b[:, half:] + last], axis=1)
        w = jnp.exp2(b) * alpha[pl.ds(at, side), :]
        high, low = split(w)
        weight[pl.ds(at, side), :] = w
        weight_hi[pl.ds(at, side), :] = high.astype(BF16)
        weight_lo[pl.ds(at, side), :] = low.astype(BF16)

    channel = iota((WIRE, length), 0)
    colour = jnp.where((channel >= GEOM) & (channel < GEOM + CHANNELS), turned[0:WIRE], 0.0)
    colour_hi, colour_lo = split(colour)
    cot = cot_ref[0]
    cot_hi, cot_lo = split(cot)
    fill = jnp.zeros((128 - 3 * WIRE, length), F32)
    fill_cot = jnp.zeros((128 - 3 * WIRE, PIXELS), F32)
    both = jnp.concatenate([colour_hi, colour_lo], axis=0).astype(BF16)
    image = dot(both, weight_hi[...], ((1,), (1,)))
    image_lo = dot(both, weight_lo[...], ((1,), (1,)))
    image = image[0:WIRE] + image[WIRE:] + image_lo[0:WIRE]
    images_ref[0] = image[GEOM : GEOM + CHANNELS]
    both = jnp.concatenate([cot_hi, cot_lo], axis=0).astype(BF16)
    grad = dot(both, weight_hi[...])
    grad_lo = dot(both, weight_lo[...])
    grad = grad[0:WIRE] + grad[WIRE:] + grad_lo[0:WIRE]
    three = jnp.concatenate([cot_hi, cot_lo, cot_hi, fill_cot], axis=0).T.astype(BF16)
    other = jnp.concatenate([colour_hi, colour_hi, colour_lo, fill], axis=0).astype(BF16)
    pull[...] = dot(three, other)

    for py in range(side):
        at = py * side
        q = pull[pl.ds(at, side), :] * weight[pl.ds(at, side), :]
        pull[pl.ds(at, side), :] = q
        put(parts, at, q)

    after[:, 0:half] = dot(parts[:, 0 : 2 * half], later[...])
    after[:, half:] = dot(parts[:, 2 * half :], later[...])

    m0 = jnp.zeros((side, length), F32)
    m1 = jnp.zeros((side, length), F32)
    m2 = jnp.zeros((side, length), F32)
    for py in range(side):
        at = py * side
        s = after[pl.ds(at, side), :]
        q = pull[pl.ds(at, side), :]
        first = s[:, half : half + 1] + q[:, half : half + 1]
        s = jnp.concatenate([s[:, 0:half] + first, s[:, half:]], axis=1)
        h = q - s * ratio[pl.ds(at, side), :]
        hy = h * dy[py : py + 1]
        m0 = m0 + h
        m1 = m1 + hy
        m2 = m2 + hy * dy[py : py + 1]

    def total(x):
        return jnp.sum(x, axis=0, keepdims=True)

    m0x = m0 * dx
    s0, sx, sy, sxx, sxy, syy = total(m0), total(m0x), total(m1), total(m0x * dx), total(m1 * dx), total(m2)
    shared = -0.5 * conic_b * sxy
    geometry = (
        conic_a * sx + conic_b * sy,
        conic_b * sx + conic_c * sy,
        shared - 0.5 * conic_a * sxx,
        -0.9 * (1.0 - skew * skew) * middle * sxy,
        shared - 0.5 * conic_c * syy,
        (1.0 - opaque) * s0,
    )
    for k, value in enumerate(geometry):
        grad = jnp.where(channel == k, value, grad)
    out_ref[:, 0:WIRE] = grad.T


def composite(slot, wire, cot):
    shards, _, capacity = wire.shape
    tiles = cot.shape[0]
    length = slot.shape[0] // tiles
    full = (PIXELS, length)
    return pl.pallas_call(
        composite_kernel,
        grid=(tiles,),
        out_shape=(
            jax.ShapeDtypeStruct((tiles, CHANNELS, PIXELS), F32),
            jax.ShapeDtypeStruct((tiles * length, 128), F32),
        ),
        in_specs=[
            whole(SMEM),
            pl.BlockSpec(wire.shape, lambda i: (0, 0, 0), pipeline_mode=pl.Buffered(1)),
            pl.BlockSpec((1, WIRE, PIXELS), lambda i: (i, 0, 0)),
        ],
        out_specs=(
            pl.BlockSpec((1, CHANNELS, PIXELS), lambda i: (i, 0, 0)),
            pl.BlockSpec((length, 128), lambda i: (i, 0)),
        ),
        scratch_shapes=[
            VMEM((shards * capacity, 128), F32),
            VMEM((length, 128), F32),
            VMEM(full, F32),
            VMEM(full, F32),
            VMEM((PIXELS, 2 * length), BF16),
            VMEM(full, F32),
            VMEM(full, F32),
            VMEM(full, BF16),
            VMEM(full, BF16),
            VMEM(full, F32),
            VMEM((PIXELS, 2 * length), BF16),
            VMEM(full, F32),
            VMEM((length, length // 2), BF16),
            VMEM((length, length // 2), BF16),
        ],
        compiler_params=params(),
        name="composite",
    )(slot, wire, cot)


def collect_kernel(half_ref, ask_ref, clash_ref, cos_ref, wire_ref, keep_ref, send_ref, table, even, odd):
    source = pl.program_id(0)
    width, half = keep_ref.shape
    capacity = wire_ref.shape[2]
    blocks = capacity // BLOCK

    @pl.when(source == 0)
    def _():
        table[...] = jnp.zeros_like(table)
        even[...] = jnp.zeros_like(even)
        odd[...] = jnp.zeros_like(odd)

    def turn(c, rows):
        lanes = slice(c * BLOCK, (c + 1) * BLOCK)
        back = wire_ref[0, :, lanes]
        scaled = cos_ref[0, :, lanes] * back
        turned = jnp.concatenate([back[0 : GEOM + CHANNELS], scaled[GEOM : GEOM + CHANNELS]], axis=0)
        rows[:, 0:width] = turned.T

    def add(c, rows):
        base = source * capacity + c * BLOCK
        for first in range(0, BLOCK, GROUP):
            places = [ask_ref[jnp.maximum(base, 0) + first + u] for u in range(GROUP)]
            sums = [table[pl.ds(r, 1), :] + rows[first + u : first + u + 1, :] for u, r in enumerate(places)]
            for r, value in zip(places, sums):
                table[pl.ds(r, 1), :] = value

    def add_slowly(c, rows):
        base = source * capacity + c * BLOCK

        def one(u, _):
            table[pl.ds(ask_ref[jnp.maximum(base, 0) + u], 1), :] += rows[pl.ds(u, 1), :]
            return 0

        lax.fori_loop(0, BLOCK, one, 0)

    def finish(c, rows, more):
        clear = clash_ref[jnp.maximum((source + c // blocks) * 128 + c % blocks, 0)] == 0

        @pl.when(clear)
        def _():
            more()
            add(c, rows)

        @pl.when(jnp.logical_not(clear))
        def _():
            more()
            add_slowly(c, rows)

    for c in range(blocks):
        now, past = (even, odd) if c % 2 == 0 else (odd, even)
        finish(c - 1, past, functools.partial(turn, c, now))

    @pl.when(source == pl.num_programs(0) - 1)
    def _():
        finish(blocks - 1, odd, lambda: None)
        for ref, base in ((keep_ref, half_ref[0]), (send_ref, half - half_ref[0])):

            def back(i, _):
                at = pl.multiple_of(i * capacity, capacity)
                there = pl.multiple_of(base + at, capacity)
                ref[:, pl.ds(at, capacity)] = table[pl.ds(there, capacity), :].T[0:width]
                return 0

            lax.fori_loop(0, half // capacity, back, 0)


def collect(half, asked, clash, cos, wire, width, columns):
    shards, _, capacity = wire.shape
    part = jax.ShapeDtypeStruct((width, columns // 2), F32)
    part_spec = pl.BlockSpec((width, columns // 2), lambda i: (0, 0), pipeline_mode=pl.Buffered(1))
    return pl.pallas_call(
        collect_kernel,
        grid=(shards,),
        out_shape=(part, part),
        in_specs=[
            whole(SMEM),
            whole(SMEM),
            whole(SMEM),
            pl.BlockSpec((1, 1, capacity), lambda i: (i, 0, 0)),
            pl.BlockSpec((1, WIRE, capacity), lambda i: (i, 0, 0)),
        ],
        out_specs=(part_spec, part_spec),
        scratch_shapes=[VMEM((columns, 128), F32), VMEM((BLOCK, 128), F32), VMEM((BLOCK, 128), F32)],
        compiler_params=params(),
        name="collect",
    )(half, asked.reshape(-1), clash.reshape(-1), cos, wire)


def per_device(gauss_rows, vis_shard, vis_row, tile_index, cotangent):
    shards = lax.axis_size("gauss")
    tiles, length = vis_row.shape
    entries = tiles * length
    capacity = 2 * entries // shards
    width, columns = gauss_rows.shape
    view = jnp.broadcast_to((tile_index // SCREEN_TILES)[:, None], (tiles, length))
    chunk = (entries // 256, 256)
    requests, valid, entry, slot = route(
        vis_shard.reshape(chunk), vis_row.reshape(chunk), view.reshape(chunk), shards, capacity
    )
    asked = lax.all_to_all(requests, "gauss", split_axis=0, concat_axis=0, tiled=True)
    asked_row = asked[:, 0]
    cos = jnp.cos(TWO_PI * asked[:, 1:2].astype(F32) / VIEWS)
    fetched, clash = fetch(asked_row, cos, gauss_rows)
    cot = jnp.pad(cotangent, ((0, 0), (GEOM, WIRE - GEOM - CHANNELS), (0, 0)))
    images, grads = composite(slot.reshape(-1), fetched, cot)
    returned = send_back(entry.reshape(-1), valid.reshape(shards, 1, capacity), grads)
    half = (lax.axis_index("view") * (columns // 2)).astype(I32).reshape(1)
    keep, send = collect(half, asked_row, clash, cos, returned, width, columns)
    other = lax.ppermute(send, "view", [(0, 1), (1, 0)])
    return (images, keep + other)


def solution(mesh):
    placed = (
        P(None, "gauss"),
        P(("gauss", "view"), None, None),
        P(("gauss", "view"), None),
        P(("gauss", "view")),
        P(("gauss", "view"), None, None),
    )
    return jax.shard_map(
        per_device,
        mesh=mesh,
        in_specs=placed,
        out_specs=(P(("gauss", "view"), None, None), P(None, ("gauss", "view"))),
        check_vma=False,
    )
```

time: 1300 us -> 426 us (0.33)
  the two profiles are of different devices: /device:TPU:1 before, /device:TPU:7 now
where the time goes in v2:
time: 426 us; the launch traced here: 423 us
  Pallas kernels  382 us (90%)
  local copies, waits for them, and re-layouts  13 us (3%)
  starting transfers between devices  10.9 us (3%)
  other arithmetic  10.5 us (2%)
  waiting for transfers between devices  5.98 us (1%)
    pallas_call x1, Pallas kernels, fetch(): pl.pallas_call(fetch_kernel, out_shape=(jax.ShapeDtypeStruct((shards, WIR...  111 us
    pallas_call x1, Pallas kernels, send_back(): pl.pallas_call(send_back_kernel, out_shape=jax.ShapeDtypeStruct((shards,...  109 us
    pallas_call x1, Pallas kernels, collect(): pl.pallas_call(collect_kernel, grid=(shards,), out_shape=(part, part), in...  77.5 us
    pallas_call x1, Pallas kernels, composite(): pl.pallas_call(composite_kernel, grid=(tiles,), out_shape=(jax.ShapeDtype...  70.3 us
    pallas_call x1, Pallas kernels, route(): pl.pallas_call(route_kernel, out_shape=(jax.ShapeDtypeStruct((shards, 2,...  14.9 us
    all_to_all x1, starting transfers between devices, per_device(): lax.all_to_all(requests, 'gauss', split_axis=0, concat_axis=0, tiled=True)  10.9 us
  transfers between devices with their start and end apart: 2, of which 2 were waited for; matrix products, arithmetic and copies ran while one was open for 2% of the time, Pallas kernels for 0%

profile of v2, /device:TPU:7, one launch (start us, length us, event | category | flops | bytes accessed | tf_op | source)
XLA Modules:
  0.0 423.3 jit_solution(8960657674184197325)
XLA Ops:
  0.6 1.0 reduce
  1.6 0.6 reshape.28.shard_ref
  2.3 0.7 and_select_fusion
  2.9 0.1 broadcast_in_dim.10
  3.0 0.1 broadcast_in_dim.11
  3.1 1.5 reshape.29.row_ref
  4.6 0.7 broadcast_in_dim.12.view_ref
  5.3 14.9 %route.1 = (s32[64,2,512]{2,1,0:T(2,128)}, s32[64,512]{1,0:T(8,128)}, s32[64,512]{1,0:T(8,128)}, s32[64,256]{1,0:T(8,128)}) custom-call(s32[64,256]{1,0:T(8,128)} %reshape.28.shard_ref, s32[64,256]{1,0:T(8,128)} %reshape.29.row_ref, s32[64,256]{1,0:T(8,128)} %broadcast_in_dim.12.view_ref), custom_call_target="tpu_custom_call" | custom-call | tf_op jit(solution)/shard_map/route/pallas_call | solution.py:96
  20.2 10.9 %all-to-all-start = ((s32[64,2,512]{2,1,0:T(2,128)}), s32[64,2,512]{2,1,0:T(2,128)S(1)}, u32[]{:S(2)}, u32[]{:S(2)}) async-start(s32[64,2,512]{2,1,0:T(2,128)} %get-tuple-element.13), calls=%async_computation | async-start | bytes 524288 | tf_op jit(solution)/shard_map/all_to_all | solution.py:567
  31.1 1.5 copy.12
  32.6 1.7 copy.9
  34.3 1.6 copy.13
  35.9 1.6 reshape.34.valid_ref
  37.6 1.2 pad.4.cot_ref
  38.8 0.1 all-to-all-done
  38.9 0.1 slice.8
  39.0 0.0 copy-start
  39.0 0.7 copy.15
  39.7 4.1 fusion.1.cos_ref
  43.8 0.0 copy-done
  43.8 111.0 %fetch.1 = (f32[64,40,512]{2,1,0:T(8,128)}, s32[64,128]{1,0:T(8,128)}) custom-call(s32[32768]{0:T(1024)} %bitcast.10, s32[64,512]{1,0:T(8,128)} %bitcast.13, f32[64,1,512]{2,1,0:T(1,128)} %fusion.1.cos_ref, f32[64,32768]{1,0:T(8,128)} %rows_ref.1), custom_call_target="tpu_custom_call" | custom-call | tf_op jit(solution)/shard_map/fetch/pallas_call | solution.py:239
  154.7 70.3 %composite.1 = (f32[32,29,256]{2,1,0:T(8,128)}, f32[16384,128]{1,0:T(8,128)}) custom-call(s32[16384]{0:T(1024)} %bitcast.14, f32[64,40,512]{2,1,0:T(8,128)} %get-tuple-element.14.wire_ref, f32[32,40,256]{2,1,0:T(8,128)} %pad.4.cot_ref), custom_call_target="tpu_custom_call" | custom-call | tf_op jit(solution)/shard_map/composite/pallas_call | solution.py:430
  225.0 108.6 %send_back.1.wire_ref = f32[64,40,512]{2,1,0:T(8,128)} custom-call(s32[32768]{0:T(1024)} %bitcast.12, s32[64,1,512]{2,1,0:T(1,128)} %reshape.34.valid_ref, f32[16384,128]{1,0:T(8,128)} %get-tuple-element.19.grads_ref), custom_call_target="tpu_custom_call" | custom-call | tf_op jit(solution)/shard_map/send_back/pallas_call | solution.py:271
  333.7 0.0 copy-start.1
  333.7 77.5 %collect.1 = (f32[64,16384]{1,0:T(8,128)}, f32[64,16384]{1,0:T(8,128)}) custom-call(s32[1]{0:T(128)} %bitcast.1.half_ref, s32[32768]{0:T(1024)} %bitcast.11, s32[8192]{0:T(1024)} %bitcast.17, f32[64,1,512]{2,1,0:T(1,128)} %fusion.1.cos_ref, f32[64,40,512]{2,1,0:T(8,128)} %send_back.1.wire_ref), custom_call_target="tpu_custom_call" | custom-call | tf_op jit(solution)/shard_map/collect/pallas_call | solution.py:538
  411.2 0.0 collective-permute-start
  411.2 0.0 copy-done.1
  411.2 1.5 copy.10
  412.7 5.9 %collective-permute-done = f32[64,16384]{1,0:T(8,128)S(1)} collective-permute-done((f32[64,16384]{1,0:T(8,128)}, f32[64,16384]{1,0:T(8,128)S(1)}, u32[]{:S(2)}, u32[]{:S(2)}) %collective-permute-start) | collective-permute-done | bytes 4194336 | tf_op jit(solution)/shard_map/ppermute | solution.py:576
  418.5 4.7 %add.6 = f32[64,16384]{1,0:T(8,128)} add(f32[64,16384]{1,0:T(8,128)} %get-tuple-element.20, f32[64,16384]{1,0:T(8,128)S(1)} %collective-permute-done) | non-fusion elementwise | flops 1048576 | bytes 12582912 | tf_op jit(solution)/shard_map/add | solution.py:577
Async XLA Ops:
  20.2 18.7 %all-to-all-start = ((s32[64,2,512]{2,1,0:T(2,128)}), s32[64,2,512]{2,1,0:T(2,128)S(1)}, u32[]{:S(2)}, u32[]{:S(2)}) async-start(s32[64,2,512]{2,1,0:T(2,128)} %get-tuple-element.13), calls=%async_computation | async-start | bytes 524288 | tf_op jit(solution)/shard_map/all_to_all | solution.py:567
  39.0 4.8 %copy-start = (s32[64,1,512]{2,1,0:T(1,128)}, s32[64,1,512]{2,1,0:T(1,128)S(1)}, u32[]{:S(2)}) copy-start(s32[64,1,512]{2,1,0:T(1,128)S(1)} %slice.8) | copy-start | bytes 393220
  333.7 77.5 %copy-start.1 = (f32[32,29,256]{2,1,0:T(8,128)S(1)}, f32[32,29,256]{2,1,0:T(8,128)}, u32[]{:S(2)}) copy-start(f32[32,29,256]{2,1,0:T(8,128)} %get-tuple-element.24) | copy-start | bytes 2850820
  411.2 7.4 %collective-permute-start = (f32[64,16384]{1,0:T(8,128)}, f32[64,16384]{1,0:T(8,128)S(1)}, u32[]{:S(2)}, u32[]{:S(2)}) collective-permute-start(f32[64,16384]{1,0:T(8,128)} %get-tuple-element.21), channel_id=1, source_target_pairs={{0,1},{1,0},{2,3},{3,2},{4,5},{5,4},{6,7},{7,6},{8,9},{9,8},{10,11... | collective-permute-start | bytes 12582920 | tf_op jit(solution)/shard_map/ppermute | solution.py:576

commit v3 on v2

v3 whole, which is shorter than its diff:
```python
import functools

import jax
import jax.numpy as jnp
from jax import lax
from jax.experimental import pallas as pl
from jax.experimental.pallas import tpu as pltpu
from jax.sharding import PartitionSpec as P

CHANNELS = 29
TILE_SIDE = 16
PIXELS = 256
VIEWS = 8
SCREEN_TILES = 8160
GEOM = 6
SENT = 35
WIRE = 40
PITCH = 36
TWO_PI = 6.283185307179586
LOG2E = 1.4426950408889634
VMEM = pltpu.VMEM
SMEM = pltpu.SMEM
F32 = jnp.float32
BF16 = jnp.bfloat16
I32 = jnp.int32
GROUP = 8
BLOCK = 128


def params(**more):
    return pltpu.CompilerParams(vmem_limit_bytes=60 * 2**20, **more)


def whole(space):
    return pl.BlockSpec(memory_space=space)


def iota(shape, dim):
    return lax.broadcasted_iota(I32, shape, dim)


def dot(a, b, contract=((1,), (0,))):
    return lax.dot_general(a, b, (contract, ((), ())), preferred_element_type=F32)


def split(x):
    high = x.astype(BF16).astype(F32)
    return high, x - high


def route_kernel(view_ref, shard_ref, row_ref, ask_ref, meta_ref, slot_ref):
    shards = ask_ref.shape[0]
    tiles, length = shard_ref.shape
    width = 256
    parts = length // width
    capacity = 2 * tiles * length // shards
    blocks = capacity // BLOCK
    before = (iota((width, width), 0) < iota((width, width), 1)).astype(F32).astype(BF16)
    lane = iota((1, width), 1).astype(F32)

    def some(i, state):
        carry, total = state
        spots = [(2 * i + u // parts, u % parts) for u in range(2 * parts)]
        shard = [shard_ref[pl.ds(t, 1), h * width : (h + 1) * width] for t, h in spots]
        hot = [(iota((shards, width), 0) == one).astype(F32) for one in shard]
        seen = dot(jnp.concatenate(hot, axis=0).astype(BF16), before)
        at, values = [], []
        for u, (t, h) in enumerate(spots):
            place = jnp.sum(hot[u] * (seen[shards * u : shards * (u + 1)] + carry), axis=0, keepdims=True)
            carry = carry + jnp.sum(hot[u], axis=1, keepdims=True)
            place = place.astype(I32)
            slot = shard[u] * capacity + place
            for b in range(width // BLOCK):
                slot_ref[pl.ds(t * (length // BLOCK) + h * (width // BLOCK) + b, 1), :] = slot[
                    :, b * BLOCK : (b + 1) * BLOCK
                ]
            at.append((iota((capacity, width), 0) == place).astype(F32).astype(BF16))
            row = row_ref[pl.ds(t, 1), h * width : (h + 1) * width]
            parts_of = (
                (row & 255).astype(F32),
                (row >> 8).astype(F32),
                jnp.full((1, width), view_ref[t] + 1, I32).astype(F32),
                lane,
                jnp.full((1, width), t * parts + h, I32).astype(F32),
            )
            values.append(jnp.concatenate([hot[u] * part for part in parts_of], axis=0).astype(BF16))
        at = jnp.concatenate(at, axis=1)
        values = jnp.concatenate(values, axis=1)
        return carry, total + dot(values, at, ((1,), (1,)))

    start = (jnp.zeros((shards, 1), F32), jnp.zeros((5 * shards, capacity), F32))
    _, total = lax.fori_loop(0, tiles // 2, some, start)
    low, high, view, lane, chunk = (total[shards * k : shards * (k + 1)].astype(I32) for k in range(5))
    used = view > 0
    row = jnp.where(used, low + 256 * high, iota((shards, capacity), 1))
    view = jnp.where(used, view - 1, 0)
    entry = lane + width * chunk
    used = used.astype(I32)
    for c in range(blocks):
        lanes = slice(c * BLOCK, (c + 1) * BLOCK)
        ask_ref[:, c, :] = row[:, lanes]
        ask_ref[:, blocks + c, :] = view[:, lanes]
        meta_ref[:, c, :] = entry[:, lanes]
        meta_ref[:, blocks + c, :] = used[:, lanes]


def route(view, shard, row, shards):
    tiles, length = shard.shape
    lists = jax.ShapeDtypeStruct((shards, 8, BLOCK), I32)
    return pl.pallas_call(
        route_kernel,
        out_shape=(lists, lists, jax.ShapeDtypeStruct((tiles * length // BLOCK, BLOCK), I32)),
        in_specs=[whole(SMEM), whole(VMEM), whole(VMEM)],
        out_specs=(whole(VMEM),) * 3,
        compiler_params=params(),
        name="route",
    )(view, shard, row)


def shifted(k, back=False):
    shards = lax.axis_size("gauss")
    side = round(shards ** (1 / 3))
    me = lax.axis_index("gauss")
    step = lax.rem(37 * k, shards)
    sign = 1 - 2 * lax.axis_index("view")
    if back:
        sign = -sign

    def part(x, by):
        return lax.rem(x // by, side)

    def moved(by):
        return lax.rem(part(me, by) + sign * part(step, by) + side, side) * by

    return moved(side * side) + moved(side) + moved(1)


def remote(src, dst, send_sem, recv_sem, to):
    return pltpu.make_async_remote_copy(
        src_ref=src,
        dst_ref=dst,
        send_sem=send_sem,
        recv_sem=recv_sem,
        device_id={"gauss": to},
        device_id_type=pl.DeviceIdType.MESH,
    )


def exchange(ask_ref, finish, table, even, odd, send, out_ref, send_sem, recv_sem, own_sem, ready):
    shards = send.shape[0]
    blocks = send.shape[1] // PITCH
    me = lax.axis_index("gauss")

    def copy(to, by):
        return remote(send.at[to], out_ref.at[by], send_sem.at[to], recv_sem.at[by], to)

    own = pltpu.make_async_copy(send.at[me], out_ref.at[me], own_sem)
    ready()

    def one(k, _):
        to, last = shifted(k), shifted(k + shards - 1)
        for c in range(blocks):
            now, past = (even, odd) if c % 2 == 0 else (odd, even)
            finish(past, *((to, c - 1) if c else (last, blocks - 1)))
            for u in range(BLOCK):
                now[u : u + 1, :] = table[pl.ds(ask_ref[to, c, u], 1), :]
            if c == 0:

                @pl.when(k == 1)
                def _():
                    own.start()

                @pl.when(k > 1)
                def _():
                    copy(last, me).start()

        return 0

    lax.fori_loop(0, shards, one, 0)
    last = shifted(shards - 1)
    finish(odd, last, blocks - 1)
    copy(last, me).start()
    own.wait()

    def end(k, _):
        copy(shifted(k), me).wait_send()
        copy(me, shifted(k, True)).wait_recv()
        return 0

    lax.fori_loop(1, shards, end, 0)


def greet():
    shards = lax.axis_size("gauss")
    me = lax.axis_index("gauss")
    barrier = pltpu.get_barrier_semaphore()

    def hail(k, _):
        pl.semaphore_signal(
            barrier, inc=1, device_id={"gauss": lax.rem(me + k, shards)}, device_id_type=pl.DeviceIdType.MESH
        )
        return 0

    lax.fori_loop(1, shards, hail, 0)

    def wait():
        pl.semaphore_wait(barrier, shards - 1)

    return wait


def exchange_scratch(shards, blocks):
    return [
        VMEM((BLOCK, 128), F32),
        VMEM((BLOCK, 128), F32),
        VMEM((shards, blocks * PITCH, BLOCK), F32),
        pltpu.SemaphoreType.DMA((shards,)),
        pltpu.SemaphoreType.DMA((shards,)),
        pltpu.SemaphoreType.DMA,
    ]


def fetch_kernel(
    cosines_ref, ask_ref, rows_ref, out_ref, asked_ref, cos_ref, clash_ref,
    table, asked, ask_send, ask_recv, ask_own, even, odd, send, send_sem, recv_sem, own_sem,
):
    width, columns = rows_ref.shape
    shards = send.shape[0]
    blocks = send.shape[1] // PITCH
    me = lax.axis_index("gauss")
    greet()()

    def copy(to, by):
        return remote(ask_ref.at[to], asked_ref.at[by], ask_send.at[to], ask_recv.at[by], to)

    def ask(k, _):
        copy(shifted(k), me).start()
        return 0

    lax.fori_loop(1, shards, ask, 0)

    def turn(i, _):
        at = pl.multiple_of(i * 512, 512)
        table[pl.ds(at, 512), 0:width] = rows_ref[:, pl.ds(at, 512)].T
        return 0

    lax.fori_loop(0, columns // 512, turn, 0)
    asked_ref[me] = ask_ref[me]

    def end(k, _):
        copy(shifted(k), me).wait_send()
        copy(me, shifted(k, True)).wait_recv()
        return 0

    lax.fori_loop(1, shards, end, 0)
    down = pltpu.make_async_copy(asked_ref, asked, ask_own)
    down.start()
    for c in range(blocks):
        row = asked_ref[:, c, :]
        view = asked_ref[:, blocks + c, :]
        cos = jnp.full(view.shape, cosines_ref[0], F32)
        for v in range(1, VIEWS):
            cos = jnp.where(view == v, cosines_ref[v], cos)
        cos_ref[:, c, :] = cos
        lane = iota(row.shape, 1) % GROUP
        same = jnp.zeros(row.shape, F32)
        for d in range(1, GROUP):
            same = jnp.where((pltpu.roll(row, d, 1) == row) & (lane >= d), 1.0, same)
        clash_ref[:, c : c + 1] = jnp.max(same, axis=1, keepdims=True).astype(I32)
    down.wait()

    def finish(rows, to, c):
        turned = rows[...].T
        second = jnp.concatenate(
            [jnp.zeros((GEOM, BLOCK), F32), turned[SENT : SENT + CHANNELS]],
            axis=0,
        )
        send[to, c * PITCH : c * PITCH + SENT, :] = turned[0:SENT] + cos_ref[to, c : c + 1, :] * second

    exchange(asked, finish, table, even, odd, send, out_ref, send_sem, recv_sem, own_sem, lambda: None)


def fetch(cosines, ask, gauss_rows):
    shards = ask.shape[0]
    blocks = ask.shape[1] // 2
    width, columns = gauss_rows.shape
    return pl.pallas_call(
        fetch_kernel,
        out_shape=(
            jax.ShapeDtypeStruct((shards, blocks * PITCH, BLOCK), F32),
            jax.ShapeDtypeStruct(ask.shape, I32),
            jax.ShapeDtypeStruct(ask.shape, F32),
            jax.ShapeDtypeStruct((shards, 128), I32),
        ),
        in_specs=[whole(SMEM), whole(VMEM), whole(VMEM)],
        out_specs=(whole(pl.ANY), whole(VMEM), whole(VMEM), whole(VMEM)),
        scratch_shapes=[
            VMEM((columns, 128), F32),
            SMEM(ask.shape, I32),
            pltpu.SemaphoreType.DMA((shards,)),
            pltpu.SemaphoreType.DMA((shards,)),
            pltpu.SemaphoreType.DMA,
        ]
        + exchange_scratch(shards, blocks),
        compiler_params=params(collective_id=0, has_side_effects=True),
        name="fetch",
    )(cosines, ask, gauss_rows)


def send_back_kernel(entry_ref, meta_ref, grads_ref, out_ref, even, odd, send, send_sem, recv_sem, own_sem):
    blocks = send.shape[1] // PITCH
    wait = greet()

    def finish(rows, to, c):
        used = meta_ref[to, blocks + c : blocks + c + 1, :] > 0
        send[to, c * PITCH : c * PITCH + SENT, :] = jnp.where(used, rows[...].T[0:SENT], 0.0)

    exchange(entry_ref, finish, grads_ref, even, odd, send, out_ref, send_sem, recv_sem, own_sem, wait)


def send_back(meta, grads):
    shards = meta.shape[0]
    blocks = meta.shape[1] // 2
    return pl.pallas_call(
        send_back_kernel,
        out_shape=jax.ShapeDtypeStruct((shards, blocks * PITCH, BLOCK), F32),
        in_specs=[whole(SMEM), whole(VMEM), whole(VMEM)],
        out_specs=whole(pl.ANY),
        scratch_shapes=exchange_scratch(shards, blocks),
        compiler_params=params(collective_id=1, has_side_effects=True),
        name="send_back",
    )(meta, meta, grads)


def composite_kernel(
    slot_ref, wire_ref, cot_ref, images_ref, out_ref,
    table, rows, alpha, ratio, logs, before, weight, weight_hi, weight_lo, pull, parts, after, earlier, later,
):
    t = pl.program_id(0)
    shards = wire_ref.shape[0]
    blocks = wire_ref.shape[1] // PITCH
    length = rows.shape[0]
    half = length // 2
    side = TILE_SIDE

    @pl.when(t == 0)
    def _():
        def unpack(s, _):
            for c in range(blocks):
                at = pl.multiple_of((s * blocks + c) * BLOCK, BLOCK)
                table[pl.ds(at, BLOCK), 0:SENT] = wire_ref[s, c * PITCH : c * PITCH + SENT, :].T
            return 0

        lax.fori_loop(0, shards, unpack, 0)
        above = iota((2 * half, half), 0) % half
        beside = iota((2 * half, half), 1)
        earlier[...] = (above < beside).astype(F32).astype(BF16)
        later[...] = (above > beside).astype(F32).astype(BF16)

    def put(ref, at, x):
        high, low = split(x)
        high, low = high.astype(BF16), low.astype(BF16)
        ref[pl.ds(at, side), 0:half] = high[:, 0:half]
        ref[pl.ds(at, side), half : 2 * half] = low[:, 0:half]
        ref[pl.ds(at, side), 2 * half : 3 * half] = high[:, half:]
        ref[pl.ds(at, side), 3 * half : 4 * half] = low[:, half:]

    def pick(i, _):
        at = pl.multiple_of(i * BLOCK, BLOCK)
        for u in range(BLOCK):
            rows[pl.ds(at + u, 1), :] = table[pl.ds(slot_ref[t * (length // BLOCK) + i, u], 1), :]
        return 0

    lax.fori_loop(0, length // BLOCK, pick, 0)
    turned = rows[...].T
    x0, y0, r2, r3, r4, r5 = (turned[k : k + 1] for k in range(GEOM))
    conic_a = jnp.exp(r2)
    conic_c = jnp.exp(r4)
    skew = jnp.tanh(r3)
    middle = jnp.sqrt(conic_a * conic_c)
    conic_b = 0.9 * skew * middle
    opaque = 1.0 / (1.0 + jnp.exp(-r5))
    spot = iota((side, length), 0).astype(F32) + 0.5
    dx = spot - x0
    dy = spot - y0
    scale = -0.5 * LOG2E
    part_x = (scale * conic_a) * dx * dx
    cross = (2.0 * scale * conic_b) * dx
    part_y = (scale * conic_c) * dy * dy + jnp.log2(0.99 * opaque)

    for py in range(side):
        at = py * side
        a = jnp.exp2(part_x + (cross * dy[py : py + 1] + part_y[py : py + 1]))
        log = jnp.log2(1.0 - a)
        alpha[pl.ds(at, side), :] = a
        ratio[pl.ds(at, side), :] = a * jnp.exp2(-log)
        put(logs, at, log)

    before[:, 0:half] = dot(logs[:, 0 : 2 * half], earlier[...])
    before[:, half:] = dot(logs[:, 2 * half :], earlier[...])

    for py in range(side):
        at = py * side
        b = before[pl.ds(at, side), :]
        last = (
            b[:, half - 1 : half]
            + logs[pl.ds(at, side), half - 1 : half].astype(F32)
            + logs[pl.ds(at, side), 2 * half - 1 : 2 * half].astype(F32)
        )
        b = jnp.concatenate([b[:, 0:half], b[:, half:] + last], axis=1)
        w = jnp.exp2(b) * alpha[pl.ds(at, side), :]
        high, low = split(w)
        weight[pl.ds(at, side), :] = w
        weight_hi[pl.ds(at, side), :] = high.astype(BF16)
        weight_lo[pl.ds(at, side), :] = low.astype(BF16)

    channel = iota((WIRE, length), 0)
    colour = jnp.where((channel >= GEOM) & (channel < GEOM + CHANNELS), turned[0:WIRE], 0.0)
    colour_hi, colour_lo = split(colour)
    cot = cot_ref[0]
    cot_hi, cot_lo = split(cot)
    fill = jnp.zeros((128 - 3 * WIRE, length), F32)
    fill_cot = jnp.zeros((128 - 3 * WIRE, PIXELS), F32)
    both = jnp.concatenate([colour_hi, colour_lo], axis=0).astype(BF16)
    image = dot(both, weight_hi[...], ((1,), (1,)))
    image_lo = dot(both, weight_lo[...], ((1,), (1,)))
    image = image[0:WIRE] + image[WIRE:] + image_lo[0:WIRE]
    images_ref[0] = image[GEOM : GEOM + CHANNELS]
    both = jnp.concatenate([cot_hi, cot_lo], axis=0).astype(BF16)
    grad = dot(both, weight_hi[...])
    grad_lo = dot(both, weight_lo[...])
    grad = grad[0:WIRE] + grad[WIRE:] + grad_lo[0:WIRE]
    three = jnp.concatenate([cot_hi, cot_lo, cot_hi, fill_cot], axis=0).T.astype(BF16)
    other = jnp.concatenate([colour_hi, colour_hi, colour_lo, fill], axis=0).astype(BF16)
    pull[...] = dot(three, other)

    for py in range(side):
        at = py * side
        q = pull[pl.ds(at, side), :] * weight[pl.ds(at, side), :]
        pull[pl.ds(at, side), :] = q
        put(parts, at, q)

    after[:, 0:half] = dot(parts[:, 0 : 2 * half], later[...])
    after[:, half:] = dot(parts[:, 2 * half :], later[...])

    m0 = jnp.zeros((side, length), F32)
    m1 = jnp.zeros((side, length), F32)
    m2 = jnp.zeros((side, length), F32)
    for py in range(side):
        at = py * side
        s = after[pl.ds(at, side), :]
        q = pull[pl.ds(at, side), :]
        first = s[:, half : half + 1] + q[:, half : half + 1]
        s = jnp.concatenate([s[:, 0:half] + first, s[:, half:]], axis=1)
        h = q - s * ratio[pl.ds(at, side), :]
        hy = h * dy[py : py + 1]
        m0 = m0 + h
        m1 = m1 + hy
        m2 = m2 + hy * dy[py : py + 1]

    def total(x):
        return jnp.sum(x, axis=0, keepdims=True)

    m0x = m0 * dx
    s0, sx, sy, sxx, sxy, syy = total(m0), total(m0x), total(m1), total(m0x * dx), total(m1 * dx), total(m2)
    shared = -0.5 * conic_b * sxy
    geometry = (
        conic_a * sx + conic_b * sy,
        conic_b * sx + conic_c * sy,
        shared - 0.5 * conic_a * sxx,
        -0.9 * (1.0 - skew * skew) * middle * sxy,
        shared - 0.5 * conic_c * syy,
        (1.0 - opaque) * s0,
    )
    for k, value in enumerate(geometry):
        grad = jnp.where(channel == k, value, grad)
    out_ref[:, 0:WIRE] = grad.T


def composite(slot, wire, cot):
    shards = wire.shape[0]
    slots = wire.shape[1] // PITCH * BLOCK
    tiles = cot.shape[0]
    length = slot.size // tiles
    full = (PIXELS, length)
    return pl.pallas_call(
        composite_kernel,
        grid=(tiles,),
        out_shape=(
            jax.ShapeDtypeStruct((tiles, CHANNELS, PIXELS), F32),
            jax.ShapeDtypeStruct((tiles * length, 128), F32),
        ),
        in_specs=[
            whole(SMEM),
            pl.BlockSpec(wire.shape, lambda i: (0, 0, 0), pipeline_mode=pl.Buffered(1)),
            pl.BlockSpec((1, WIRE, PIXELS), lambda i: (i, 0, 0)),
        ],
        out_specs=(
            pl.BlockSpec((1, CHANNELS, PIXELS), lambda i: (i, 0, 0)),
            pl.BlockSpec((length, 128), lambda i: (i, 0)),
        ),
        scratch_shapes=[
            VMEM((shards * slots, 128), F32),
            VMEM((length, 128), F32),
            VMEM(full, F32),
            VMEM(full, F32),
            VMEM((PIXELS, 2 * length), BF16),
            VMEM(full, F32),
            VMEM(full, F32),
            VMEM(full, BF16),
            VMEM(full, BF16),
            VMEM(full, F32),
            VMEM((PIXELS, 2 * length), BF16),
            VMEM(full, F32),
            VMEM((length, length // 2), BF16),
            VMEM((length, length // 2), BF16),
        ],
        compiler_params=params(),
        name="composite",
    )(slot, wire, cot)


def collect_kernel(half_ref, ask_ref, clash_ref, cos_ref, wire_ref, keep_ref, send_ref, table, table2, even, odd):
    source = pl.program_id(0)
    width, half = keep_ref.shape
    blocks = wire_ref.shape[1] // PITCH
    step = 512

    @pl.when(source == 0)
    def _():
        table[...] = jnp.zeros_like(table)
        table2[...] = jnp.zeros_like(table2)
        even[...] = jnp.zeros_like(even)
        odd[...] = jnp.zeros_like(odd)

    def turn(c, rows):
        back = wire_ref[0, c * PITCH : c * PITCH + SENT, :]
        scaled = cos_ref[0, c : c + 1, :] * back
        rows[:, 0:width] = jnp.concatenate([back, scaled[GEOM:SENT]], axis=0).T

    def add(at, c, rows):
        for g in range(BLOCK // GROUP):
            into = (table, table2)[g % 2]
            places = [ask_ref[at, c, g * GROUP + u] for u in range(GROUP)]
            sums = [into[pl.ds(r, 1), :] + rows[g * GROUP + u : g * GROUP + u + 1, :] for u, r in enumerate(places)]
            for r, value in zip(places, sums):
                into[pl.ds(r, 1), :] = value

    def add_slowly(at, c, rows):
        def one(u, _):
            table[pl.ds(ask_ref[at, c, u], 1), :] += rows[pl.ds(u, 1), :]
            return 0

        lax.fori_loop(0, BLOCK, one, 0)

    def finish(at, c, rows, more):
        clear = clash_ref[at, c] == 0

        @pl.when(clear)
        def _():
            more()
            add(at, c, rows)

        @pl.when(jnp.logical_not(clear))
        def _():
            more()
            add_slowly(at, c, rows)

    for c in range(blocks):
        now, past = (even, odd) if c % 2 == 0 else (odd, even)
        at = source if c else jnp.maximum(source - 1, 0)
        finish(at, (c - 1) % blocks, past, functools.partial(turn, c, now))

    @pl.when(source == pl.num_programs(0) - 1)
    def _():
        finish(source, blocks - 1, odd, lambda: None)
        for ref, base in ((keep_ref, half_ref[0]), (send_ref, half - half_ref[0])):

            def back(i, _):
                at = pl.multiple_of(i * step, step)
                there = pl.multiple_of(base + at, step)
                both = table[pl.ds(there, step), :] + table2[pl.ds(there, step), :]
                ref[:, pl.ds(at, step)] = both.T[0:width]
                return 0

            lax.fori_loop(0, half // step, back, 0)


def collect(half, asked, clash, cos, wire, width, columns):
    shards, sent, _ = wire.shape
    part = jax.ShapeDtypeStruct((width, columns // 2), F32)
    part_spec = pl.BlockSpec((width, columns // 2), lambda i: (0, 0), pipeline_mode=pl.Buffered(1))
    return pl.pallas_call(
        collect_kernel,
        grid=(shards,),
        out_shape=(part, part),
        in_specs=[
            whole(SMEM),
            whole(SMEM),
            whole(SMEM),
            pl.BlockSpec((1,) + cos.shape[1:], lambda i: (i, 0, 0)),
            pl.BlockSpec((1, sent, BLOCK), lambda i: (i, 0, 0)),
        ],
        out_specs=(part_spec, part_spec),
        scratch_shapes=[
            VMEM((columns, 128), F32),
            VMEM((columns, 128), F32),
            VMEM((BLOCK, 128), F32),
            VMEM((BLOCK, 128), F32),
        ],
        compiler_params=params(),
        name="collect",
    )(half, asked, clash, cos, wire)


def per_device(gauss_rows, vis_shard, vis_row, tile_index, cotangent):
    shards = lax.axis_size("gauss")
    width, columns = gauss_rows.shape
    ask, meta, slot = route(tile_index // SCREEN_TILES, vis_shard.reshape(vis_row.shape), vis_row, shards)
    cosines = jnp.cos(TWO_PI * jnp.arange(VIEWS, dtype=I32).astype(F32) / VIEWS)
    fetched, asked, cos, clash = fetch(cosines, ask, gauss_rows)
    cot = jnp.pad(cotangent, ((0, 0), (GEOM, WIRE - GEOM - CHANNELS), (0, 0)))
    images, grads = composite(slot, fetched, cot)
    returned = send_back(meta, grads)
    half = (lax.axis_index("view") * (columns // 2)).astype(I32).reshape(1)
    keep, send = collect(half, asked, clash, cos, returned, width, columns)
    other = lax.ppermute(send, "view", [(0, 1), (1, 0)])
    return (images, keep + other)


def solution(mesh):
    placed = (
        P(None, "gauss"),
        P(("gauss", "view"), None, None),
        P(("gauss", "view"), None),
        P(("gauss", "view")),
        P(("gauss", "view"), None, None),
    )
    return jax.shard_map(
        per_device,
        mesh=mesh,
        in_specs=placed,
        out_specs=(P(("gauss", "view"), None, None), P(None, ("gauss", "view"))),
        check_vma=False,
    )
```

time: 426 us -> 337 us (0.79)
  the two profiles are of different devices: /device:TPU:7 before, /device:TPU:1 now
where the time goes in v3:
time: 337 us; the launch traced here: 334 us
  Pallas kernels  314 us (93%)
  other arithmetic  6.55 us (2%)
  local copies, waits for them, and re-layouts  5.89 us (2%)
  waiting for transfers between devices  5.51 us (2%)
    pallas_call x1, Pallas kernels, fetch(): pl.pallas_call(fetch_kernel, out_shape=(jax.ShapeDtypeStruct((shards, blo...  93.1 us
    pallas_call x1, Pallas kernels, send_back(): pl.pallas_call(send_back_kernel, out_shape=jax.ShapeDtypeStruct((shards,...  69.5 us
    pallas_call x1, Pallas kernels, composite(): pl.pallas_call(composite_kernel, grid=(tiles,), out_shape=(jax.ShapeDtype...  68.2 us
    pallas_call x1, Pallas kernels, collect(): pl.pallas_call(collect_kernel, grid=(shards,), out_shape=(part, part), in...  67.6 us
    pallas_call x1, Pallas kernels, route(): pl.pallas_call(route_kernel, out_shape=(lists, lists, jax.ShapeDtypeStruc...  15.1 us
  transfers between devices with their start and end apart: 1, of which 1 were waited for; matrix products, arithmetic and copies ran while one was open for 0% of the time, Pallas kernels for 0%

profile of v3, /device:TPU:1, one launch (start us, length us, event | category | flops | bytes accessed | tf_op | source)
XLA Modules:
  0.0 334.1 jit_solution(3445493088021168799)
XLA Ops:
  0.6 0.6 multiply_cosine_fusion.cosines_ref
  1.2 1.5 copy.11
  2.7 1.2 and_select_fusion.view_ref
  3.9 1.7 copy.7
  5.7 1.2 pad.4.cot_ref
  6.8 15.1 %route.1 = (s32[64,8,128]{2,1,0:T(8,128)}, s32[64,8,128]{2,1,0:T(8,128)}, s32[128,128]{1,0:T(8,128)}) custom-call(s32[32]{0:T(128)} %and_select_fusion.view_ref, s32[32,512]{1,0:T(8,128)} %bitcast.4, s32[32,512]{1,0:T(8,128)} %row_ref.1), custom_call_target="tpu_custom_call" | custom-call | tf_op jit(solution)/shard_map/route/pallas_call | solution.py:110
  22.0 93.1 %fetch.1 = (f32[64,144,128]{2,1,0:T(8,128)}, s32[64,8,128]{2,1,0:T(8,128)}, f32[64,8,128]{2,1,0:T(8,128)}, s32[64,128]{1,0:T(8,128)}) custom-call(f32[8]{0:T(128)} %multiply_cosine_fusion.cosines_ref, s32[64,8,128]{2,1,0:T(8,128)} %get-tuple-element.14.ask_ref, f32[64,32768]{1,0:T(8,128)} %rows_ref.1), custom_call_target="tpu_custom_call" | custom-call | tf_op jit(solution)/shard_map/fetch/pallas_call | solution.py:287
  115.1 68.2 %composite.1 = (f32[32,29,256]{2,1,0:T(8,128)}, f32[16384,128]{1,0:T(8,128)}) custom-call(s32[128,128]{1,0:T(8,128)} %get-tuple-element.13.slot_ref, f32[64,144,128]{2,1,0:T(8,128)} %get-tuple-element.15.wire_ref, f32[32,40,256]{2,1,0:T(8,128)} %pad.4.cot_ref), custom_call_target="tpu_custom_call" | custom-call | tf_op jit(solution)/shard_map/composite/pallas_call | solution.py:486
  183.3 69.5 %send_back.1.wire_ref = f32[64,144,128]{2,1,0:T(8,128)} custom-call(s32[64,8,128]{2,1,0:T(8,128)} %get-tuple-element.20.entry_ref.meta_ref, s32[64,8,128]{2,1,0:T(8,128)} %get-tuple-element.20.entry_ref.meta_ref, f32[16384,128]{1,0:T(8,128)} %get-tuple-element.21.grads_ref), custom_call_target="tpu_custom_call" | custom-call | tf_op jit(solution)/shard_map/send_back/pallas_call | solution.py:324
  252.8 0.0 copy-start
  252.8 67.6 %collect.1 = (f32[64,16384]{1,0:T(8,128)}, f32[64,16384]{1,0:T(8,128)}) custom-call(s32[1]{0:T(128)} %bitcast.half_ref, s32[64,8,128]{2,1,0:T(8,128)} %get-tuple-element.17.ask_ref, s32[64,128]{1,0:T(8,128)} %get-tuple-element.18.clash_ref, f32[64,8,128]{2,1,0:T(8,128)} %get-tuple-element.19.cos_ref, f32[64,144,128]{2,1,0:T(8,128)} %send_back.1.wire_ref), custom_call_target="tpu_custom_call" | custom-call | tf_op jit(solution)/shard_map/collect/pallas_call | solution.py:593
  320.4 2.0 collective-permute-start
  322.4 0.0 copy-done
  322.4 1.5 copy.8
  323.9 5.5 %collective-permute-done = f32[64,16384]{1,0:T(8,128)S(1)} collective-permute-done((f32[64,16384]{1,0:T(8,128)}, f32[64,16384]{1,0:T(8,128)S(1)}, u32[]{:S(2)}, u32[]{:S(2)}) %collective-permute-start) | collective-permute-done | bytes 4194336 | tf_op jit(solution)/shard_map/ppermute | solution.py:627
  329.4 4.7 %add.6 = f32[64,16384]{1,0:T(8,128)} add(f32[64,16384]{1,0:T(8,128)} %get-tuple-element.22, f32[64,16384]{1,0:T(8,128)S(1)} %collective-permute-done) | non-fusion elementwise | flops 1048576 | bytes 12582912 | tf_op jit(solution)/shard_map/add | solution.py:628
Async XLA Ops:
  252.8 69.6 %copy-start = (f32[32,29,256]{2,1,0:T(8,128)S(1)}, f32[32,29,256]{2,1,0:T(8,128)}, u32[]{:S(2)}) copy-start(f32[32,29,256]{2,1,0:T(8,128)} %get-tuple-element.24) | copy-start | bytes 2850820
  320.4 9.0 %collective-permute-start = (f32[64,16384]{1,0:T(8,128)}, f32[64,16384]{1,0:T(8,128)S(1)}, u32[]{:S(2)}, u32[]{:S(2)}) collective-permute-start(f32[64,16384]{1,0:T(8,128)} %get-tuple-element.23), channel_id=1, source_target_pairs={{0,1},{1,0},{2,3},{3,2},{4,5},{5,4},{6,7},{7,6},{8,9},{9,8},{10,11... | collective-permute-start | bytes 12582920 | tf_op jit(solution)/shard_map/ppermute | solution.py:627

commit v4 on v3

v4 whole, which is shorter than its diff:
```python
import functools
import math

import jax
import jax.numpy as jnp
from jax import lax
from jax.experimental import pallas as pl
from jax.experimental.pallas import tpu as pltpu
from jax.sharding import PartitionSpec as P

CHANNELS = 29
TILE_SIDE = 16
PIXELS = 256
VIEWS = 8
SCREEN_TILES = 8160
GEOM = 6
SENT = 35
WIRE = 40
PITCH = 36
TWO_PI = 6.283185307179586
LOG2E = 1.4426950408889634
VMEM = pltpu.VMEM
SMEM = pltpu.SMEM
F32 = jnp.float32
BF16 = jnp.bfloat16
I32 = jnp.int32
GROUP = 8
BLOCK = 128
SOURCES = 8
PICKS = 8


def params(**more):
    return pltpu.CompilerParams(vmem_limit_bytes=60 * 2**20, **more)


def whole(space):
    return pl.BlockSpec(memory_space=space)


def iota(shape, dim):
    return lax.broadcasted_iota(I32, shape, dim)


def dot(a, b, contract=((1,), (0,))):
    return lax.dot_general(a, b, (contract, ((), ())), preferred_element_type=F32)


def view_cosines():
    return [math.cos(TWO_PI * v / VIEWS) for v in range(VIEWS)]


def split(x):
    high = x.astype(BF16).astype(F32)
    return high, x - high


def route_kernel(tile_ref, shard_ref, row_ref, ask_ref, meta_ref, slot_ref):
    shards = ask_ref.shape[0]
    tiles, length = row_ref.shape
    tile_blocks = length // BLOCK
    width = 256
    parts = length // width
    capacity = 2 * tiles * length // shards
    blocks = capacity // BLOCK
    before = (iota((width, width), 0) < iota((width, width), 1)).astype(F32).astype(BF16)
    lane = iota((1, width), 1).astype(F32)

    def some(i, state):
        carry, total = state
        spots = [(2 * i + u // parts, u % parts) for u in range(2 * parts)]
        shard = [
            jnp.concatenate(
                [shard_ref[pl.ds(t * tile_blocks + h * (width // BLOCK) + b, 1), :] for b in range(width // BLOCK)],
                axis=1,
            )
            for t, h in spots
        ]
        hot = [(iota((shards, width), 0) == one).astype(F32) for one in shard]
        seen = dot(jnp.concatenate(hot, axis=0).astype(BF16), before)
        at, values = [], []
        for u, (t, h) in enumerate(spots):
            place = jnp.sum(hot[u] * (seen[shards * u : shards * (u + 1)] + carry), axis=0, keepdims=True)
            carry = carry + jnp.sum(hot[u], axis=1, keepdims=True)
            place = place.astype(I32)
            slot = shard[u] * capacity + place
            for b in range(width // BLOCK):
                slot_ref[pl.ds(t * tile_blocks + h * (width // BLOCK) + b, 1), :] = slot[
                    :, b * BLOCK : (b + 1) * BLOCK
                ]
            at.append((iota((capacity, width), 0) == place).astype(F32).astype(BF16))
            row = row_ref[pl.ds(t, 1), h * width : (h + 1) * width]
            parts_of = (
                (row & 255).astype(F32),
                (row >> 8).astype(F32),
                sum(
                    (jnp.full((1, width), tile_ref[t], I32) >= SCREEN_TILES * v).astype(F32) for v in range(VIEWS)
                ),
                lane,
                jnp.full((1, width), t * parts + h, I32).astype(F32),
            )
            values.append(jnp.concatenate([hot[u] * part for part in parts_of], axis=0).astype(BF16))
        at = jnp.concatenate(at, axis=1)
        values = jnp.concatenate(values, axis=1)
        return carry, total + dot(values, at, ((1,), (1,)))

    start = (jnp.zeros((shards, 1), F32), jnp.zeros((5 * shards, capacity), F32))
    _, total = lax.fori_loop(0, tiles // 2, some, start)
    low, high, view, lane, chunk = (total[shards * k : shards * (k + 1)].astype(I32) for k in range(5))
    used = view > 0
    row = jnp.where(used, low + 256 * high, iota((shards, capacity), 1))
    view = jnp.where(used, view - 1, 0)
    entry = lane + width * chunk
    used = used.astype(I32)
    for c in range(blocks):
        lanes = slice(c * BLOCK, (c + 1) * BLOCK)
        ask_ref[:, c, :] = row[:, lanes]
        ask_ref[:, blocks + c, :] = view[:, lanes]
        meta_ref[:, c, :] = entry[:, lanes]
        meta_ref[:, blocks + c, :] = used[:, lanes]


def route(tile, shard, row, shards):
    tiles, length = row.shape
    lists = jax.ShapeDtypeStruct((shards, 8, BLOCK), I32)
    return pl.pallas_call(
        route_kernel,
        out_shape=(lists, lists, jax.ShapeDtypeStruct((tiles * length // BLOCK, BLOCK), I32)),
        in_specs=[whole(SMEM), whole(VMEM), whole(VMEM)],
        out_specs=(whole(VMEM),) * 3,
        compiler_params=params(),
        name="route",
    )(tile, shard, row)


def shifted(k, back=False):
    shards = lax.axis_size("gauss")
    side = round(shards ** (1 / 3))
    me = lax.axis_index("gauss")
    step = lax.rem(37 * k, shards)
    sign = 1 - 2 * lax.axis_index("view")
    if back:
        sign = -sign

    def part(x, by):
        return lax.rem(x // by, side)

    def moved(by):
        return lax.rem(part(me, by) + sign * part(step, by) + side, side) * by

    return moved(side * side) + moved(side) + moved(1)


def remote(src, dst, send_sem, recv_sem, to):
    return pltpu.make_async_remote_copy(
        src_ref=src,
        dst_ref=dst,
        send_sem=send_sem,
        recv_sem=recv_sem,
        device_id={"gauss": to},
        device_id_type=pl.DeviceIdType.MESH,
    )


def exchange(ask_ref, finish, table, even, odd, send, to_ref, send_sem, recv_sem, arrived, own):
    shards = send.shape[0]
    blocks = send.shape[1] // PITCH
    me = lax.axis_index("gauss")

    def copy(to, by):
        return remote(send.at[to], to_ref.at[by], send_sem.at[to], recv_sem.at[by], to)

    def one(k, _):
        to, last = shifted(k), shifted(k + shards - 1)
        for c in range(blocks):
            now, past = (even, odd) if c % 2 == 0 else (odd, even)
            finish(past, *((to, c - 1) if c else (last, blocks - 1)))
            for u in range(BLOCK):
                now[u : u + 1, :] = table[pl.ds(ask_ref[to, c, u], 1), :]
            if c == 0:

                @pl.when(k == 1)
                def _():
                    own()

                @pl.when(k > 1)
                def _():
                    copy(last, me).start()

        return 0

    lax.fori_loop(0, shards, one, 0)
    last = shifted(shards - 1)
    finish(odd, last, blocks - 1)
    copy(last, me).start()

    def end(k, _):
        by = shifted(k, True)
        copy(me, by).wait_recv()
        arrived(by)
        copy(shifted(k), me).wait_send()
        return 0

    lax.fori_loop(1, shards, end, 0)


def greet():
    shards = lax.axis_size("gauss")
    me = lax.axis_index("gauss")
    barrier = pltpu.get_barrier_semaphore()

    def hail(k, _):
        pl.semaphore_signal(
            barrier, inc=1, device_id={"gauss": lax.rem(me + k, shards)}, device_id_type=pl.DeviceIdType.MESH
        )
        return 0

    lax.fori_loop(1, shards, hail, 0)

    def wait():
        pl.semaphore_wait(barrier, shards - 1)

    return wait


class Tile:
    def __init__(self, t, cot_ref, images_ref, grads, rows, earlier, later, scratch):
        self.t, self.cot_ref, self.images_ref, self.grads, self.rows = t, cot_ref, images_ref, grads, rows
        self.earlier, self.later = earlier, later
        self.turned, self.alpha, self.ratio, self.parts, self.sums, self.weight, self.high, self.low, self.pull = scratch
        self.length = rows.shape[0]
        self.half = self.length // 2

    def put(self, at, x):
        half = self.half
        high, low = split(x)
        high, low = high.astype(BF16), low.astype(BF16)
        self.parts[pl.ds(at, TILE_SIDE), 0:half] = high[:, 0:half]
        self.parts[pl.ds(at, TILE_SIDE), half : 2 * half] = low[:, 0:half]
        self.parts[pl.ds(at, TILE_SIDE), 2 * half : 3 * half] = high[:, half:]
        self.parts[pl.ds(at, TILE_SIDE), 3 * half : 4 * half] = low[:, half:]

    def turn(self):
        self.turned[...] = self.rows[...].T[0:WIRE]

    def shape(self):
        turned = self.turned
        self.x0, self.y0, r2, r3, r4, r5 = (turned[k : k + 1, :] for k in range(GEOM))
        self.conic_a = jnp.exp(r2)
        self.conic_c = jnp.exp(r4)
        self.skew = jnp.tanh(r3)
        self.middle = jnp.sqrt(self.conic_a * self.conic_c)
        self.conic_b = 0.9 * self.skew * self.middle
        self.opaque = 1.0 / (1.0 + jnp.exp(-r5))
        spot = iota((TILE_SIDE, self.length), 0).astype(F32) + 0.5
        self.dx = spot - self.x0
        self.dy = spot - self.y0
        scale = -0.5 * LOG2E
        self.part_x = (scale * self.conic_a) * self.dx * self.dx
        self.cross = (2.0 * scale * self.conic_b) * self.dx
        self.part_y = (scale * self.conic_c) * self.dy * self.dy + jnp.log2(0.99 * self.opaque)

    def alphas(self, py):
        at = py * TILE_SIDE
        a = jnp.exp2(self.part_x + (self.cross * self.dy[py : py + 1] + self.part_y[py : py + 1]))
        log = jnp.log2(1.0 - a)
        self.alpha[pl.ds(at, TILE_SIDE), :] = a
        self.ratio[pl.ds(at, TILE_SIDE), :] = a * jnp.exp2(-log)
        self.put(at, log)

    def prefix(self):
        half = self.half
        self.sums[:, 0:half] = dot(self.parts[:, 0 : 2 * half], self.earlier[...])
        self.sums[:, half:] = dot(self.parts[:, 2 * half :], self.earlier[...])

    def weights(self, py):
        at, half = py * TILE_SIDE, self.half
        b = self.sums[pl.ds(at, TILE_SIDE), :]
        last = (
            b[:, half - 1 : half]
            + self.parts[pl.ds(at, TILE_SIDE), half - 1 : half].astype(F32)
            + self.parts[pl.ds(at, TILE_SIDE), 2 * half - 1 : 2 * half].astype(F32)
        )
        b = jnp.concatenate([b[:, 0:half], b[:, half:] + last], axis=1)
        w = jnp.exp2(b) * self.alpha[pl.ds(at, TILE_SIDE), :]
        high, low = split(w)
        self.weight[pl.ds(at, TILE_SIDE), :] = w
        self.high[pl.ds(at, TILE_SIDE), :] = high.astype(BF16)
        self.low[pl.ds(at, TILE_SIDE), :] = low.astype(BF16)

    def products(self):
        channel = iota((WIRE, self.length), 0)
        colour = jnp.where((channel >= GEOM) & (channel < SENT), self.turned[...], 0.0)
        colour_hi, colour_lo = split(colour)
        cot = jnp.concatenate(
            [jnp.zeros((GEOM, PIXELS), F32), self.cot_ref[self.t], jnp.zeros((WIRE - SENT, PIXELS), F32)], axis=0
        )
        cot_hi, cot_lo = split(cot)
        fill = jnp.zeros((128 - 3 * WIRE, self.length), F32)
        fill_cot = jnp.zeros((128 - 3 * WIRE, PIXELS), F32)
        three = jnp.concatenate([cot_hi, cot_lo, cot_hi, fill_cot], axis=0).T.astype(BF16)
        other = jnp.concatenate([colour_hi, colour_hi, colour_lo, fill], axis=0).astype(BF16)
        self.pull[...] = dot(three, other)
        both = jnp.concatenate([colour_hi, colour_lo], axis=0).astype(BF16)
        image = dot(both, self.high[...], ((1,), (1,)))
        image_lo = dot(both[0:48], self.low[...], ((1,), (1,)))
        image = image[0:WIRE] + image[WIRE:] + image_lo[0:WIRE]
        self.images_ref[self.t] = image[GEOM:SENT]
        both = jnp.concatenate([cot_hi, cot_lo], axis=0).astype(BF16)
        grad = dot(both, self.high[...])
        grad_lo = dot(both[0:48], self.low[...])
        self.turned[...] = grad[0:WIRE] + grad[WIRE:] + grad_lo[0:WIRE]

    def terms(self, py):
        at = py * TILE_SIDE
        q = self.pull[pl.ds(at, TILE_SIDE), :] * self.weight[pl.ds(at, TILE_SIDE), :]
        self.pull[pl.ds(at, TILE_SIDE), :] = q
        self.put(at, q)

    def suffix(self):
        half = self.half
        self.sums[:, 0:half] = dot(self.parts[:, 0 : 2 * half], self.later[...])
        self.sums[:, half:] = dot(self.parts[:, 2 * half :], self.later[...])

    def moments(self, py):
        at, half = py * TILE_SIDE, self.half
        s = self.sums[pl.ds(at, TILE_SIDE), :]
        q = self.pull[pl.ds(at, TILE_SIDE), :]
        first = s[:, half : half + 1] + q[:, half : half + 1]
        s = jnp.concatenate([s[:, 0:half] + first, s[:, half:]], axis=1)
        h = q - s * self.ratio[pl.ds(at, TILE_SIDE), :]
        hy = h * self.dy[py : py + 1]
        hyy = hy * self.dy[py : py + 1]
        if py == 0:
            self.m0, self.m1, self.m2 = h, hy, hyy
        else:
            self.m0, self.m1, self.m2 = self.m0 + h, self.m1 + hy, self.m2 + hyy

    def close(self):
        def total(x):
            return jnp.sum(x, axis=0, keepdims=True)

        m0x = self.m0 * self.dx
        s0, sx, sy = total(self.m0), total(m0x), total(self.m1)
        sxx, sxy, syy = total(m0x * self.dx), total(self.m1 * self.dx), total(self.m2)
        shared = -0.5 * self.conic_b * sxy
        geometry = (
            self.conic_a * sx + self.conic_b * sy,
            self.conic_b * sx + self.conic_c * sy,
            shared - 0.5 * self.conic_a * sxx,
            -0.9 * (1.0 - self.skew * self.skew) * self.middle * sxy,
            shared - 0.5 * self.conic_c * syy,
            (1.0 - self.opaque) * s0,
        )
        grad = self.turned[...]
        channel = iota(grad.shape, 0)
        for k, value in enumerate(geometry):
            grad = jnp.where(channel == k, value, grad)
        at = pl.multiple_of(self.t * self.length, self.length)
        self.grads[pl.ds(at, self.length), 0:WIRE] = grad.T


def paint(slot_ref, cot_ref, images_ref, table, grads, rows, earlier, later, scratch):
    tiles = cot_ref.shape[0]
    length = rows[0].shape[0]
    blocks = length // BLOCK
    half = length // 2
    above = iota((2 * half, half), 0) % half
    beside = iota((2 * half, half), 1)
    earlier[...] = (above < beside).astype(F32).astype(BF16)
    later[...] = (above > beside).astype(F32).astype(BF16)

    def pick(into, t, start, count):
        for u in range(start, start + count):
            into[u : u + 1, :] = table[pl.ds(slot_ref[t * blocks + u // BLOCK, u % BLOCK], 1), :]

    pick(rows[0], 0, 0, length)
    pick(rows[1], 1, 0, length)

    def two(i, _):
        a, b = (
            Tile(2 * i + k, cot_ref, images_ref, grads, rows[k], earlier, later, scratch[k]) for k in range(2)
        )
        following = [jnp.minimum(2 * i + 2 + k, tiles - 1) for k in range(2)]
        todo = [(k, start) for start in range(0, length, PICKS) for k in range(2)]

        def more():
            if todo:
                k, start = todo.pop(0)
                pick(rows[k], following[k], start, PICKS)

        def sweep(step):
            for py in range(TILE_SIDE):
                step(py)
                more()

        a.turn()
        b.turn()
        a.shape()
        sweep(a.alphas)
        a.prefix()
        b.shape()
        sweep(b.alphas)
        b.prefix()
        sweep(a.weights)
        a.products()
        sweep(b.weights)
        b.products()
        sweep(a.terms)
        a.suffix()
        sweep(b.terms)
        b.suffix()
        sweep(a.moments)
        a.close()
        sweep(b.moments)
        b.close()
        while todo:
            more()
        return 0

    lax.fori_loop(0, tiles // 2, two, 0)


def paint_scratch(length):
    full = (PIXELS, length)
    one = [
        VMEM((WIRE, length), F32),
        VMEM(full, F32),
        VMEM(full, F32),
        VMEM((PIXELS, 2 * length), BF16),
        VMEM(full, F32),
        VMEM(full, F32),
        VMEM(full, BF16),
        VMEM(full, BF16),
        VMEM(full, F32),
    ]
    return [VMEM((length, 128), F32)] * 2 + [VMEM((length, length // 2), BF16)] * 2 + one + one


def render_kernel(
    slot_ref, entry_ref, ask_ref, meta_ref, rows_ref, cot_ref,
    images_ref, back_ref, asked_ref, cos_ref, clash_ref,
    held, table, asked, ask_send, ask_recv, own_sem, even, odd, send, got,
    send_sem, recv_sem, back_send, back_recv, grads, *scratch,
):
    width, columns = held.shape
    shards = send.shape[0]
    blocks = send.shape[1] // PITCH
    me = lax.axis_index("gauss")
    load = pltpu.make_async_copy(rows_ref, held, own_sem)
    load.start()
    greet()()

    def copy(to, by):
        return remote(ask_ref.at[to], asked_ref.at[by], ask_send.at[to], ask_recv.at[by], to)

    def ask(k, _):
        copy(shifted(k), me).start()
        return 0

    lax.fori_loop(1, shards, ask, 0)
    load.wait()

    def turn(i, _):
        at = pl.multiple_of(i * 512, 512)
        table[pl.ds(at, 512), 0:width] = held[:, pl.ds(at, 512)].T
        return 0

    lax.fori_loop(0, columns // 512, turn, 0)
    asked_ref[me] = ask_ref[me]

    def end(k, _):
        copy(shifted(k), me).wait_send()
        copy(me, shifted(k, True)).wait_recv()
        return 0

    lax.fori_loop(1, shards, end, 0)
    down = pltpu.make_async_copy(asked_ref, asked, own_sem)
    down.start()
    for c in range(blocks):
        row = asked_ref[:, c, :]
        view = asked_ref[:, blocks + c, :]
        cos = jnp.zeros(view.shape, F32)
        for v, value in enumerate(view_cosines()):
            cos = jnp.where(view == v, value, cos)
        cos_ref[:, c, :] = cos
        lane = iota(row.shape, 1) % GROUP
        same = jnp.zeros(row.shape, F32)
        for d in range(1, GROUP):
            same = jnp.where((pltpu.roll(row, d, 1) == row) & (lane >= d), 1.0, same)
        clash_ref[:, c : c + 1] = jnp.max(same, axis=1, keepdims=True).astype(I32)
    down.wait()

    def blend(rows, to, c):
        turned = rows[...].T
        second = jnp.concatenate([jnp.zeros((GEOM, BLOCK), F32), turned[SENT : SENT + CHANNELS]], axis=0)
        send[to, c * PITCH : c * PITCH + SENT, :] = turned[0:SENT] + cos_ref[to, c : c + 1, :] * second

    def unpack(source, by):
        for c in range(blocks):
            at = pl.multiple_of((by * blocks + c) * BLOCK, BLOCK)
            table[pl.ds(at, BLOCK), 0:SENT] = source[by, c * PITCH : c * PITCH + SENT, :].T

    def arrived(by):
        unpack(got, by)

    exchange(asked, blend, table, even, odd, send, got, send_sem, recv_sem, arrived, lambda: None)
    unpack(send, me)

    paint(
        slot_ref, cot_ref, images_ref, table, grads, scratch[0:2], scratch[2], scratch[3], (scratch[4:13], scratch[13:22])
    )

    def mask(rows, to, c):
        used = meta_ref[to, blocks + c : blocks + c + 1, :] > 0
        send[to, c * PITCH : c * PITCH + SENT, :] = jnp.where(used, rows[...].T[0:SENT], 0.0)

    own = pltpu.make_async_copy(send.at[me], back_ref.at[me], own_sem)
    exchange(entry_ref, mask, grads, even, odd, send, back_ref, back_send, back_recv, lambda by: None, own.start)
    own.wait()


def render(slot, meta, ask, gauss_rows, cot):
    shards = ask.shape[0]
    blocks = ask.shape[1] // 2
    width, columns = gauss_rows.shape
    tiles = cot.shape[0]
    length = slot.size // tiles
    wire = (shards, blocks * PITCH, BLOCK)
    sems = pltpu.SemaphoreType.DMA((shards,))
    return pl.pallas_call(
        render_kernel,
        out_shape=(
            jax.ShapeDtypeStruct((tiles, CHANNELS, PIXELS), F32),
            jax.ShapeDtypeStruct(wire, F32),
            jax.ShapeDtypeStruct(ask.shape, I32),
            jax.ShapeDtypeStruct(ask.shape, F32),
            jax.ShapeDtypeStruct((shards, 128), I32),
        ),
        in_specs=[whole(SMEM), whole(SMEM), whole(VMEM), whole(VMEM), whole(pl.ANY), whole(VMEM)],
        out_specs=(whole(VMEM), whole(pl.ANY), whole(VMEM), whole(VMEM), whole(VMEM)),
        scratch_shapes=[
            VMEM((width, columns), F32),
            VMEM((columns, 128), F32),
            SMEM(ask.shape, I32),
            sems,
            sems,
            pltpu.SemaphoreType.DMA,
            VMEM((BLOCK, 128), F32),
            VMEM((BLOCK, 128), F32),
            VMEM(wire, F32),
            VMEM(wire, F32),
            sems,
            sems,
            sems,
            sems,
            VMEM((tiles * length, 128), F32),
        ]
        + paint_scratch(length),
        compiler_params=params(collective_id=0, has_side_effects=True),
        name="render",
    )(slot, meta, ask, meta, gauss_rows, cot)


def collect_kernel(half_ref, ask_ref, clash_ref, cos_ref, wire_ref, keep_ref, send_ref, table, table2, even, odd):
    step_id = pl.program_id(0)
    sources = wire_ref.shape[0]
    width, half = keep_ref.shape
    blocks = wire_ref.shape[1] // PITCH
    step = 512

    @pl.when(step_id == 0)
    def _():
        table[...] = jnp.zeros_like(table)
        table2[...] = jnp.zeros_like(table2)
        even[...] = jnp.zeros_like(even)
        odd[...] = jnp.zeros_like(odd)

    def turn(s, c, rows):
        back = wire_ref[s, c * PITCH : c * PITCH + SENT, :]
        scaled = cos_ref[s, c : c + 1, :] * back
        rows[:, 0:width] = jnp.concatenate([back, scaled[GEOM:SENT]], axis=0).T

    def add(at, c, rows):
        for g in range(BLOCK // GROUP):
            into = (table, table2)[g % 2]
            places = [ask_ref[at, c, g * GROUP + u] for u in range(GROUP)]
            sums = [into[pl.ds(r, 1), :] + rows[g * GROUP + u : g * GROUP + u + 1, :] for u, r in enumerate(places)]
            for r, value in zip(places, sums):
                into[pl.ds(r, 1), :] = value

    def add_slowly(at, c, rows):
        def one(u, _):
            table[pl.ds(ask_ref[at, c, u], 1), :] += rows[pl.ds(u, 1), :]
            return 0

        lax.fori_loop(0, BLOCK, one, 0)

    def finish(at, c, rows, more):
        clear = clash_ref[at, c] == 0

        @pl.when(clear)
        def _():
            more()
            add(at, c, rows)

        @pl.when(jnp.logical_not(clear))
        def _():
            more()
            add_slowly(at, c, rows)

    def one(s, _):
        source = step_id * sources + s
        for c in range(blocks):
            now, past = (even, odd) if c % 2 == 0 else (odd, even)
            at = source if c else jnp.maximum(source - 1, 0)
            finish(at, (c - 1) % blocks, past, functools.partial(turn, s, c, now))
        return 0

    lax.fori_loop(0, sources, one, 0)

    @pl.when(step_id == pl.num_programs(0) - 1)
    def _():
        finish(pl.num_programs(0) * sources - 1, blocks - 1, odd, lambda: None)
        for ref, base in ((keep_ref, half_ref[0]), (send_ref, half - half_ref[0])):

            def back(i, _):
                at = pl.multiple_of(i * step, step)
                there = pl.multiple_of(base + at, step)
                both = table[pl.ds(there, step), :] + table2[pl.ds(there, step), :]
                ref[:, pl.ds(at, step)] = both.T[0:width]
                return 0

            lax.fori_loop(0, half // step, back, 0)


def collect(half, asked, clash, cos, wire, width, columns):
    shards, sent, _ = wire.shape
    part = jax.ShapeDtypeStruct((width, columns // 2), F32)
    part_spec = pl.BlockSpec((width, columns // 2), lambda i: (0, 0), pipeline_mode=pl.Buffered(1))
    return pl.pallas_call(
        collect_kernel,
        grid=(shards // SOURCES,),
        out_shape=(part, part),
        in_specs=[
            whole(SMEM),
            whole(SMEM),
            whole(SMEM),
            pl.BlockSpec((SOURCES,) + cos.shape[1:], lambda i: (i, 0, 0)),
            pl.BlockSpec((SOURCES, sent, BLOCK), lambda i: (i, 0, 0)),
        ],
        out_specs=(part_spec, part_spec),
        scratch_shapes=[
            VMEM((columns, 128), F32),
            VMEM((columns, 128), F32),
            VMEM((BLOCK, 128), F32),
            VMEM((BLOCK, 128), F32),
        ],
        compiler_params=params(),
        name="collect",
    )(half, asked, clash, cos, wire)


def per_device(gauss_rows, vis_shard, vis_row, tile_index, cotangent):
    shards = lax.axis_size("gauss")
    width, columns = gauss_rows.shape
    ask, meta, slot = route(tile_index, vis_shard.reshape(-1, BLOCK), vis_row, shards)
    images, returned, asked, cos, clash = render(slot, meta, ask, gauss_rows, cotangent)
    half = (lax.axis_index("view") * (columns // 2)).astype(I32).reshape(1)
    keep, send = collect(half, asked, clash, cos, returned, width, columns)
    other = lax.ppermute(send, "view", [(0, 1), (1, 0)])
    return (images, keep + other)


def solution(mesh):
    placed = (
        P(None, "gauss"),
        P(("gauss", "view"), None, None),
        P(("gauss", "view"), None),
        P(("gauss", "view")),
        P(("gauss", "view"), None, None),
    )
    return jax.shard_map(
        per_device,
        mesh=mesh,
        in_specs=placed,
        out_specs=(P(("gauss", "view"), None, None), P(None, ("gauss", "view"))),
        check_vma=False,
    )
```

time: 337 us -> 291 us (0.86)
  Pallas kernels: 314 us -> 272 us
    pallas_call x4 -> x2, Pallas kernels: 298 us -> 257 us  [the longest x1 201 us: render(): pl.pallas_call(render_kernel, out_shape=(jax.ShapeDtypeStruct((tiles, CHA...]
  transfers between devices with their start and end apart: 1 -> 1, of which waited for: 1 -> 1; matrix products, arithmetic and copies ran while one was open for 0% -> 1% of each run, Pallas kernels for 0% -> 0%
where the time goes in v4:
time: 291 us; the launch traced here: 287 us
  Pallas kernels  272 us (93%)
  waiting for transfers between devices  5.87 us (2%)
  other arithmetic  4.73 us (2%)
  local copies, waits for them, and re-layouts  4.21 us (1%)
    pallas_call x1, Pallas kernels, render(): pl.pallas_call(render_kernel, out_shape=(jax.ShapeDtypeStruct((tiles, CHA...  201 us
    pallas_call x1, Pallas kernels, collect(): pl.pallas_call(collect_kernel, grid=(shards // SOURCES,), out_shape=(part...  56.2 us
    pallas_call x1, Pallas kernels, route(): pl.pallas_call(route_kernel, out_shape=(lists, lists, jax.ShapeDtypeStruc...  15 us
    ppermute x1, waiting for transfers between devices, per_device(): other = lax.ppermute(send, 'view', [(0, 1), (1, 0)])  5.87 us
  transfers between devices with their start and end apart: 1, of which 1 were waited for; matrix products, arithmetic and copies ran while one was open for 1% of the time, Pallas kernels for 0%

profile of v4, /device:TPU:1, one launch (start us, length us, event | category | flops | bytes accessed | tf_op | source)
XLA Modules:
  0.0 287.3 jit_solution(2696986355625973592)
XLA Ops:
  0.6 2.7 copy.7.cot_ref
  3.4 15.0 %route.1 = (s32[64,8,128]{2,1,0:T(8,128)}, s32[64,8,128]{2,1,0:T(8,128)}, s32[128,128]{1,0:T(8,128)}) custom-call(s32[32]{0:T(128)} %tile_ref.1, s32[128,128]{1,0:T(8,128)} %bitcast.2, s32[32,512]{1,0:T(8,128)} %row_ref.1), custom_call_target="tpu_custom_call" | custom-call | tf_op jit(solution)/shard_map/route/pallas_call | solution.py:126
  18.4 200.6 %render.1 = (f32[32,29,256]{2,1,0:T(8,128)}, f32[64,144,128]{2,1,0:T(8,128)}, s32[64,8,128]{2,1,0:T(8,128)}, f32[64,8,128]{2,1,0:T(8,128)}, s32[64,128]{1,0:T(8,128)}) custom-call(s32[128,128]{1,0:T(8,128)} %get-tuple-element.12.slot_ref, s32[64,8,128]{2,1,0:T(8,128)} %get-tuple-element.13.entry_ref.meta_ref, s32[64,8,128]{2,1,0:T(8,128)} %get-tuple-element.14.ask_ref, ...), custom_call_target="tpu_custom_call" | custom-call | tf_op jit(solution)/shard_map/render/pallas_call | solution.py:531
  219.0 0.0 copy-start
  219.1 56.2 %collect.1 = (f32[64,16384]{1,0:T(8,128)}, f32[64,16384]{1,0:T(8,128)}) custom-call(s32[1]{0:T(128)} %bitcast.1.half_ref, s32[64,8,128]{2,1,0:T(8,128)} %get-tuple-element.16.ask_ref, s32[64,128]{1,0:T(8,128)} %get-tuple-element.17.clash_ref, f32[64,8,128]{2,1,0:T(8,128)} %get-tuple-element.18.cos_ref, f32[64,144,128]{2,1,0:T(8,128)} %get-tuple-element.19.wire_ref), custom_call_target="tpu_custom_call" | custom-call | tf_op jit(solution)/shard_map/collect/pallas_call | solution.py:641
  275.2 0.0 collective-permute-start
  275.2 0.0 copy-done
  275.2 1.5 copy.8
  276.7 5.9 %collective-permute-done = f32[64,16384]{1,0:T(8,128)S(1)} collective-permute-done((f32[64,16384]{1,0:T(8,128)}, f32[64,16384]{1,0:T(8,128)S(1)}, u32[]{:S(2)}, u32[]{:S(2)}) %collective-permute-start) | collective-permute-done | bytes 4194336 | tf_op jit(solution)/shard_map/ppermute | solution.py:671
  282.6 4.7 %add.3 = f32[64,16384]{1,0:T(8,128)} add(f32[64,16384]{1,0:T(8,128)} %get-tuple-element.20, f32[64,16384]{1,0:T(8,128)S(1)} %collective-permute-done) | non-fusion elementwise | flops 1048576 | bytes 12582912 | tf_op jit(solution)/shard_map/add | solution.py:672
Async XLA Ops:
  219.0 56.2 %copy-start = (f32[32,29,256]{2,1,0:T(8,128)S(1)}, f32[32,29,256]{2,1,0:T(8,128)}, u32[]{:S(2)}) copy-start(f32[32,29,256]{2,1,0:T(8,128)} %get-tuple-element.22) | copy-start | bytes 2850820
  275.2 7.4 %collective-permute-start = (f32[64,16384]{1,0:T(8,128)}, f32[64,16384]{1,0:T(8,128)S(1)}, u32[]{:S(2)}, u32[]{:S(2)}) collective-permute-start(f32[64,16384]{1,0:T(8,128)} %get-tuple-element.21), channel_id=1, source_target_pairs={{0,1},{1,0},{2,3},{3,2},{4,5},{5,4},{6,7},{7,6},{8,9},{9,8},{10,11... | collective-permute-start | bytes 12582920 | tf_op jit(solution)/shard_map/ppermute | solution.py:671

commit v5 on v4

--- a/solution.py
+++ b/solution.py
@@ -26,7 +26,11 @@
 I32 = jnp.int32
 GROUP = 8
 BLOCK = 128
+REGIONS = 2
+FIRST = 3 / 8
+SECOND = 5 / 8
 SOURCES = 8
+COPIES = 4
 PICKS = 8
 
 
@@ -55,7 +59,7 @@
     return high, x - high
 
 
-def route_kernel(tile_ref, shard_ref, row_ref, ask_ref, meta_ref, slot_ref):
+def route_kernel(tile_ref, shard_ref, row_ref, ask_ref, entry_ref, used_ref, slot_ref, carry_ref, early_ref):
     shards = ask_ref.shape[0]
     tiles, length = row_ref.shape
     tile_blocks = length // BLOCK
@@ -63,11 +67,16 @@
     parts = length // width
     capacity = 2 * tiles * length // shards
     blocks = capacity // BLOCK
+    part = float(capacity // REGIONS)
+    first, second = int(tiles * FIRST) // 2, int(tiles * SECOND) // 2
     before = (iota((width, width), 0) < iota((width, width), 1)).astype(F32).astype(BF16)
     lane = iota((1, width), 1).astype(F32)
 
     def some(i, state):
-        carry, total = state
+        total = state
+        carry = carry_ref[...]
+        early_ref[...] = jnp.maximum(early_ref[...], carry * jnp.where(i == first, 1.0, 0.0))
+        carry = jnp.maximum(carry, jnp.where(i == second, part, 0.0))
         spots = [(2 * i + u // parts, u % parts) for u in range(2 * parts)]
         shard = [
             jnp.concatenate(
@@ -81,9 +90,9 @@
         at, values = [], []
         for u, (t, h) in enumerate(spots):
             place = jnp.sum(hot[u] * (seen[shards * u : shards * (u + 1)] + carry), axis=0, keepdims=True)
-            carry = carry + jnp.sum(hot[u], axis=1, keepdims=True)
+            carry = carry + jnp.broadcast_to(jnp.sum(hot[u], axis=1, keepdims=True), hot[u].shape)
             place = place.astype(I32)
-            slot = shard[u] * capacity + place
+            slot = shard[u] * capacity + jnp.minimum(place, capacity - 1)
             for b in range(width // BLOCK):
                 slot_ref[pl.ds(t * tile_blocks + h * (width // BLOCK) + b, 1), :] = slot[
                     :, b * BLOCK : (b + 1) * BLOCK
@@ -102,32 +111,43 @@
             values.append(jnp.concatenate([hot[u] * part for part in parts_of], axis=0).astype(BF16))
         at = jnp.concatenate(at, axis=1)
         values = jnp.concatenate(values, axis=1)
-        return carry, total + dot(values, at, ((1,), (1,)))
-
-    start = (jnp.zeros((shards, 1), F32), jnp.zeros((5 * shards, capacity), F32))
-    _, total = lax.fori_loop(0, tiles // 2, some, start)
+        carry_ref[...] = carry
+        return total + dot(values, at, ((1,), (1,)))
+
+    carry_ref[...] = jnp.zeros_like(carry_ref)
+    early_ref[...] = jnp.zeros_like(early_ref)
+    total = lax.fori_loop(0, tiles // 2, some, jnp.zeros((5 * shards, capacity), F32))
+    over = (early_ref[...] > part) | (carry_ref[...] > float(capacity))
+    over = jnp.max(over.astype(F32), axis=(0, 1), keepdims=True)
     low, high, view, lane, chunk = (total[shards * k : shards * (k + 1)].astype(I32) for k in range(5))
     used = view > 0
     row = jnp.where(used, low + 256 * high, iota((shards, capacity), 1))
-    view = jnp.where(used, view - 1, 0)
+    view = jnp.where(over > 0.0, VIEWS, jnp.where(used, view - 1, 0))
     entry = lane + width * chunk
     used = used.astype(I32)
     for c in range(blocks):
         lanes = slice(c * BLOCK, (c + 1) * BLOCK)
         ask_ref[:, c, :] = row[:, lanes]
         ask_ref[:, blocks + c, :] = view[:, lanes]
-        meta_ref[:, c, :] = entry[:, lanes]
-        meta_ref[:, blocks + c, :] = used[:, lanes]
+        entry_ref[:, c, :] = entry[:, lanes]
+        used_ref[:, c, :] = used[:, lanes]
 
 
 def route(tile, shard, row, shards):
     tiles, length = row.shape
-    lists = jax.ShapeDtypeStruct((shards, 8, BLOCK), I32)
+    blocks = 2 * tiles * length // shards // BLOCK
+    lists = jax.ShapeDtypeStruct((shards, blocks, BLOCK), I32)
     return pl.pallas_call(
         route_kernel,
-        out_shape=(lists, lists, jax.ShapeDtypeStruct((tiles * length // BLOCK, BLOCK), I32)),
+        out_shape=(
+            jax.ShapeDtypeStruct((shards, 2 * blocks, BLOCK), I32),
+            lists,
+            lists,
+            jax.ShapeDtypeStruct((tiles * length // BLOCK, BLOCK), I32),
+        ),
         in_specs=[whole(SMEM), whole(VMEM), whole(VMEM)],
-        out_specs=(whole(VMEM),) * 3,
+        out_specs=(whole(VMEM),) * 4,
+        scratch_shapes=[VMEM((shards, 256), F32)] * 2,
         compiler_params=params(),
         name="route",
     )(tile, shard, row)
@@ -162,46 +182,72 @@
     )
 
 
-def exchange(ask_ref, finish, table, even, odd, send, to_ref, send_sem, recv_sem, arrived, own):
-    shards = send.shape[0]
-    blocks = send.shape[1] // PITCH
-    me = lax.axis_index("gauss")
-
-    def copy(to, by):
-        return remote(send.at[to], to_ref.at[by], send_sem.at[to], recv_sem.at[by], to)
-
-    def one(k, _):
-        to, last = shifted(k), shifted(k + shards - 1)
-        for c in range(blocks):
-            now, past = (even, odd) if c % 2 == 0 else (odd, even)
-            finish(past, *((to, c - 1) if c else (last, blocks - 1)))
-            for u in range(BLOCK):
-                now[u : u + 1, :] = table[pl.ds(ask_ref[to, c, u], 1), :]
-            if c == 0:
-
-                @pl.when(k == 1)
-                def _():
-                    own()
-
-                @pl.when(k > 1)
-                def _():
-                    copy(last, me).start()
-
-        return 0
-
-    lax.fori_loop(0, shards, one, 0)
-    last = shifted(shards - 1)
-    finish(odd, last, blocks - 1)
-    copy(last, me).start()
-
-    def end(k, _):
-        by = shifted(k, True)
-        copy(me, by).wait_recv()
-        arrived(by)
-        copy(shifted(k), me).wait_send()
-        return 0
-
-    lax.fori_loop(1, shards, end, 0)
+class Exchange:
+    def __init__(self, ask_ref, finish, table, even, odd, send, to_ref, send_sem, recv_sem, own=None):
+        self.ask_ref, self.finish, self.table, self.even, self.odd = ask_ref, finish, table, even, odd
+        self.send, self.to_ref, self.send_sem, self.recv_sem, self.own = send, to_ref, send_sem, recv_sem, own
+        self.shards = send.shape[0]
+        self.rows = send.shape[1] // REGIONS
+        self.blocks = self.rows // PITCH
+        self.me = lax.axis_index("gauss")
+
+    def piece(self, ref, shard, part):
+        return ref.at[shard, pl.ds(part * self.rows, self.rows)]
+
+    def copy(self, part, to, by):
+        return remote(
+            self.piece(self.send, to, part),
+            self.piece(self.to_ref, by, part),
+            self.send_sem.at[part, to],
+            self.recv_sem.at[part, by],
+            to,
+        )
+
+    def kept(self, part):
+        return pltpu.make_async_copy(
+            self.piece(self.send, self.me, part), self.piece(self.to_ref, self.me, part), self.own.at[part]
+        )
+
+    def start(self, part):
+        blocks = self.blocks
+
+        def one(k, _):
+            to, last = shifted(k), shifted(k + self.shards - 1)
+            for c in range(blocks):
+                now, past = (self.even, self.odd) if c % 2 == 0 else (self.odd, self.even)
+                self.finish(past, *((to, part * blocks + c - 1) if c else (last, part * blocks + blocks - 1)))
+                for u in range(BLOCK):
+                    now[u : u + 1, :] = self.table[pl.ds(self.ask_ref[to, part * blocks + c, u], 1), :]
+                if c == 0:
+                    if self.own is not None:
+
+                        @pl.when(k == 1)
+                        def _():
+                            self.kept(part).start()
+
+                    @pl.when(k > 1)
+                    def _():
+                        self.copy(part, last, self.me).start()
+
+            return 0
+
+        lax.fori_loop(0, self.shards, one, 0)
+        last = shifted(self.shards - 1)
+        self.finish(self.odd, last, part * blocks + blocks - 1)
+        self.copy(part, last, self.me).start()
+
+    def wait(self, part, arrived=None):
+        def end(k, _):
+            by = shifted(k, True)
+            self.copy(part, self.me, by).wait_recv()
+            if arrived is not None:
+                arrived(by)
+            self.copy(part, shifted(k), self.me).wait_send()
+            return 0
+
+        lax.fori_loop(1, self.shards, end, 0)
+        if self.own is not None:
+            self.kept(part).wait()
 
 
 def greet():
@@ -216,11 +262,9 @@
         return 0
 
     lax.fori_loop(1, shards, hail, 0)
-
-    def wait():
-        pl.semaphore_wait(barrier, shards - 1)
-
-    return wait
+    beside = 1 - lax.axis_index("view")
+    pl.semaphore_signal(barrier, inc=1, device_id={"view": beside}, device_id_type=pl.DeviceIdType.MESH)
+    pl.semaphore_wait(barrier, shards)
 
 
 class Tile:
@@ -360,7 +404,7 @@
         self.grads[pl.ds(at, self.length), 0:WIRE] = grad.T
 
 
-def paint(slot_ref, cot_ref, images_ref, table, grads, rows, earlier, later, scratch):
+def paint(slot_ref, cot_ref, images_ref, table, grads, rows, earlier, later, scratch, between):
     tiles = cot_ref.shape[0]
     length = rows[0].shape[0]
     blocks = length // BLOCK
@@ -378,6 +422,24 @@
     pick(rows[1], 1, 0, length)
 
     def two(i, _):
+        for share, read, step in between:
+
+            @pl.when(i == int(tiles * share) // 2)
+            def _(read=read, step=step):
+                step()
+                if read:
+
+                    def again(j, _):
+                        at = pl.multiple_of(j * BLOCK, BLOCK)
+                        for k in range(2):
+                            for u in range(BLOCK):
+                                rows[k][pl.ds(at + u, 1), :] = table[
+                                    pl.ds(slot_ref[(2 * i + k) * blocks + j, u], 1), :
+                                ]
+                        return 0
+
+                    lax.fori_loop(0, blocks, again, 0)
+
         a, b = (
             Tile(2 * i + k, cot_ref, images_ref, grads, rows[k], earlier, later, scratch[k]) for k in range(2)
         )
@@ -438,10 +500,10 @@
 
 
 def render_kernel(
-    slot_ref, entry_ref, ask_ref, meta_ref, rows_ref, cot_ref,
-    images_ref, back_ref, asked_ref, cos_ref, clash_ref,
-    held, table, asked, ask_send, ask_recv, own_sem, even, odd, send, got,
-    send_sem, recv_sem, back_send, back_recv, grads, *scratch,
+    slot_ref, entry_ref, ask_ref, used_ref, rows_ref, cot_ref,
+    images_ref, back_ref, named_ref, cos_ref, clash_ref, void_ref,
+    held, table, asked_ref, asked, ask_send, ask_recv, own_sem, even, odd, send, got,
+    send_sem, recv_sem, back_send, back_recv, kept_sem, here, there, void_sem, grads, *scratch,
 ):
     width, columns = held.shape
     shards = send.shape[0]
@@ -449,7 +511,7 @@
     me = lax.axis_index("gauss")
     load = pltpu.make_async_copy(rows_ref, held, own_sem)
     load.start()
-    greet()()
+    greet()
 
     def copy(to, by):
         return remote(ask_ref.at[to], asked_ref.at[by], ask_send.at[to], ask_recv.at[by], to)
@@ -475,8 +537,11 @@
         return 0
 
     lax.fori_loop(1, shards, end, 0)
-    down = pltpu.make_async_copy(asked_ref, asked, own_sem)
+    for c in range(blocks):
+        named_ref[:, c, :] = asked_ref[:, c, :]
+    down = pltpu.make_async_copy(named_ref, asked, own_sem)
     down.start()
+    void = jnp.zeros((1, 1), F32)
     for c in range(blocks):
         row = asked_ref[:, c, :]
         view = asked_ref[:, blocks + c, :]
@@ -484,11 +549,23 @@
         for v, value in enumerate(view_cosines()):
             cos = jnp.where(view == v, value, cos)
         cos_ref[:, c, :] = cos
+        void = jnp.maximum(void, jnp.max((view == VIEWS).astype(F32), axis=(0, 1), keepdims=True))
         lane = iota(row.shape, 1) % GROUP
         same = jnp.zeros(row.shape, F32)
         for d in range(1, GROUP):
             same = jnp.where((pltpu.roll(row, d, 1) == row) & (lane >= d), 1.0, same)
         clash_ref[:, c : c + 1] = jnp.max(same, axis=1, keepdims=True).astype(I32)
+    here[...] = jnp.broadcast_to(void, here.shape)
+    beside = 1 - lax.axis_index("view")
+    tell = pltpu.make_async_remote_copy(
+        src_ref=here,
+        dst_ref=there,
+        send_sem=void_sem.at[0],
+        recv_sem=void_sem.at[1],
+        device_id={"view": beside},
+        device_id_type=pl.DeviceIdType.MESH,
+    )
+    tell.start()
     down.wait()
 
     def blend(rows, to, c):
@@ -496,31 +573,36 @@
         second = jnp.concatenate([jnp.zeros((GEOM, BLOCK), F32), turned[SENT : SENT + CHANNELS]], axis=0)
         send[to, c * PITCH : c * PITCH + SENT, :] = turned[0:SENT] + cos_ref[to, c : c + 1, :] * second
 
-    def unpack(source, by):
-        for c in range(blocks):
+    def unpack(source, by, part):
+        for c in range(part * blocks // REGIONS, (part + 1) * blocks // REGIONS):
             at = pl.multiple_of((by * blocks + c) * BLOCK, BLOCK)
             table[pl.ds(at, BLOCK), 0:SENT] = source[by, c * PITCH : c * PITCH + SENT, :].T
 
-    def arrived(by):
-        unpack(got, by)
-
-    exchange(asked, blend, table, even, odd, send, got, send_sem, recv_sem, arrived, lambda: None)
-    unpack(send, me)
-
-    paint(
-        slot_ref, cot_ref, images_ref, table, grads, scratch[0:2], scratch[2], scratch[3], (scratch[4:13], scratch[13:22])
-    )
+    out = Exchange(asked, blend, table, even, odd, send, got, send_sem, recv_sem)
+
+    def take(part):
+        out.wait(part, lambda by: unpack(got, by, part))
+        unpack(send, me, part)
 
     def mask(rows, to, c):
-        used = meta_ref[to, blocks + c : blocks + c + 1, :] > 0
+        used = used_ref[to, c : c + 1, :] > 0
         send[to, c * PITCH : c * PITCH + SENT, :] = jnp.where(used, rows[...].T[0:SENT], 0.0)
 
-    own = pltpu.make_async_copy(send.at[me], back_ref.at[me], own_sem)
-    exchange(entry_ref, mask, grads, even, odd, send, back_ref, back_send, back_recv, lambda by: None, own.start)
-    own.wait()
-
-
-def render(slot, meta, ask, gauss_rows, cot):
+    back = Exchange(entry_ref, mask, grads, even, odd, send, back_ref, back_send, back_recv, kept_sem)
+    out.start(0)
+    out.start(1)
+    take(0)
+    between = ((FIRST, True, lambda: take(1)), (SECOND, False, lambda: back.start(0)))
+    tiles = scratch[4:13], scratch[13:22]
+    paint(slot_ref, cot_ref, images_ref, table, grads, scratch[0:2], scratch[2], scratch[3], tiles, between)
+    back.start(1)
+    back.wait(0)
+    back.wait(1)
+    tell.wait()
+    void_ref[...] = jnp.maximum(here[...], there[...]).astype(I32)
+
+
+def render(slot, entry, used, ask, gauss_rows, cot):
     shards = ask.shape[0]
     blocks = ask.shape[1] // 2
     width, columns = gauss_rows.shape
@@ -528,21 +610,24 @@
     length = slot.size // tiles
     wire = (shards, blocks * PITCH, BLOCK)
     sems = pltpu.SemaphoreType.DMA((shards,))
+    pairs = pltpu.SemaphoreType.DMA((REGIONS, shards))
     return pl.pallas_call(
         render_kernel,
         out_shape=(
             jax.ShapeDtypeStruct((tiles, CHANNELS, PIXELS), F32),
             jax.ShapeDtypeStruct(wire, F32),
-            jax.ShapeDtypeStruct(ask.shape, I32),
-            jax.ShapeDtypeStruct(ask.shape, F32),
+            jax.ShapeDtypeStruct(entry.shape, I32),
+            jax.ShapeDtypeStruct(entry.shape, F32),
             jax.ShapeDtypeStruct((shards, 128), I32),
+            jax.ShapeDtypeStruct((8, 128), I32),
         ),
         in_specs=[whole(SMEM), whole(SMEM), whole(VMEM), whole(VMEM), whole(pl.ANY), whole(VMEM)],
-        out_specs=(whole(VMEM), whole(pl.ANY), whole(VMEM), whole(VMEM), whole(VMEM)),
+        out_specs=(whole(VMEM), whole(pl.ANY), whole(VMEM), whole(VMEM), whole(VMEM), whole(VMEM)),
         scratch_shapes=[
             VMEM((width, columns), F32),
             VMEM((columns, 128), F32),
-            SMEM(ask.shape, I32),
+            VMEM(ask.shape, I32),
+            SMEM(entry.shape, I32),
             sems,
             sems,
             pltpu.SemaphoreType.DMA,
@@ -550,19 +635,25 @@
             VMEM((BLOCK, 128), F32),
             VMEM(wire, F32),
             VMEM(wire, F32),
-            sems,
-            sems,
-            sems,
-            sems,
+            pairs,
+            pairs,
+            pairs,
+            pairs,
+            pltpu.SemaphoreType.DMA((REGIONS,)),
+            VMEM((8, 128), F32),
+            VMEM((8, 128), F32),
+            pltpu.SemaphoreType.DMA((2,)),
             VMEM((tiles * length, 128), F32),
         ]
         + paint_scratch(length),
         compiler_params=params(collective_id=0, has_side_effects=True),
         name="render",
-    )(slot, meta, ask, meta, gauss_rows, cot)
-
-
-def collect_kernel(half_ref, ask_ref, clash_ref, cos_ref, wire_ref, keep_ref, send_ref, table, table2, even, odd):
+    )(slot, entry, ask, used, gauss_rows, cot)
+
+
+def collect_kernel(
+    half_ref, ask_ref, clash_ref, cos_ref, wire_ref, keep_ref, send_ref, table, table2, even, odd, wide, sems
+):
     step_id = pl.program_id(0)
     sources = wire_ref.shape[0]
     width, half = keep_ref.shape
@@ -590,24 +681,20 @@
                 into[pl.ds(r, 1), :] = value
 
     def add_slowly(at, c, rows):
-        def one(u, _):
-            table[pl.ds(ask_ref[at, c, u], 1), :] += rows[pl.ds(u, 1), :]
-            return 0
-
-        lax.fori_loop(0, BLOCK, one, 0)
+        for u in range(BLOCK):
+            into = (table, table2)[u % 2]
+            into[pl.ds(ask_ref[at, c, u], 1), :] += rows[u : u + 1, :]
 
     def finish(at, c, rows, more):
-        clear = clash_ref[at, c] == 0
-
-        @pl.when(clear)
-        def _():
+        def quick():
             more()
             add(at, c, rows)
 
-        @pl.when(jnp.logical_not(clear))
-        def _():
+        def careful():
             more()
             add_slowly(at, c, rows)
+
+        lax.cond(clash_ref[at, c] == 0, quick, careful)
 
     def one(s, _):
         source = step_id * sources + s
@@ -622,22 +709,30 @@
     @pl.when(step_id == pl.num_programs(0) - 1)
     def _():
         finish(pl.num_programs(0) * sources - 1, blocks - 1, odd, lambda: None)
-        for ref, base in ((keep_ref, half_ref[0]), (send_ref, half - half_ref[0])):
-
-            def back(i, _):
-                at = pl.multiple_of(i * step, step)
-                there = pl.multiple_of(base + at, step)
-                both = table[pl.ds(there, step), :] + table2[pl.ds(there, step), :]
-                ref[:, pl.ds(at, step)] = both.T[0:width]
-                return 0
-
-            lax.fori_loop(0, half // step, back, 0)
+        copies = []
+        for ref, base in ((send_ref, half - half_ref[0]), (keep_ref, half_ref[0])):
+            for part in range(COPIES):
+                length = half // COPIES
+                held = wide.at[len(copies)]
+
+                def back(i, _):
+                    at = pl.multiple_of(i * step, step)
+                    there = pl.multiple_of(base + part * length + at, step)
+                    both = table[pl.ds(there, step), :] + table2[pl.ds(there, step), :]
+                    held[:, pl.ds(at, step)] = both.T[0:width]
+                    return 0
+
+                lax.fori_loop(0, length // step, back, 0)
+                into = ref.at[:, pl.ds(part * length, length)]
+                copies.append(pltpu.make_async_copy(held, into, sems.at[len(copies)]))
+                copies[-1].start()
+        for copy in copies:
+            copy.wait()
 
 
 def collect(half, asked, clash, cos, wire, width, columns):
     shards, sent, _ = wire.shape
     part = jax.ShapeDtypeStruct((width, columns // 2), F32)
-    part_spec = pl.BlockSpec((width, columns // 2), lambda i: (0, 0), pipeline_mode=pl.Buffered(1))
     return pl.pallas_call(
         collect_kernel,
         grid=(shards // SOURCES,),
@@ -649,27 +744,115 @@
             pl.BlockSpec((SOURCES,) + cos.shape[1:], lambda i: (i, 0, 0)),
             pl.BlockSpec((SOURCES, sent, BLOCK), lambda i: (i, 0, 0)),
         ],
-        out_specs=(part_spec, part_spec),
+        out_specs=(whole(pl.ANY), whole(pl.ANY)),
         scratch_shapes=[
             VMEM((columns, 128), F32),
             VMEM((columns, 128), F32),
             VMEM((BLOCK, 128), F32),
             VMEM((BLOCK, 128), F32),
+            VMEM((2 * COPIES, width, columns // 2 // COPIES), F32),
+            pltpu.SemaphoreType.DMA((2 * COPIES,)),
         ],
         compiler_params=params(),
         name="collect",
     )(half, asked, clash, cos, wire)
 
 
+def plain_composite(entry_params, view_cos, cotangent):
+    pixel = jnp.arange(PIXELS)
+    across = (pixel % TILE_SIDE).astype(jnp.float32) + 0.5
+    down = (pixel // TILE_SIDE).astype(jnp.float32) + 0.5
+
+    def render(params):
+        off_x = across[None, :] - params[:, 0][:, None]
+        off_y = down[None, :] - params[:, 1][:, None]
+        conic_a = jnp.exp(params[:, 2])
+        conic_c = jnp.exp(params[:, 4])
+        conic_b = 0.9 * jnp.tanh(params[:, 3]) * jnp.sqrt(conic_a * conic_c)
+        power = -0.5 * (
+            conic_a[:, None] * off_x * off_x
+            + 2.0 * conic_b[:, None] * off_x * off_y
+            + conic_c[:, None] * off_y * off_y
+        )
+        alpha = 0.99 * jax.nn.sigmoid(params[:, 5])[:, None] * jnp.exp(power)
+        logs = jnp.log(1.0 - alpha)
+        before = jnp.cumsum(logs, axis=0) - logs
+        weight = jnp.exp(before) * alpha
+        colour = params[:, 6 : 6 + CHANNELS] + view_cos * params[:, 6 + CHANNELS : 6 + 2 * CHANNELS]
+        return lax.dot_general(
+            colour, weight, (((0,), (0,)), ((), ())), precision=lax.Precision.HIGHEST
+        )
+
+    image, pull = jax.vjp(render, entry_params)
+    grads = pull(cotangent)
+    return (image, grads[0])
+
+
+def plain(gauss_rows, vis_shard, vis_row, tile_index, cotangent):
+    shards = lax.axis_size("gauss")
+    tiles, length = vis_row.shape
+    entries = tiles * length
+    capacity = 2 * entries // shards
+    width = gauss_rows.shape[0]
+    own_cols = gauss_rows.shape[1]
+    shard_of = vis_shard.reshape(entries)
+    row_of = vis_row.reshape(entries)
+    hits = (shard_of[:, None] == jnp.arange(shards, dtype=jnp.int32)[None, :]).astype(jnp.int32)
+    place = jnp.sum((jnp.cumsum(hits, axis=0) - 1) * hits, axis=1)
+    slot_of = shard_of * capacity + place
+    requests = (
+        jnp.zeros((shards * capacity,), jnp.int32).at[slot_of].set(row_of).reshape(shards, capacity)
+    )
+    row_major = jnp.transpose(gauss_rows)
+    asked = lax.all_to_all(requests, "gauss", split_axis=0, concat_axis=0, tiled=True)
+    fetched = jnp.take(row_major, asked.reshape(-1), axis=0).reshape(
+        asked.shape[0], asked.shape[1], width
+    )
+    sent = lax.all_to_all(fetched, "gauss", split_axis=0, concat_axis=0, tiled=True)
+    entry_rows = jnp.take(sent.reshape(shards * capacity, width), slot_of, axis=0)
+    tile_rows = entry_rows.reshape(tiles, length, width)
+    view_cos = jnp.cos(TWO_PI * (tile_index // SCREEN_TILES).astype(jnp.float32) / VIEWS)
+
+    def one_tile(packed):
+        return plain_composite(packed[0], packed[1], packed[2])
+
+    images, grads = lax.map(one_tile, (tile_rows, view_cos, cotangent), batch_size=4)
+    entry_grads = grads.reshape(entries, width)
+    outgoing = (
+        jnp.zeros((shards * capacity, width), jnp.float32)
+        .at[slot_of]
+        .set(entry_grads)
+        .reshape(shards, capacity, width)
+    )
+    returned = lax.all_to_all(outgoing, "gauss", split_axis=0, concat_axis=0, tiled=True)
+    row_totals = (
+        jnp.zeros((own_cols, width), jnp.float32)
+        .at[asked.reshape(-1)]
+        .add(returned.reshape(shards * capacity, width))
+    )
+    totals = jnp.transpose(row_totals)
+    half = own_cols // 2
+    summed = lax.psum(totals, "view")
+    gradient = lax.dynamic_slice_in_dim(summed, lax.axis_index("view") * half, half, 1)
+    return (images, gradient)
+
+
 def per_device(gauss_rows, vis_shard, vis_row, tile_index, cotangent):
     shards = lax.axis_size("gauss")
     width, columns = gauss_rows.shape
-    ask, meta, slot = route(tile_index, vis_shard.reshape(-1, BLOCK), vis_row, shards)
-    images, returned, asked, cos, clash = render(slot, meta, ask, gauss_rows, cotangent)
-    half = (lax.axis_index("view") * (columns // 2)).astype(I32).reshape(1)
-    keep, send = collect(half, asked, clash, cos, returned, width, columns)
-    other = lax.ppermute(send, "view", [(0, 1), (1, 0)])
-    return (images, keep + other)
+    ask, entry, used, slot = route(tile_index, vis_shard.reshape(-1, BLOCK), vis_row, shards)
+    images, returned, named, cos, clash, void = render(slot, entry, used, ask, gauss_rows, cotangent)
+
+    def quick():
+        half = (lax.axis_index("view") * (columns // 2)).astype(I32).reshape(1)
+        keep, send = collect(half, named, clash, cos, returned, width, columns)
+        other = lax.ppermute(send, "view", [(0, 1), (1, 0)])
+        return (images, keep + other)
+
+    def careful():
+        return plain(gauss_rows, vis_shard, vis_row, tile_index, cotangent)
+
+    return lax.cond(void[0, 0] == 0, quick, careful)
 
 
 def solution(mesh):

time: 291 us -> 277 us (0.952); the launches traced: 287 us -> 276 us
  Pallas kernels: 272 us -> 245 us
  between operations: 0.66 us -> 14.7 us
    pallas_call x1, Pallas kernels: 201 us -> 181 us  [render(): pl.pallas_call(render_kernel, out_shape=(jax.ShapeDtypeStruct((tiles, CHA...]
    pallas_call x1, Pallas kernels: 56.2 us -> 49.5 us  [collect(): pl.pallas_call(collect_kernel, grid=(shards // SOURCES,), out_shape=(part...]
where the time goes in v5:
time: 277 us; the launch traced here: 276 us
  Pallas kernels  245 us (88%)
  between operations  14.7 us (5%)
  waiting for transfers between devices  5.57 us (2%)
  local copies, waits for them, and re-layouts  5.41 us (2%)
  other arithmetic  4.73 us (2%)
    pallas_call x1, Pallas kernels, render(): pl.pallas_call(render_kernel, out_shape=(jax.ShapeDtypeStruct((tiles, CHA...  181 us
    pallas_call x1, Pallas kernels, collect(): pl.pallas_call(collect_kernel, grid=(shards // SOURCES,), out_shape=(part...  49.5 us
    pallas_call x1, Pallas kernels, route(): pl.pallas_call(route_kernel, out_shape=(jax.ShapeDtypeStruct((shards, 2 *...  15.1 us
    ppermute x1, waiting for transfers between devices, quick(): other = lax.ppermute(send, 'view', [(0, 1), (1, 0)])  5.57 us
  transfers between devices with their start and end apart: 1, of which 1 were waited for; matrix products, arithmetic and copies ran while one was open for 1% of the time, Pallas kernels for 0%

profile of v5, /device:TPU:1, one launch (start us, length us, event | category | flops | bytes accessed | tf_op | source)
XLA Modules:
  0.0 276.3 jit_solution(18396419752755173967)
XLA Ops:
  7.2 15.1 %route.1 = (s32[64,8,128]{2,1,0:T(8,128)}, s32[64,4,128]{2,1,0:T(4,128)}, s32[64,4,128]{2,1,0:T(4,128)}, s32[128,128]{1,0:T(8,128)}) custom-call(s32[32]{0:T(128)} %tile_ref.1, s32[128,128]{1,0:T(8,128)} %bitcast.187, s32[32,512]{1,0:T(8,128)} %row_ref.1), custom_call_target="tpu_custom_call" | custom-call | tf_op jit(solution)/shard_map/route/pallas_call | solution.py:140
  22.2 2.7 copy.140.cot_ref
  25.0 0.0 copy-start.4
  25.0 0.0 copy-start.5
  25.0 0.0 copy-start.9
  25.0 0.0 copy-start.10
  25.0 180.7 %render.1 = (f32[32,29,256]{2,1,0:T(8,128)}, f32[64,144,128]{2,1,0:T(8,128)}, s32[64,4,128]{2,1,0:T(4,128)}, f32[64,4,128]{2,1,0:T(4,128)}, s32[64,128]{1,0:T(8,128)}, /*index=5*/s32[8,128]{1,0:T(8,128)}) custom-call(s32[128,128]{1,0:T(8,128)} %get-tuple-element.125.slot_ref, s32[64,4,128]{2,1,0:T(4,128)} %get-tuple-element.126.entry_ref, ...), custom_call_target="tpu_custom_call" | custom-call | tf_op jit(solution)/shard_map/render/pallas_call | solution.py:614
  205.7 1.2 slice.81
  207.5 0.0 copy-done.4
  207.5 0.0 copy-done.5
  207.5 0.0 copy-done.9
  207.5 0.0 copy-done.10
  207.5 61.9 %conditional.1 = (f32[32,29,256]{2,0,1:T(8,128)}, f32[64,16384]{1,0:T(8,128)}) conditional(s32[]{:T(128)} %bitcast.40, (s32[32,512,1]{1,2,0:T(1,128)S(1)}, s32[32,512]{1,0:T(8,128)S(1)}, f32[64,32768]{1,0:T(8,128)}, s32[32]{0:T(128)S(1)}, f32[32,29,256]{2,0,1:T(8,128)S(1)}) %tuple.114, (s32[64,4,128]{2,1,0:T(4,128)}, s32[64,128]{1,0:T(8,128)}, ...), branch_computations={%region_0.20_spmd, %region_20.21_spmd} | conditional | flops 878436608 | bytes 423196992 | solution.py:855
  207.8 0.0 copy-start.6
  207.8 49.5 %collect.1 = (f32[64,16384]{1,0:T(8,128)}, f32[64,16384]{1,0:T(8,128)}) custom-call(s32[1]{0:T(128)} %bitcast.38.half_ref, s32[64,4,128]{2,1,0:T(4,128)} %get-tuple-element.107.ask_ref, s32[64,128]{1,0:T(8,128)} %get-tuple-element.108.clash_ref, f32[64,4,128]{2,1,0:T(4,128)} %get-tuple-element.109.cos_ref, f32[64,144,128]{2,1,0:T(8,128)} %get-tuple-element.110.wire_ref), custom_call_target="tpu_custom_call" | custom-call | tf_op jit(solution)/shard_map/cond/branch_1_fun/collect/pallas_call | solution.py:736
  257.3 0.4 collective-permute-start
  257.7 0.0 copy-done.6
  257.7 1.5 copy.151
  259.1 5.6 %collective-permute-done = f32[64,16384]{1,0:T(8,128)S(1)} collective-permute-done((f32[64,16384]{1,0:T(8,128)}, f32[64,16384]{1,0:T(8,128)S(1)}, u32[]{:S(2)}, u32[]{:S(2)}) %collective-permute-start) | collective-permute-done | bytes 4194336 | tf_op jit(solution)/shard_map/cond/branch_1_fun/ppermute | solution.py:849
  264.7 4.7 %add.210 = f32[64,16384]{1,0:T(8,128)} add(f32[64,16384]{1,0:T(8,128)} %get-tuple-element.111, f32[64,16384]{1,0:T(8,128)S(1)} %collective-permute-done) | non-fusion elementwise | flops 1048576 | bytes 12582912 | tf_op jit(solution)/shard_map/cond/branch_1_fun/add | solution.py:850
Async XLA Ops:
  25.0 182.5 %copy-start.4 = (f32[32,29,256]{2,0,1:T(8,128)S(1)}, f32[32,29,256]{2,0,1:T(8,128)}, u32[]{:S(2)}) copy-start(f32[32,29,256]{2,0,1:T(8,128)} %param.13) | copy-start | bytes 2850820
  25.0 182.5 %copy-start.5 = (s32[32,512,1]{1,2,0:T(1,128)S(1)}, s32[32,512,1]{1,2,0:T(1,128)}, u32[]{:S(2)}) copy-start(s32[32,512,1]{1,2,0:T(1,128)} %param.10) | copy-start | bytes 196612
  25.0 182.6 %copy-start.9 = (s32[32,512]{1,0:T(8,128)S(1)}, s32[32,512]{1,0:T(8,128)}, u32[]{:S(2)}) copy-start(s32[32,512]{1,0:T(8,128)} %row_ref.1) | copy-start | bytes 196612
  25.0 182.6 %copy-start.10 = (s32[32]{0:T(128)S(1)}, s32[32]{0:T(128)}, u32[]{:S(2)}) copy-start(s32[32]{0:T(128)} %tile_ref.1) | copy-start | bytes 388
  207.8 49.9 %copy-start.6 = (f32[32,29,256]{2,1,0:T(8,128)S(1)}, f32[32,29,256]{2,1,0:T(8,128)}, u32[]{:S(2)}) copy-start(f32[32,29,256]{2,1,0:T(8,128)} %get-tuple-element.180) | copy-start | bytes 2850820 | tf_op jit(solution)/shard_map/cond
  257.3 7.4 %collective-permute-start = (f32[64,16384]{1,0:T(8,128)}, f32[64,16384]{1,0:T(8,128)S(1)}, u32[]{:S(2)}, u32[]{:S(2)}) collective-permute-start(f32[64,16384]{1,0:T(8,128)} %get-tuple-element.112), channel_id=1, source_target_pairs={{0,1},{1,0},{2,3},{3,2},{4,5},{5,4},{6,7},{7,6},{8,9},{9,8},{10,11... | collective-permute-start | bytes 12582920 | tf_op jit(solution)/shard_map/cond/branch_1_fun/ppermute | solution.py:849

commit v6 on v5

--- a/solution.py
+++ b/solution.py
@@ -16,7 +16,6 @@
 GEOM = 6
 SENT = 35
 WIRE = 40
-PITCH = 36
 TWO_PI = 6.283185307179586
 LOG2E = 1.4426950408889634
 VMEM = pltpu.VMEM
@@ -26,9 +25,8 @@
 I32 = jnp.int32
 GROUP = 8
 BLOCK = 128
-REGIONS = 2
-FIRST = 3 / 8
-SECOND = 5 / 8
+LEAVE = (3 / 8, 5 / 8, 7 / 8)
+READ = 2
 SOURCES = 8
 COPIES = 4
 PICKS = 8
@@ -67,16 +65,16 @@
     parts = length // width
     capacity = 2 * tiles * length // shards
     blocks = capacity // BLOCK
-    part = float(capacity // REGIONS)
-    first, second = int(tiles * FIRST) // 2, int(tiles * SECOND) // 2
+    leave = [int(tiles * share) // 2 for share in LEAVE]
     before = (iota((width, width), 0) < iota((width, width), 1)).astype(F32).astype(BF16)
     lane = iota((1, width), 1).astype(F32)
 
     def some(i, state):
         total = state
         carry = carry_ref[...]
-        early_ref[...] = jnp.maximum(early_ref[...], carry * jnp.where(i == first, 1.0, 0.0))
-        carry = jnp.maximum(carry, jnp.where(i == second, part, 0.0))
+        early_ref[...] = jnp.maximum(early_ref[...], carry * jnp.where(i == leave[0], 1.0, 0.0))
+        least = sum(jnp.where(i == pair, float((n + 1) * BLOCK), 0.0) for n, pair in enumerate(leave))
+        carry = jnp.maximum(carry, least)
         spots = [(2 * i + u // parts, u % parts) for u in range(2 * parts)]
         shard = [
             jnp.concatenate(
@@ -117,7 +115,7 @@
     carry_ref[...] = jnp.zeros_like(carry_ref)
     early_ref[...] = jnp.zeros_like(early_ref)
     total = lax.fori_loop(0, tiles // 2, some, jnp.zeros((5 * shards, capacity), F32))
-    over = (early_ref[...] > part) | (carry_ref[...] > float(capacity))
+    over = (early_ref[...] > float(READ * BLOCK)) | (carry_ref[...] > float(capacity))
     over = jnp.max(over.astype(F32), axis=(0, 1), keepdims=True)
     low, high, view, lane, chunk = (total[shards * k : shards * (k + 1)].astype(I32) for k in range(5))
     used = view > 0
@@ -153,22 +151,26 @@
     )(tile, shard, row)
 
 
-def shifted(k, back=False):
-    shards = lax.axis_size("gauss")
-    side = round(shards ** (1 / 3))
-    me = lax.axis_index("gauss")
-    step = lax.rem(37 * k, shards)
-    sign = 1 - 2 * lax.axis_index("view")
-    if back:
-        sign = -sign
-
-    def part(x, by):
-        return lax.rem(x // by, side)
-
-    def moved(by):
-        return lax.rem(part(me, by) + sign * part(step, by) + side, side) * by
-
-    return moved(side * side) + moved(side) + moved(1)
+class Partners:
+    def __init__(self):
+        self.shards = lax.axis_size("gauss")
+        self.side = round(self.shards ** (1 / 3))
+        self.me = lax.axis_index("gauss")
+        self.units = (self.side * self.side, self.side, 1)
+        self.here = [lax.rem(lax.div(self.me, jnp.int32(unit)), self.side) + self.side for unit in self.units]
+        self.sign = 1 - 2 * lax.axis_index("view")
+
+    def __call__(self, k):
+        step = lax.rem(37 * k, self.shards)
+        to = 0
+        for unit, here in zip(self.units, self.here):
+            by = lax.div(step, jnp.int32(unit)) if unit > 1 else step
+            by = lax.rem(by, self.side) if unit < self.side * self.side else by
+            to = to + lax.rem(here + self.sign * by, self.side) * unit
+        return to
+
+    def any(self, k):
+        return lax.rem(self.me + k, self.shards)
 
 
 def remote(src, dst, send_sem, recv_sem, to):
@@ -183,66 +185,69 @@
 
 
 class Exchange:
-    def __init__(self, ask_ref, finish, table, even, odd, send, to_ref, send_sem, recv_sem, own=None):
-        self.ask_ref, self.finish, self.table, self.even, self.odd = ask_ref, finish, table, even, odd
+    def __init__(self, ask_ref, finish, table, even, odd, send, to_ref, send_sem, recv_sem, blocks, own=None):
+        self.ask_ref, self.finish, self.table, self.buffers = ask_ref, finish, table, (even, odd)
         self.send, self.to_ref, self.send_sem, self.recv_sem, self.own = send, to_ref, send_sem, recv_sem, own
-        self.shards = send.shape[0]
-        self.rows = send.shape[1] // REGIONS
-        self.blocks = self.rows // PITCH
-        self.me = lax.axis_index("gauss")
+        self.blocks = blocks
+        self.partner = Partners()
+        self.shards, self.me = self.partner.shards, self.partner.me
 
     def piece(self, ref, shard, part):
-        return ref.at[shard, pl.ds(part * self.rows, self.rows)]
+        return ref.at[shard] if part is None else ref.at[shard, pl.ds(part * self.blocks, self.blocks)]
 
     def copy(self, part, to, by):
+        send_sem, recv_sem = self.send_sem, self.recv_sem
+        if self.own is None:
+            send_sem, recv_sem = send_sem.at[part], recv_sem.at[part]
         return remote(
-            self.piece(self.send, to, part),
-            self.piece(self.to_ref, by, part),
-            self.send_sem.at[part, to],
-            self.recv_sem.at[part, by],
-            to,
+            self.piece(self.send, to, part), self.piece(self.to_ref, by, part), send_sem.at[to], recv_sem.at[by], to
         )
 
     def kept(self, part):
         return pltpu.make_async_copy(
-            self.piece(self.send, self.me, part), self.piece(self.to_ref, self.me, part), self.own.at[part]
+            self.piece(self.send, self.me, part), self.piece(self.to_ref, self.me, part), self.own
         )
 
+    def leave(self, part, k, to):
+        if self.own is not None:
+
+            @pl.when(k == 0)
+            def _():
+                self.kept(part).start()
+
+        @pl.when(k > 0)
+        def _():
+            self.copy(part, to, self.me).start()
+
     def start(self, part):
-        blocks = self.blocks
-
-        def one(k, _):
-            to, last = shifted(k), shifted(k + self.shards - 1)
-            for c in range(blocks):
-                now, past = (self.even, self.odd) if c % 2 == 0 else (self.odd, self.even)
-                self.finish(past, *((to, part * blocks + c - 1) if c else (last, part * blocks + blocks - 1)))
-                for u in range(BLOCK):
-                    now[u : u + 1, :] = self.table[pl.ds(self.ask_ref[to, part * blocks + c, u], 1), :]
+        blocks, base = self.blocks, part * self.blocks
+
+        def some(i, last):
+            for n in range(2):
+                k, c = (2 * i + n, 0) if blocks == 1 else (i, n)
+                to = self.partner(k) if c == 0 else to
+                now, past = self.buffers[n], self.buffers[1 - n]
+                self.finish(past, *((to, base + c - 1) if c else (last, base + blocks - 1)))
+                for u in range(0, BLOCK, 8):
+                    picked = [self.table[pl.ds(self.ask_ref[to, base + c, u + v], 1), :] for v in range(8)]
+                    now[u : u + 8, :] = jnp.concatenate(picked, axis=0)
                 if c == 0:
-                    if self.own is not None:
-
-                        @pl.when(k == 1)
-                        def _():
-                            self.kept(part).start()
-
-                    @pl.when(k > 1)
-                    def _():
-                        self.copy(part, last, self.me).start()
-
-            return 0
-
-        lax.fori_loop(0, self.shards, one, 0)
-        last = shifted(self.shards - 1)
-        self.finish(self.odd, last, part * blocks + blocks - 1)
+                    pl.when(k > 0)(functools.partial(self.leave, part, k - 1, last))
+                if c == blocks - 1:
+                    last = to
+            return last
+
+        last = lax.fori_loop(0, self.shards * blocks // 2, some, self.me)
+        self.finish(self.buffers[1], last, base + blocks - 1)
         self.copy(part, last, self.me).start()
 
-    def wait(self, part, arrived=None):
+    def wait(self, part=None, arrived=None):
         def end(k, _):
-            by = shifted(k, True)
+            by = self.partner.any(k)
             self.copy(part, self.me, by).wait_recv()
             if arrived is not None:
                 arrived(by)
-            self.copy(part, shifted(k), self.me).wait_send()
+            self.copy(part, by, self.me).wait_send()
             return 0
 
         lax.fori_loop(1, self.shards, end, 0)
@@ -415,8 +420,9 @@
     later[...] = (above > beside).astype(F32).astype(BF16)
 
     def pick(into, t, start, count):
-        for u in range(start, start + count):
-            into[u : u + 1, :] = table[pl.ds(slot_ref[t * blocks + u // BLOCK, u % BLOCK], 1), :]
+        for u in range(start, start + count, 8):
+            picked = [table[pl.ds(slot_ref[t * blocks + u // BLOCK, (u + v) % BLOCK], 1), :] for v in range(8)]
+            into[u : u + 8, :] = jnp.concatenate(picked, axis=0)
 
     pick(rows[0], 0, 0, length)
     pick(rows[1], 1, 0, length)
@@ -432,10 +438,11 @@
                     def again(j, _):
                         at = pl.multiple_of(j * BLOCK, BLOCK)
                         for k in range(2):
-                            for u in range(BLOCK):
-                                rows[k][pl.ds(at + u, 1), :] = table[
-                                    pl.ds(slot_ref[(2 * i + k) * blocks + j, u], 1), :
+                            for u in range(0, BLOCK, 8):
+                                picked = [
+                                    table[pl.ds(slot_ref[(2 * i + k) * blocks + j, u + v], 1), :] for v in range(8)
                                 ]
+                                rows[k][pl.ds(at + u, 8), :] = jnp.concatenate(picked, axis=0)
                         return 0
 
                     lax.fori_loop(0, blocks, again, 0)
@@ -507,17 +514,19 @@
 ):
     width, columns = held.shape
     shards = send.shape[0]
-    blocks = send.shape[1] // PITCH
+    blocks = send.shape[1]
     me = lax.axis_index("gauss")
     load = pltpu.make_async_copy(rows_ref, held, own_sem)
     load.start()
     greet()
 
+    partner = Partners()
+
     def copy(to, by):
         return remote(ask_ref.at[to], asked_ref.at[by], ask_send.at[to], ask_recv.at[by], to)
 
     def ask(k, _):
-        copy(shifted(k), me).start()
+        copy(partner(k), me).start()
         return 0
 
     lax.fori_loop(1, shards, ask, 0)
@@ -532,8 +541,9 @@
     asked_ref[me] = ask_ref[me]
 
     def end(k, _):
-        copy(shifted(k), me).wait_send()
-        copy(me, shifted(k, True)).wait_recv()
+        by = partner.any(k)
+        copy(me, by).wait_recv()
+        copy(by, me).wait_send()
         return 0
 
     lax.fori_loop(1, shards, end, 0)
@@ -571,14 +581,14 @@
     def blend(rows, to, c):
         turned = rows[...].T
         second = jnp.concatenate([jnp.zeros((GEOM, BLOCK), F32), turned[SENT : SENT + CHANNELS]], axis=0)
-        send[to, c * PITCH : c * PITCH + SENT, :] = turned[0:SENT] + cos_ref[to, c : c + 1, :] * second
+        send[to, c] = turned[0:SENT] + cos_ref[to, c : c + 1, :] * second
 
     def unpack(source, by, part):
-        for c in range(part * blocks // REGIONS, (part + 1) * blocks // REGIONS):
+        for c in range(part * READ, (part + 1) * READ):
             at = pl.multiple_of((by * blocks + c) * BLOCK, BLOCK)
-            table[pl.ds(at, BLOCK), 0:SENT] = source[by, c * PITCH : c * PITCH + SENT, :].T
-
-    out = Exchange(asked, blend, table, even, odd, send, got, send_sem, recv_sem)
+            table[pl.ds(at, BLOCK), 0:SENT] = source[by, c].T
+
+    out = Exchange(asked, blend, table, even, odd, send, got, send_sem, recv_sem, READ)
 
     def take(part):
         out.wait(part, lambda by: unpack(got, by, part))
@@ -586,18 +596,26 @@
 
     def mask(rows, to, c):
         used = used_ref[to, c : c + 1, :] > 0
-        send[to, c * PITCH : c * PITCH + SENT, :] = jnp.where(used, rows[...].T[0:SENT], 0.0)
-
-    back = Exchange(entry_ref, mask, grads, even, odd, send, back_ref, back_send, back_recv, kept_sem)
-    out.start(0)
-    out.start(1)
+        send[to, c] = jnp.where(used, rows[...].T[0:SENT], 0.0)
+
+    back = Exchange(entry_ref, mask, grads, even, odd, send, back_ref, back_send, back_recv, 1, kept_sem.at[0])
+    parts = blocks // READ
+    for part in range(parts):
+        out.start(part)
     take(0)
-    between = ((FIRST, True, lambda: take(1)), (SECOND, False, lambda: back.start(0)))
+
+    def first():
+        back.start(0)
+        for part in range(1, parts):
+            take(part)
+
+    between = [(LEAVE[0], True, first)]
+    for n in range(1, blocks - 1):
+        between.append((LEAVE[n], False, functools.partial(back.start, n)))
     tiles = scratch[4:13], scratch[13:22]
     paint(slot_ref, cot_ref, images_ref, table, grads, scratch[0:2], scratch[2], scratch[3], tiles, between)
-    back.start(1)
-    back.wait(0)
-    back.wait(1)
+    back.start(blocks - 1)
+    back.wait()
     tell.wait()
     void_ref[...] = jnp.maximum(here[...], there[...]).astype(I32)
 
@@ -608,9 +626,9 @@
     width, columns = gauss_rows.shape
     tiles = cot.shape[0]
     length = slot.size // tiles
-    wire = (shards, blocks * PITCH, BLOCK)
+    wire = (shards, blocks, SENT, BLOCK)
     sems = pltpu.SemaphoreType.DMA((shards,))
-    pairs = pltpu.SemaphoreType.DMA((REGIONS, shards))
+    some = pltpu.SemaphoreType.DMA((blocks // READ, shards))
     return pl.pallas_call(
         render_kernel,
         out_shape=(
@@ -635,11 +653,11 @@
             VMEM((BLOCK, 128), F32),
             VMEM(wire, F32),
             VMEM(wire, F32),
-            pairs,
-            pairs,
-            pairs,
-            pairs,
-            pltpu.SemaphoreType.DMA((REGIONS,)),
+            some,
+            some,
+            sems,
+            sems,
+            pltpu.SemaphoreType.DMA((1,)),
             VMEM((8, 128), F32),
             VMEM((8, 128), F32),
             pltpu.SemaphoreType.DMA((2,)),
@@ -657,7 +675,7 @@
     step_id = pl.program_id(0)
     sources = wire_ref.shape[0]
     width, half = keep_ref.shape
-    blocks = wire_ref.shape[1] // PITCH
+    blocks = wire_ref.shape[1]
     step = 512
 
     @pl.when(step_id == 0)
@@ -668,7 +686,7 @@
         odd[...] = jnp.zeros_like(odd)
 
     def turn(s, c, rows):
-        back = wire_ref[s, c * PITCH : c * PITCH + SENT, :]
+        back = wire_ref[s, c]
         scaled = cos_ref[s, c : c + 1, :] * back
         rows[:, 0:width] = jnp.concatenate([back, scaled[GEOM:SENT]], axis=0).T
 
@@ -731,7 +749,7 @@
 
 
 def collect(half, asked, clash, cos, wire, width, columns):
-    shards, sent, _ = wire.shape
+    shards = wire.shape[0]
     part = jax.ShapeDtypeStruct((width, columns // 2), F32)
     return pl.pallas_call(
         collect_kernel,
@@ -742,7 +760,7 @@
             whole(SMEM),
             whole(SMEM),
             pl.BlockSpec((SOURCES,) + cos.shape[1:], lambda i: (i, 0, 0)),
-            pl.BlockSpec((SOURCES, sent, BLOCK), lambda i: (i, 0, 0)),
+            pl.BlockSpec((SOURCES,) + wire.shape[1:], lambda i: (i, 0, 0, 0)),
         ],
         out_specs=(whole(pl.ANY), whole(pl.ANY)),
         scratch_shapes=[

time: 277 us -> 265 us (0.957)
  Pallas kernels: 245 us -> 229 us
  starting transfers between devices: 0.38 us -> 4.46 us
    pallas_call x1, Pallas kernels: 181 us -> 165 us  [render(): pl.pallas_call(render_kernel, out_shape=(jax.ShapeDtypeStruct((tiles, CHA...]
    ppermute x1, starting transfers between devices: 0.38 us -> 4.46 us  [quick(): other = lax.ppermute(send, 'view', [(0, 1), (1, 0)])]
where the time goes in v6:
time: 265 us; the launch traced here: 264 us
  Pallas kernels  229 us (86%)
  between operations  14.7 us (6%)
  waiting for transfers between devices  5.51 us (2%)
  local copies, waits for them, and re-layouts  5.41 us (2%)
  other arithmetic  4.73 us (2%)
  starting transfers between devices  4.46 us (2%)
    pallas_call x1, Pallas kernels, render(): pl.pallas_call(render_kernel, out_shape=(jax.ShapeDtypeStruct((tiles, CHA...  165 us
    pallas_call x1, Pallas kernels, collect(): pl.pallas_call(collect_kernel, grid=(shards // SOURCES,), out_shape=(part...  49.1 us
    pallas_call x1, Pallas kernels, route(): pl.pallas_call(route_kernel, out_shape=(jax.ShapeDtypeStruct((shards, 2 *...  15.2 us
    ppermute x1, waiting for transfers between devices, quick(): other = lax.ppermute(send, 'view', [(0, 1), (1, 0)])  5.51 us
  transfers between devices with their start and end apart: 1, of which 1 were waited for; matrix products, arithmetic and copies ran while one was open for 1% of the time, Pallas kernels for 0%

profile of v6, /device:TPU:1, one launch (start us, length us, event | category | flops | bytes accessed | tf_op | source)
XLA Modules:
  0.0 264.3 jit_solution(14235295110486922719)
XLA Ops:
  7.2 15.2 %route.1 = (s32[64,8,128]{2,1,0:T(8,128)}, s32[64,4,128]{2,1,0:T(4,128)}, s32[64,4,128]{2,1,0:T(4,128)}, s32[128,128]{1,0:T(8,128)}) custom-call(s32[32]{0:T(128)} %tile_ref.1, s32[128,128]{1,0:T(8,128)} %bitcast.187, s32[32,512]{1,0:T(8,128)} %row_ref.1), custom_call_target="tpu_custom_call" | custom-call | tf_op jit(solution)/shard_map/route/pallas_call | solution.py:138
  22.3 2.7 %copy.140.cot_ref = f32[32,29,256]{2,1,0:T(8,128)} copy(f32[32,29,256]{2,0,1:T(8,128)} %param.13) | data formatting | bytes 1900544 | tf_op args[4]
  25.0 0.0 copy-start.4
  25.0 0.0 copy-start.5
  25.0 0.0 copy-start.9
  25.0 0.0 copy-start.10
  25.0 165.0 %render.1 = (f32[32,29,256]{2,1,0:T(8,128)}, f32[64,4,35,128]{3,2,1,0:T(8,128)}, s32[64,4,128]{2,1,0:T(4,128)}, f32[64,4,128]{2,1,0:T(4,128)}, s32[64,128]{1,0:T(8,128)}, /*index=5*/s32[8,128]{1,0:T(8,128)}) custom-call(s32[128,128]{1,0:T(8,128)} %get-tuple-element.125.slot_ref, s32[64,4,128]{2,1,0:T(4,128)} %get-tuple-element.126.entry_ref, ...), custom_call_target="tpu_custom_call" | custom-call | tf_op jit(solution)/shard_map/render/pallas_call | solution.py:632
  190.0 1.2 slice.81
  191.9 0.0 copy-done.4
  191.9 0.0 copy-done.5
  191.9 0.0 copy-done.9
  191.9 0.0 copy-done.10
  191.9 65.5 %conditional.1 = (f32[32,29,256]{2,0,1:T(8,128)}, f32[64,16384]{1,0:T(8,128)}) conditional(s32[]{:T(128)} %bitcast.40, (s32[32,512,1]{1,2,0:T(1,128)S(1)}, s32[32,512]{1,0:T(8,128)S(1)}, f32[64,32768]{1,0:T(8,128)}, s32[32]{0:T(128)S(1)}, f32[32,29,256]{2,0,1:T(8,128)S(1)}) %tuple.114, (s32[64,4,128]{2,1,0:T(4,128)}, s32[64,128]{1,0:T(8,128)}, ...), branch_computations={%region_0.20_spmd, %region_20.21_spmd} | conditional | flops 878436608 | bytes 423196992 | solution.py:873
  192.2 0.0 copy-start.6
  192.2 49.1 %collect.1 = (f32[64,16384]{1,0:T(8,128)}, f32[64,16384]{1,0:T(8,128)}) custom-call(s32[1]{0:T(128)} %bitcast.38.half_ref, s32[64,4,128]{2,1,0:T(4,128)} %get-tuple-element.107.ask_ref, s32[64,128]{1,0:T(8,128)} %get-tuple-element.108.clash_ref, f32[64,4,128]{2,1,0:T(4,128)} %get-tuple-element.109.cos_ref, f32[64,4,35,128]{3,2,1,0:T(8,128)} %get-tuple-element.110.wire_ref), custom_call_target="tpu_custom_call" | custom-call | tf_op jit(solution)/shard_map/cond/branch_1_fun/collect/pallas_call | solution.py:754
  241.3 4.5 %collective-permute-start = (f32[64,16384]{1,0:T(8,128)}, f32[64,16384]{1,0:T(8,128)S(1)}, u32[]{:S(2)}, u32[]{:S(2)}) collective-permute-start(f32[64,16384]{1,0:T(8,128)} %get-tuple-element.112), channel_id=1, source_target_pairs={{0,1},{1,0},{2,3},{3,2},{4,5},{5,4},{6,7},{7,6},{8,9},{9,8},{10,11... | collective-permute-start | bytes 12582920 | tf_op jit(solution)/shard_map/cond/branch_1_fun/ppermute | solution.py:867
  245.7 0.0 copy-done.6
  245.7 1.5 copy.151
  247.2 5.5 %collective-permute-done = f32[64,16384]{1,0:T(8,128)S(1)} collective-permute-done((f32[64,16384]{1,0:T(8,128)}, f32[64,16384]{1,0:T(8,128)S(1)}, u32[]{:S(2)}, u32[]{:S(2)}) %collective-permute-start) | collective-permute-done | bytes 4194336 | tf_op jit(solution)/shard_map/cond/branch_1_fun/ppermute | solution.py:867
  252.7 4.7 %add.210 = f32[64,16384]{1,0:T(8,128)} add(f32[64,16384]{1,0:T(8,128)} %get-tuple-element.111, f32[64,16384]{1,0:T(8,128)S(1)} %collective-permute-done) | non-fusion elementwise | flops 1048576 | bytes 12582912 | tf_op jit(solution)/shard_map/cond/branch_1_fun/add | solution.py:868
Async XLA Ops:
  25.0 166.8 %copy-start.4 = (f32[32,29,256]{2,0,1:T(8,128)S(1)}, f32[32,29,256]{2,0,1:T(8,128)}, u32[]{:S(2)}) copy-start(f32[32,29,256]{2,0,1:T(8,128)} %param.13) | copy-start | bytes 2850820
  25.0 166.9 %copy-start.5 = (s32[32,512,1]{1,2,0:T(1,128)S(1)}, s32[32,512,1]{1,2,0:T(1,128)}, u32[]{:S(2)}) copy-start(s32[32,512,1]{1,2,0:T(1,128)} %param.10) | copy-start | bytes 196612
  25.0 166.9 %copy-start.9 = (s32[32,512]{1,0:T(8,128)S(1)}, s32[32,512]{1,0:T(8,128)}, u32[]{:S(2)}) copy-start(s32[32,512]{1,0:T(8,128)} %row_ref.1) | copy-start | bytes 196612
  25.0 166.9 %copy-start.10 = (s32[32]{0:T(128)S(1)}, s32[32]{0:T(128)}, u32[]{:S(2)}) copy-start(s32[32]{0:T(128)} %tile_ref.1) | copy-start | bytes 388
  192.2 53.6 %copy-start.6 = (f32[32,29,256]{2,1,0:T(8,128)S(1)}, f32[32,29,256]{2,1,0:T(8,128)}, u32[]{:S(2)}) copy-start(f32[32,29,256]{2,1,0:T(8,128)} %get-tuple-element.180) | copy-start | bytes 2850820 | tf_op jit(solution)/shard_map/cond
  241.3 11.5 %collective-permute-start = (f32[64,16384]{1,0:T(8,128)}, f32[64,16384]{1,0:T(8,128)S(1)}, u32[]{:S(2)}, u32[]{:S(2)}) collective-permute-start(f32[64,16384]{1,0:T(8,128)} %get-tuple-element.112), channel_id=1, source_target_pairs={{0,1},{1,0},{2,3},{3,2},{4,5},{5,4},{6,7},{7,6},{8,9},{9,8},{10,11... | collective-permute-start | bytes 12582920 | tf_op jit(solution)/shard_map/cond/branch_1_fun/ppermute | solution.py:867

commit v7 on v6

--- a/solution.py
+++ b/solution.py
@@ -208,38 +208,45 @@
             self.piece(self.send, self.me, part), self.piece(self.to_ref, self.me, part), self.own
         )
 
-    def leave(self, part, k, to):
+    def gather(self, to, block, into):
+        for u in range(0, BLOCK, 8):
+            picked = [self.table[pl.ds(self.ask_ref[to, block, u + v], 1), :] for v in range(8)]
+            into[u : u + 8, :] = jnp.concatenate(picked, axis=0)
+
+    def start(self, part):
+        blocks, base, me = self.blocks, part * self.blocks, self.me
+        even, odd = self.buffers
+        first = self.partner(1)
+        self.gather(me, base, even)
+        if blocks == 1:
+            self.gather(first, base, odd)
+            self.finish(even, me, base)
+        else:
+            self.gather(me, base + 1, odd)
+            self.finish(even, me, base)
+            self.gather(first, base, even)
+            self.finish(odd, me, base + 1)
+            self.gather(first, base + 1, odd)
+            self.finish(even, first, base)
         if self.own is not None:
-
-            @pl.when(k == 0)
-            def _():
-                self.kept(part).start()
-
-        @pl.when(k > 0)
-        def _():
-            self.copy(part, to, self.me).start()
-
-    def start(self, part):
-        blocks, base = self.blocks, part * self.blocks
+            self.kept(part).start()
 
         def some(i, last):
             for n in range(2):
-                k, c = (2 * i + n, 0) if blocks == 1 else (i, n)
+                k, c = (2 * i + n + 2, 0) if blocks == 1 else (i + 2, n)
                 to = self.partner(k) if c == 0 else to
                 now, past = self.buffers[n], self.buffers[1 - n]
                 self.finish(past, *((to, base + c - 1) if c else (last, base + blocks - 1)))
-                for u in range(0, BLOCK, 8):
-                    picked = [self.table[pl.ds(self.ask_ref[to, base + c, u + v], 1), :] for v in range(8)]
-                    now[u : u + 8, :] = jnp.concatenate(picked, axis=0)
+                self.gather(to, base + c, now)
                 if c == 0:
-                    pl.when(k > 0)(functools.partial(self.leave, part, k - 1, last))
+                    self.copy(part, last, me).start()
                 if c == blocks - 1:
                     last = to
             return last
 
-        last = lax.fori_loop(0, self.shards * blocks // 2, some, self.me)
-        self.finish(self.buffers[1], last, base + blocks - 1)
-        self.copy(part, last, self.me).start()
+        last = lax.fori_loop(0, (self.shards - 2) * blocks // 2, some, first)
+        self.finish(odd, last, base + blocks - 1)
+        self.copy(part, last, me).start()
 
     def wait(self, part=None, arrived=None):
         def end(k, _):
@@ -507,10 +514,10 @@
 
 
 def render_kernel(
-    slot_ref, entry_ref, ask_ref, used_ref, rows_ref, cot_ref,
+    slots_ref, entries_ref, ask_ref, used_ref, rows_ref, cots_ref,
     images_ref, back_ref, named_ref, cos_ref, clash_ref, void_ref,
     held, table, asked_ref, asked, ask_send, ask_recv, own_sem, even, odd, send, got,
-    send_sem, recv_sem, back_send, back_recv, kept_sem, here, there, void_sem, grads, *scratch,
+    send_sem, recv_sem, back_send, back_recv, kept_sem, here, there, void_sem, slot_ref, entry_ref, cot_ref, late_sem, grads, *scratch,
 ):
     width, columns = held.shape
     shards = send.shape[0]
@@ -518,6 +525,12 @@
     me = lax.axis_index("gauss")
     load = pltpu.make_async_copy(rows_ref, held, own_sem)
     load.start()
+    late = [
+        pltpu.make_async_copy(source, into, late_sem.at[n])
+        for n, (source, into) in enumerate(((slots_ref, slot_ref), (entries_ref, entry_ref), (cots_ref, cot_ref)))
+    ]
+    for one in late:
+        one.start()
     greet()
 
     partner = Partners()
@@ -603,6 +616,8 @@
     for part in range(parts):
         out.start(part)
     take(0)
+    for one in late:
+        one.wait()
 
     def first():
         back.start(0)
@@ -639,7 +654,7 @@
             jax.ShapeDtypeStruct((shards, 128), I32),
             jax.ShapeDtypeStruct((8, 128), I32),
         ),
-        in_specs=[whole(SMEM), whole(SMEM), whole(VMEM), whole(VMEM), whole(pl.ANY), whole(VMEM)],
+        in_specs=[whole(pl.ANY), whole(pl.ANY), whole(VMEM), whole(VMEM), whole(pl.ANY), whole(pl.ANY)],
         out_specs=(whole(VMEM), whole(pl.ANY), whole(VMEM), whole(VMEM), whole(VMEM), whole(VMEM)),
         scratch_shapes=[
             VMEM((width, columns), F32),
@@ -661,6 +676,10 @@
             VMEM((8, 128), F32),
             VMEM((8, 128), F32),
             pltpu.SemaphoreType.DMA((2,)),
+            SMEM(slot.shape, I32),
+            SMEM(entry.shape, I32),
+            VMEM(cot.shape, F32),
+            pltpu.SemaphoreType.DMA((3,)),
             VMEM((tiles * length, 128), F32),
         ]
         + paint_scratch(length),
@@ -670,7 +689,8 @@
 
 
 def collect_kernel(
-    half_ref, ask_ref, clash_ref, cos_ref, wire_ref, keep_ref, send_ref, table, table2, even, odd, wide, sems
+    half_ref, names_ref, clashes_ref, cos_ref, wire_ref, keep_ref, send_ref,
+    table, table2, even, odd, wide, sems, ask_ref, clash_ref, load_sem,
 ):
     step_id = pl.program_id(0)
     sources = wire_ref.shape[0]
@@ -680,10 +700,18 @@
 
     @pl.when(step_id == 0)
     def _():
+        loads = [
+            pltpu.make_async_copy(names_ref, ask_ref, load_sem.at[0]),
+            pltpu.make_async_copy(clashes_ref, clash_ref, load_sem.at[1]),
+        ]
+        for load in loads:
+            load.start()
         table[...] = jnp.zeros_like(table)
         table2[...] = jnp.zeros_like(table2)
         even[...] = jnp.zeros_like(even)
         odd[...] = jnp.zeros_like(odd)
+        for load in loads:
+            load.wait()
 
     def turn(s, c, rows):
         back = wire_ref[s, c]
@@ -757,8 +785,8 @@
         out_shape=(part, part),
         in_specs=[
             whole(SMEM),
-            whole(SMEM),
-            whole(SMEM),
+            whole(pl.ANY),
+            whole(pl.ANY),
             pl.BlockSpec((SOURCES,) + cos.shape[1:], lambda i: (i, 0, 0)),
             pl.BlockSpec((SOURCES,) + wire.shape[1:], lambda i: (i, 0, 0, 0)),
         ],
@@ -770,6 +798,9 @@
             VMEM((BLOCK, 128), F32),
             VMEM((2 * COPIES, width, columns // 2 // COPIES), F32),
             pltpu.SemaphoreType.DMA((2 * COPIES,)),
+            SMEM(asked.shape, I32),
+            SMEM(clash.shape, I32),
+            pltpu.SemaphoreType.DMA((2,)),
         ],
         compiler_params=params(),
         name="collect",

time: 265 us -> 262 us (0.989)
  Pallas kernels: 229 us -> 223 us
    pallas_call x1, Pallas kernels: 165 us -> 160 us  [render(): pl.pallas_call(render_kernel, out_shape=(jax.ShapeDtypeStruct((tiles, CHA...]
where the time goes in v7:
time: 262 us; the launch traced here: 260 us
  Pallas kernels  223 us (85%)
  between operations  14.7 us (6%)
  starting transfers between devices  7.08 us (3%)
  waiting for transfers between devices  5.51 us (2%)
  local copies, waits for them, and re-layouts  5.41 us (2%)
  other arithmetic  4.73 us (2%)
    pallas_call x1, Pallas kernels, render(): pl.pallas_call(render_kernel, out_shape=(jax.ShapeDtypeStruct((tiles, CHA...  160 us
    pallas_call x1, Pallas kernels, collect(): pl.pallas_call(collect_kernel, grid=(shards // SOURCES,), out_shape=(part...  47.8 us
    pallas_call x1, Pallas kernels, route(): pl.pallas_call(route_kernel, out_shape=(jax.ShapeDtypeStruct((shards, 2 *...  15.2 us
    ppermute x1, starting transfers between devices, quick(): other = lax.ppermute(send, 'view', [(0, 1), (1, 0)])  7.08 us
    ppermute x1, waiting for transfers between devices, quick(): other = lax.ppermute(send, 'view', [(0, 1), (1, 0)])  5.51 us
  transfers between devices with their start and end apart: 1, of which 1 were waited for; matrix products, arithmetic and copies ran while one was open for 1% of the time, Pallas kernels for 0%

profile of v7, /device:TPU:1, one launch (start us, length us, event | category | flops | bytes accessed | tf_op | source)
XLA Modules:
  0.0 260.4 jit_solution(17623177262859934714)
XLA Ops:
  7.2 15.2 %route.1 = (s32[64,8,128]{2,1,0:T(8,128)}, s32[64,4,128]{2,1,0:T(4,128)}, s32[64,4,128]{2,1,0:T(4,128)}, s32[128,128]{1,0:T(8,128)}) custom-call(s32[32]{0:T(128)} %tile_ref.1, s32[128,128]{1,0:T(8,128)} %bitcast.187, s32[32,512]{1,0:T(8,128)} %row_ref.1), custom_call_target="tpu_custom_call" | custom-call | tf_op jit(solution)/shard_map/route/pallas_call | solution.py:138
  22.3 2.7 %copy.140.cots_ref = f32[32,29,256]{2,1,0:T(8,128)} copy(f32[32,29,256]{2,0,1:T(8,128)} %param.13) | data formatting | bytes 1900544 | tf_op args[4]
  25.0 0.0 copy-start.4
  25.0 0.0 copy-start.5
  25.0 0.0 copy-start.9
  25.0 0.0 copy-start.10
  25.0 159.7 %render.1 = (f32[32,29,256]{2,1,0:T(8,128)}, f32[64,4,35,128]{3,2,1,0:T(8,128)}, s32[64,4,128]{2,1,0:T(4,128)}, f32[64,4,128]{2,1,0:T(4,128)}, s32[64,128]{1,0:T(8,128)}, /*index=5*/s32[8,128]{1,0:T(8,128)}) custom-call(s32[128,128]{1,0:T(8,128)} %get-tuple-element.125.slots_ref, s32[64,4,128]{2,1,0:T(4,128)} %get-tuple-element.126.entries_ref, ...), custom_call_target="tpu_custom_call" | custom-call | tf_op jit(solution)/shard_map/render/pallas_call | solution.py:647
  184.7 1.2 slice.81
  186.6 0.0 copy-done.4
  186.6 0.0 copy-done.5
  186.6 0.0 copy-done.9
  186.6 0.0 copy-done.10
  186.6 66.9 %conditional.1 = (f32[32,29,256]{2,0,1:T(8,128)}, f32[64,16384]{1,0:T(8,128)}) conditional(s32[]{:T(128)} %bitcast.40, (s32[32,512,1]{1,2,0:T(1,128)S(1)}, s32[32,512]{1,0:T(8,128)S(1)}, f32[64,32768]{1,0:T(8,128)}, s32[32]{0:T(128)S(1)}, f32[32,29,256]{2,0,1:T(8,128)S(1)}) %tuple.114, (s32[64,4,128]{2,1,0:T(4,128)}, s32[64,128]{1,0:T(8,128)}, ...), branch_computations={%region_0.20_spmd, %region_20.21_spmd} | conditional | flops 878436608 | bytes 423196992 | solution.py:904
  186.9 0.0 copy-start.6
  186.9 47.8 %collect.1 = (f32[64,16384]{1,0:T(8,128)}, f32[64,16384]{1,0:T(8,128)}) custom-call(s32[1]{0:T(128)} %bitcast.38.half_ref, s32[64,4,128]{2,1,0:T(4,128)} %get-tuple-element.107.names_ref, s32[64,128]{1,0:T(8,128)} %get-tuple-element.108.clashes_ref, f32[64,4,128]{2,1,0:T(4,128)} %get-tuple-element.109.cos_ref, f32[64,4,35,128]{3,2,1,0:T(8,128)} %get-tuple-element.110.wire_ref), custom_call_target="tpu_custom_call" | custom-call | tf_op jit(solution)/shard_map/cond/branch_1_fun/collect/pallas_call | solution.py:782
  234.7 7.1 %collective-permute-start = (f32[64,16384]{1,0:T(8,128)}, f32[64,16384]{1,0:T(8,128)S(1)}, u32[]{:S(2)}, u32[]{:S(2)}) collective-permute-start(f32[64,16384]{1,0:T(8,128)} %get-tuple-element.112), channel_id=1, source_target_pairs={{0,1},{1,0},{2,3},{3,2},{4,5},{5,4},{6,7},{7,6},{8,9},{9,8},{10,11... | collective-permute-start | bytes 12582920 | tf_op jit(solution)/shard_map/cond/branch_1_fun/ppermute | solution.py:898
  241.8 0.0 copy-done.6
  241.8 1.5 copy.151
  243.3 5.5 %collective-permute-done = f32[64,16384]{1,0:T(8,128)S(1)} collective-permute-done((f32[64,16384]{1,0:T(8,128)}, f32[64,16384]{1,0:T(8,128)S(1)}, u32[]{:S(2)}, u32[]{:S(2)}) %collective-permute-start) | collective-permute-done | bytes 4194336 | tf_op jit(solution)/shard_map/cond/branch_1_fun/ppermute | solution.py:898
  248.8 4.7 %add.210 = f32[64,16384]{1,0:T(8,128)} add(f32[64,16384]{1,0:T(8,128)} %get-tuple-element.111, f32[64,16384]{1,0:T(8,128)S(1)} %collective-permute-done) | non-fusion elementwise | flops 1048576 | bytes 12582912 | tf_op jit(solution)/shard_map/cond/branch_1_fun/add | solution.py:899
Async XLA Ops:
  25.0 161.5 %copy-start.4 = (f32[32,29,256]{2,0,1:T(8,128)S(1)}, f32[32,29,256]{2,0,1:T(8,128)}, u32[]{:S(2)}) copy-start(f32[32,29,256]{2,0,1:T(8,128)} %param.13) | copy-start | bytes 2850820
  25.0 161.6 %copy-start.5 = (s32[32,512,1]{1,2,0:T(1,128)S(1)}, s32[32,512,1]{1,2,0:T(1,128)}, u32[]{:S(2)}) copy-start(s32[32,512,1]{1,2,0:T(1,128)} %param.10) | copy-start | bytes 196612
  25.0 161.6 %copy-start.9 = (s32[32,512]{1,0:T(8,128)S(1)}, s32[32,512]{1,0:T(8,128)}, u32[]{:S(2)}) copy-start(s32[32,512]{1,0:T(8,128)} %row_ref.1) | copy-start | bytes 196612
  25.0 161.6 %copy-start.10 = (s32[32]{0:T(128)S(1)}, s32[32]{0:T(128)}, u32[]{:S(2)}) copy-start(s32[32]{0:T(128)} %tile_ref.1) | copy-start | bytes 388
  186.9 54.9 %copy-start.6 = (f32[32,29,256]{2,1,0:T(8,128)S(1)}, f32[32,29,256]{2,1,0:T(8,128)}, u32[]{:S(2)}) copy-start(f32[32,29,256]{2,1,0:T(8,128)} %get-tuple-element.180) | copy-start | bytes 2850820 | tf_op jit(solution)/shard_map/cond
  234.7 14.1 %collective-permute-start = (f32[64,16384]{1,0:T(8,128)}, f32[64,16384]{1,0:T(8,128)S(1)}, u32[]{:S(2)}, u32[]{:S(2)}) collective-permute-start(f32[64,16384]{1,0:T(8,128)} %get-tuple-element.112), channel_id=1, source_target_pairs={{0,1},{1,0},{2,3},{3,2},{4,5},{5,4},{6,7},{7,6},{8,9},{9,8},{10,11... | collective-permute-start | bytes 12582920 | tf_op jit(solution)/shard_map/cond/branch_1_fun/ppermute | solution.py:898
